TPU v7x, 32 devices: a whole 2x2x4 slice. The times are simulated.
32 devices in a mesh: parts: 2 (over x), group: 8 (over z, core), local: 2 (over y).
Axes of the slice: x: 2, y: 2, z: 4, core: 2. Of those that a mesh axis runs over, the one named last changes fastest.
Arguments:
- tokens: bfloat16 [128, 7168], P(('parts', 'group', 'local')), parts along dimension 0, may hold values from -6 to 6
- routes: int32 [128, 4], P(('parts', 'group', 'local')), parts along dimension 0, may hold values from 0 to 7, all different within a row; in each aligned block of 4 rows (0 to 3, 4 to 7, ...) at most 4 rows name the same one
- gate_weights: bfloat16 [128, 8], P(('parts', 'group', 'local')), parts along dimension 0, may hold values from 0.099609375 to 1
- w_gate: bfloat16 [16, 7168, 1024], P('group', None, 'local'), may hold values from -0.0625 to 0.0625
- w_up: bfloat16 [16, 7168, 1024], P('group', None, 'local'), may hold values from -0.0625 to 0.0625
- w_down: bfloat16 [16, 1024, 7168], P('group', 'local'), may hold values from -0.1875 to 0.1875
Outputs:
- mixed_rows: bfloat16 [128, 7168], P(('parts', 'group', 'local')), parts along dimension 0
There are 2 independent parts, one for each index of `parts`. A program takes and returns all parts, laid end to end along the dimension named above; an argument that names none is the same for every part. Nothing has to cross between parts.
Inputs may be any that keep to these rules, and one draw needn't show every extreme that they name: `routes`: each row names 4 different groups; among the rows of one device no group is named by more than 4 rows, a bound that some block reaches.
All inputs are finite; a program needn't handle non-finite values.
Results may differ from a plain program's by a relative error of at most 0.005.
Values may be sent and summed in bfloat16 or wider, within the bound.
No kernel may reach another device: no remote copies, remote signals or barrier semaphores. Data moves between devices by JAX's collectives and lax.ppermute only.
A program may use at most 128 MiB of HBM per device.

v0:
```python
import jax
import jax.numpy as jnp
from jax import lax
from jax.sharding import PartitionSpec as P


def on_device(tokens, routes, gate_weights, w_gate, w_up, w_down):
    group_count = lax.axis_size("group")
    local_count = lax.axis_size("local")
    rows_here = tokens.shape[0]
    model_width = tokens.shape[1]
    groups_row = routes.shape[1]
    expert_pairs = w_gate.shape[0]
    capacity = min(rows_here, 2 * rows_here * groups_row // group_count)
    hit_marks = routes[:, :, None] == jnp.arange(group_count, dtype=jnp.int32)[None, None, :]
    member = jnp.sum(hit_marks.astype(jnp.int32), axis=1)
    position = jnp.cumsum(member, axis=0) - 1
    slot_ids = jnp.arange(capacity, dtype=jnp.int32)[None, :, None]
    select_mask = (member.T[:, None, :] == 1) & (position.T[:, None, :] == slot_ids)
    select_bf = select_mask.astype(jnp.bfloat16)
    select_fp = select_mask.astype(jnp.float32)
    gate_pairs = gate_weights.reshape(rows_here, groups_row, expert_pairs).astype(jnp.float32)
    row_weights = jnp.einsum(
        "rkg,rke->rge", hit_marks.astype(jnp.float32), gate_pairs, precision=lax.Precision.HIGHEST
    )
    send_rows = jnp.einsum(
        "gcr,rd->gcd", select_bf, tokens, preferred_element_type=jnp.float32
    ).astype(jnp.bfloat16)
    send_weights = jnp.einsum(
        "gcr,rge->gce", select_fp, row_weights, precision=lax.Precision.HIGHEST
    ).astype(jnp.bfloat16)
    near_rows, near_weights = (
        lax.all_to_all(send_rows, "group", split_axis=0, concat_axis=0, tiled=True),
        lax.all_to_all(send_weights, "group", split_axis=0, concat_axis=0, tiled=True),
    )
    got_rows, got_weights = (
        lax.all_gather(near_rows, "local", axis=0, tiled=True),
        lax.all_gather(near_weights, "local", axis=0, tiled=True),
    )
    local_dim = 0
    block_shape = (local_count, group_count, capacity, model_width)
    flat_rows = got_rows.reshape(-1, model_width)
    flat_weights = got_weights.reshape(-1, expert_pairs).astype(jnp.float32)
    partial_value = jnp.zeros((flat_rows.shape[0], model_width), jnp.float32)
    for expert_slot in range(expert_pairs):
        gate_act = jnp.dot(flat_rows, w_gate[expert_slot], preferred_element_type=jnp.float32)
        up_act = jnp.dot(flat_rows, w_up[expert_slot], preferred_element_type=jnp.float32)
        hidden = (jax.nn.silu(gate_act) * up_act).astype(jnp.bfloat16)
        expert_out = jnp.dot(hidden, w_down[expert_slot], preferred_element_type=jnp.float32)
        partial_value = partial_value + flat_weights[:, expert_slot : expert_slot + 1] * expert_out
    partial_blocks = partial_value.reshape(block_shape)
    partial_blocks = jnp.swapaxes(partial_blocks, 0, 1)
    outgoing = partial_blocks.reshape(group_count * local_count, capacity, model_width)
    returned_all = lax.all_to_all(
        outgoing, ("group", "local"), split_axis=0, concat_axis=0, tiled=True
    )
    returned = jnp.sum(
        returned_all.reshape(group_count, local_count, capacity, model_width), axis=1
    )
    mixed_rows = jnp.einsum("gcr,gcd->rd", select_fp, returned, precision=lax.Precision.HIGHEST)
    return mixed_rows.astype(jnp.bfloat16)


def solution(mesh):
    return jax.shard_map(
        on_device,
        mesh=mesh,
        in_specs=(
            P(("parts", "group", "local"), None),
            P(("parts", "group", "local"), None),
            P(("parts", "group", "local"), None),
            P("group", None, "local"),
            P("group", None, "local"),
            P("group", "local", None),
        ),
        out_specs=P(("parts", "group", "local"), None),
        check_vma=False,
    )
```

profile of v0, /device:TPU:0, one launch (start us, length us, event | category | flops | bytes accessed | tf_op | source)
XLA Modules:
  0.0 123.5 jit_solution(14812366826739713012)
XLA Ops:
  0.0 0.8 convert_reduce_fusion
  0.8 0.8 copy.31
  1.6 0.1 copy.32
  1.7 0.9 fusion.48
  2.7 0.1 copy.33
  2.8 0.8 convolution_convert_fusion.1
  3.6 6.3 %all-to-all-start = ((bf16[8,4,2]{1,2,0:T(2,128)(2,1)}), bf16[8,4,2]{1,2,0:T(2,128)(2,1)S(1)}, u32[]{:S(2)}, u32[]{:S(2)}) async-start(bf16[8,4,2]{1,2,0:T(2,128)(2,1)} %convolution_convert_fusion.1), calls=%async_computation | async-start | bytes 8192 | tf_op jit(solution)/shard_map/all_to_all | solution.py:34
  9.9 0.3 convolution_convert_fusion
  10.2 1.1 copy.37
  11.4 4.0 %all-to-all-done = bf16[8,4,2]{1,2,0:T(2,128)(2,1)S(1)} async-done(((bf16[8,4,2]{1,2,0:T(2,128)(2,1)}), bf16[8,4,2]{1,2,0:T(2,128)(2,1)S(1)}, u32[]{:S(2)}, u32[]{:S(2)}) %all-to-all-start) | async-done | bytes 160 | tf_op jit(solution)/shard_map/all_to_all | solution.py:34
  15.4 3.5 %all-to-all-start.1 = ((bf16[8,4,7168]{2,1,0:T(4,128)(2,1)}), bf16[8,4,7168]{2,1,0:T(4,128)(2,1)S(1)}, u32[]{:S(2)}, u32[]{:S(2)}) async-start(bf16[8,4,7168]{2,1,0:T(4,128)(2,1)} %copy.37), calls=%async_computation.1 | async-start | bytes 917504 | tf_op jit(solution)/shard_map/all_to_all | solution.py:33
  18.9 4.4 %all_gather.6 = bf16[16,4,2]{1,2,0:T(2,128)(2,1)S(1)} all-gather(bf16[8,4,2]{1,2,0:T(2,128)(2,1)S(1)} %all-to-all-done), channel_id=1, replica_groups=mesh['parts'=2,'group'=8,'local'=2] {'local'}, dimensions={0}, use_global_device_ids=true | all-gather | bytes 384 | tf_op jit(solution)/shard_map/all_gather | solution.py:38
  23.5 9.2 %all-to-all-done.1 = bf16[8,4,7168]{2,1,0:T(4,128)(2,1)S(1)} async-done(((bf16[8,4,7168]{2,1,0:T(4,128)(2,1)}), bf16[8,4,7168]{2,1,0:T(4,128)(2,1)S(1)}, u32[]{:S(2)}, u32[]{:S(2)}) %all-to-all-start.1) | async-done | bytes 458784 | tf_op jit(solution)/shard_map/all_to_all | solution.py:33
  32.7 12.7 %all_gather.7 = bf16[16,4,7168]{2,1,0:T(4,128)(2,1)S(1)} all-gather(bf16[8,4,7168]{2,1,0:T(4,128)(2,1)S(1)} %all-to-all-done.1), channel_id=1, replica_groups=mesh['parts'=2,'group'=8,'local'=2] {'local'}, dimensions={0}, use_global_device_ids=true | all-gather | bytes 1376256 | tf_op jit(solution)/shard_map/all_gather | solution.py:37
  45.5 0.2 reshape.23
  45.7 4.5 %fusion.5 = f32[64,512]{1,0:T(8,128)S(1)} fusion(bf16[64,7168]{1,0:T(8,128)(2,1)S(1)} %reshape.23, bf16[2,7168,512]{2,1,0:T(8,128)(2,1)} %param.9), kind=kOutput, calls=%fused_computation.9 | convolution fusion | flops 469762048 | bytes 8388608 | tf_op jit(solution)/shard_map/dot_general | solution.py:46
  50.1 4.5 %fusion.10 = f32[64,512]{1,0:T(8,128)S(1)} fusion(bf16[64,7168]{1,0:T(8,128)(2,1)S(1)} %reshape.23, bf16[2,7168,512]{2,1,0:T(8,128)(2,1)} %param.9), kind=kOutput, calls=%fused_computation.14 | convolution fusion | flops 469762048 | bytes 8388608 | tf_op jit(solution)/shard_map/dot_general | solution.py:46
  54.6 8.1 %convolution_multiply_fusion.1 = f32[64,7168]{1,0:T(8,128)S(1)} fusion(bf16[2,512,7168]{2,1,0:T(8,128)(2,1)} %param.11, f32[64]{0:T(128)S(1)} %get-tuple-element.6, bf16[64,7168]{1,0:T(8,128)(2,1)S(1)} %reshape.23, bf16[2,7168,512]{2,1,0:T(8,128)(2,1)} %param.10, f32[64,512]{1,0:T(8,128)S(1)} %fusion.10), kind=kOutput, calls=%fused_computation.2 | convolution fusion | flops 940179456 | bytes 17563904 | tf_op jit(solution)/shard_map/dot_general | solution.py:49
  62.7 9.3 %fusion = f32[64,7168]{1,0:T(8,128)} fusion(f32[64,7168]{1,0:T(8,128)S(1)} %convolution_multiply_fusion.1, bf16[2,512,7168]{2,1,0:T(8,128)(2,1)} %param.11, f32[64]{0:T(128)S(1)} %get-tuple-element.5, bf16[64,7168]{1,0:T(8,128)(2,1)S(1)} %reshape.23, bf16[2,7168,512]{2,1,0:T(8,128)(2,1)} %param.10, f32[64,512]{1,0:T(8,128)S(1)} %fusion.5), kind=kOutput, calls=%fused_computation.1 | convolution fusion | flops 940638208 | bytes 19398912 | tf_op jit(solution)/shard_map/dot_general | solution.py:49
  72.0 1.9 %reshape.24 = f32[2,8,4,7168]{3,2,1,0:T(4,128)S(1)} reshape(f32[64,7168]{1,0:T(8,128)} %fusion) | data formatting | bytes 3670016 | tf_op jit(solution)/shard_map/reshape | solution.py:51
  73.9 0.1 copy.38
  74.0 47.5 %all_to_all.15 = f32[16,4,7168]{2,1,0:T(4,128)S(1)} all-to-all(f32[16,4,7168]{2,1,0:T(4,128)S(1)} %bitcast.62), channel_id=1, replica_groups=mesh['parts'=2,'group'=8,'local'=2] {'group','local'}, dimensions={0} | all-to-all | bytes 3670016 | tf_op jit(solution)/shard_map/all_to_all | solution.py:54
  121.5 0.4 bitcast_reduce_fusion
  121.9 1.5 %fusion.1 = bf16[4,7168]{1,0:T(4,128)(2,1)} fusion(pred[8,4,4]{0,2,1:T(4,128)(4,1)S(1)} %fusion.49, f32[8,4,7168]{2,1,0:T(4,128)S(1)} %bitcast_reduce_fusion), kind=kOutput, calls=%fused_computation.5 | convolution fusion | flops 11038720 | bytes 974976 | tf_op jit(solution)/shard_map/gcr,gcd->rd/dot_general | solution.py:60
  (11 shorter events, 0.5 us)
Async XLA Ops:
  0.0 9.9 %copy-start = (bf16[4,7168]{1,0:T(4,128)(2,1)S(1)}, bf16[4,7168]{1,0:T(4,128)(2,1)}, u32[]{:S(2)}) copy-start(bf16[4,7168]{1,0:T(4,128)(2,1)} %param.6) | copy-start | bytes 172036
  3.6 11.8 %all-to-all-start = ((bf16[8,4,2]{1,2,0:T(2,128)(2,1)}), bf16[8,4,2]{1,2,0:T(2,128)(2,1)S(1)}, u32[]{:S(2)}, u32[]{:S(2)}) async-start(bf16[8,4,2]{1,2,0:T(2,128)(2,1)} %convolution_convert_fusion.1), calls=%async_computation | async-start | bytes 8192 | tf_op jit(solution)/shard_map/all_to_all | solution.py:34
  15.4 17.4 %all-to-all-start.1 = ((bf16[8,4,7168]{2,1,0:T(4,128)(2,1)}), bf16[8,4,7168]{2,1,0:T(4,128)(2,1)S(1)}, u32[]{:S(2)}, u32[]{:S(2)}) async-start(bf16[8,4,7168]{2,1,0:T(4,128)(2,1)} %copy.37), calls=%async_computation.1 | async-start | bytes 917504 | tf_op jit(solution)/shard_map/all_to_all | solution.py:33
where the time goes:
time: 124 us; the launch traced here: 123 us
  blocking collectives  64.6 us (52%)
  matrix products  29.8 us (24%)
  waiting for transfers between devices  13.2 us (11%)
  starting transfers between devices  9.8 us (8%)
  local copies, waits for them, and re-layouts  4.71 us (4%)
  other arithmetic  1.24 us (1%)
    all_to_all x1, blocking collectives, on_device(): lax.all_to_all(outgoing, ('group', 'local'), split_axis=0, concat_axis=0,...  47.5 us
    dot_general x2, matrix products, on_device(): jnp.dot(hidden, w_down[expert_slot], preferred_element_type=jnp.float32)  17.4 us
    all_gather x1, blocking collectives, on_device(): lax.all_gather(near_rows, 'local', axis=0, tiled=True)  12.7 us
    all_to_all x1, waiting for transfers between devices, on_device(): lax.all_to_all(send_rows, 'group', split_axis=0, concat_axis=0, tiled=True)  9.2 us
    dot_general x2, matrix products, on_device(): jnp.dot(flat_rows, w_gate[expert_slot], preferred_element_type=jnp.float32)  8.91 us
    all_to_all x1, starting transfers between devices, on_device(): lax.all_to_all(send_weights, 'group', split_axis=0, concat_axis=0, tiled=...  6.33 us
    all_gather x1, blocking collectives, on_device(): lax.all_gather(near_weights, 'local', axis=0, tiled=True)  4.37 us
    all_to_all x1, waiting for transfers between devices, on_device(): lax.all_to_all(send_weights, 'group', split_axis=0, concat_axis=0, tiled=...  4.01 us
  transfers between devices with their start and end apart: 2, of which 2 were waited for; matrix products, arithmetic and copies ran while one was open for 1% of the time, Pallas kernels for 0%

commit v1 on v0

v1 whole, which is shorter than its diff:
```python
import jax
import jax.numpy as jnp
from jax import lax
from jax.experimental import pallas as pl
from jax.experimental.pallas import tpu as pltpu
from jax.sharding import PartitionSpec as P

LANES = 128


def rotate(value, axis, shift, stride):
    size = lax.axis_size(axis)
    return lax.ppermute(value, axis, [(i, (i + shift * stride) % size) for i in range(size)])


def other_core(value):
    return lax.ppermute(value, "group", [(i, i ^ 1) for i in range(lax.axis_size("group"))])


def experts_kernel(x_ref, gate_ref, up_ref, down_ref, keep_ref, send_ref):
    rows = x_ref.shape[0]
    width = down_ref.shape[1]
    pairs, _, hidden_here = gate_ref.shape
    keep_rows = keep_ref.shape[0]
    group = lax.axis_index("group").astype(jnp.float32)
    side = x_ref[:, width:].astype(jnp.float32)
    lane = lax.broadcasted_iota(jnp.int32, (rows, LANES), 1)
    groups_row = 4
    parts = []
    x = x_ref[:, :width]
    for e in range(pairs):
        weight = jnp.zeros((rows, 1), jnp.float32)
        for k in range(groups_row):
            hit = side[:, k : k + 1] == group
            column = groups_row + k * pairs + e
            weight = weight + jnp.where(hit, side[:, column : column + 1], 0.0)
        gate_act = jnp.dot(x, gate_ref[e], preferred_element_type=jnp.float32)
        up_act = jnp.dot(x, up_ref[e], preferred_element_type=jnp.float32)
        hidden = gate_act / (1.0 + jnp.exp(-gate_act)) * up_act
        parts.append((hidden * weight).astype(jnp.bfloat16))
    hidden = jnp.concatenate(parts, axis=1)
    step = 1024
    for c in range(0, width, step):
        y = jnp.dot(hidden, down_ref[:, c : c + step], preferred_element_type=jnp.float32)
        keep_ref[:, c : c + step] = y[:keep_rows]
        send_ref[:, c : c + step] = y[keep_rows:].astype(jnp.bfloat16)


def on_device(tokens, routes, gate_weights, w_gate, w_up, w_down):
    chips = lax.axis_size("group") // 2
    locals_ = lax.axis_size("local")
    rows_here, width = tokens.shape
    pairs, _, hidden_here = w_gate.shape
    side = routes.shape[1] + gate_weights.shape[1]
    mine = jnp.concatenate(
        [tokens, routes.astype(jnp.bfloat16), gate_weights, jnp.zeros((rows_here, LANES - side), jnp.bfloat16)], axis=1
    )
    line = jnp.concatenate([mine] + [rotate(mine, "group", k, 2) for k in range(1, chips)], axis=0)
    plane = jnp.concatenate([line] + [rotate(line, "local", k, 1) for k in range(1, locals_)], axis=0)
    x = jnp.concatenate([plane, other_core(plane)], axis=0)
    half = plane.shape[0]
    keep, send = pl.pallas_call(
        experts_kernel,
        out_shape=(
            jax.ShapeDtypeStruct((half, width), jnp.float32),
            jax.ShapeDtypeStruct((half, width), jnp.bfloat16),
        ),
        compiler_params=pltpu.CompilerParams(vmem_limit_bytes=6 << 20),
    )(x, w_gate, w_up, w_down.reshape(pairs * hidden_here, width))
    total = keep + other_core(send).astype(jnp.float32)
    blocks = total.reshape(locals_, chips * rows_here, width)
    total = blocks[0]
    for k in range(1, locals_):
        back = rotate(blocks[k].astype(jnp.bfloat16), "local", -k, 1)
        total = total + back.astype(jnp.float32)
    blocks = total.reshape(chips, rows_here, width)
    total = blocks[0]
    for k in range(1, chips):
        back = rotate(blocks[k].astype(jnp.bfloat16), "group", -k, 2)
        total = total + back.astype(jnp.float32)
    return total.astype(jnp.bfloat16)


def solution(mesh):
    return jax.shard_map(
        on_device,
        mesh=mesh,
        in_specs=(
            P(("parts", "group", "local"), None),
            P(("parts", "group", "local"), None),
            P(("parts", "group", "local"), None),
            P("group", None, "local"),
            P("group", None, "local"),
            P("group", "local", None),
        ),
        out_specs=P(("parts", "group", "local"), None),
        check_vma=False,
    )
```

time: 124 us -> 64.5 us (0.52)
  blocking collectives: 64.6 us -> 0 us
  matrix products: 29.8 us -> 0 us
  local copies, waits for them, and re-layouts: 4.71 us -> 17.2 us
  waiting for transfers between devices: 13.2 us -> 23.1 us
  Pallas kernels: 0 us -> 7.73 us
  starting transfers between devices: 9.8 us -> 14.4 us
    all_to_all x1 -> x0, blocking collectives: 47.5 us -> none  [on_device(): lax.all_to_all(outgoing, ('group', 'local'), split_axis=0, concat_axis=0,...]
    dot_general x8 -> x0, matrix products: 29.8 us -> none  [the longest x2 17.4 us: on_device(): jnp.dot(hidden, w_down[expert_slot], preferred_element_type=jnp.float32)]
    ppermute x0 -> x10, waiting for transfers between devices: none -> 23.1 us  [the longest x8 19.6 us: rotate(): lax.ppermute(value, axis, [(i, (i + shift * stride) % size) for i in rang...]
    all_gather x2 -> x0, blocking collectives: 17.1 us -> none  [the longest x1 12.7 us: on_device(): lax.all_gather(near_rows, 'local', axis=0, tiled=True)]
    unnamed x3 -> x6, local copies, waits for them, and re-layouts: 0.77 us -> 15.5 us
    ppermute x0 -> x10, starting transfers between devices: none -> 14.4 us  [the longest x8 14.1 us: rotate(): lax.ppermute(value, axis, [(i, (i + shift * stride) % size) for i in rang...]
    all_to_all x2 -> x0, waiting for transfers between devices: 13.2 us -> none  [the longest x1 9.2 us: on_device(): lax.all_to_all(send_rows, 'group', split_axis=0, concat_axis=0, tiled=True)]
    all_to_all x2 -> x0, starting transfers between devices: 9.8 us -> none  [the longest x1 6.33 us: on_device(): lax.all_to_all(send_weights, 'group', split_axis=0, concat_axis=0, tiled=...]
  transfers between devices with their start and end apart: 2 -> 10, of which waited for: 2 -> 9; matrix products, arithmetic and copies ran while one was open for 1% -> 0% of each run, Pallas kernels for 0% -> 0%
where the time goes in v1:
time: 64.5 us; the launch traced here: 64.2 us
  waiting for transfers between devices  23.1 us (36%)
  local copies, waits for them, and re-layouts  17.2 us (27%)
  starting transfers between devices  14.4 us (22%)
  Pallas kernels  7.73 us (12%)
  other arithmetic  1.64 us (3%)
    ppermute x8, waiting for transfers between devices, rotate(): lax.ppermute(value, axis, [(i, (i + shift * stride) % size) for i in rang...  19.6 us
    unnamed x6, local copies, waits for them, and re-layouts  15.5 us
    ppermute x8, starting transfers between devices, rotate(): lax.ppermute(value, axis, [(i, (i + shift * stride) % size) for i in rang...  14.1 us
    pallas_call x1, Pallas kernels, on_device(): pl.pallas_call(experts_kernel, out_shape=(jax.ShapeDtypeStruct((half, wid...  7.73 us
    ppermute x2, waiting for transfers between devices, other_core(): lax.ppermute(value, 'group', [(i, i ^ 1) for i in range(lax.axis_size('gr...  3.49 us
  transfers between devices with their start and end apart: 10, of which 9 were waited for; matrix products, arithmetic and copies ran while one was open for 0% of the time, Pallas kernels for 0%

profile of v1, /device:TPU:0, one launch (start us, length us, event | category | flops | bytes accessed | tf_op | source)
XLA Modules:
  0.0 64.2 jit_solution(2641125300457262392)
XLA Ops:
  0.0 0.7 %convert_element_type.25 = bf16[4,4]{1,0:T(4,128)(2,1)S(1)} convert(s32[4,4]{1,0:T(4,128)} %param.7) | non-fusion elementwise | flops 16 | bytes 96 | tf_op jit(solution)/shard_map/convert_element_type | solution.py:56
  0.7 0.9 %concatenate.14 = bf16[4,7296]{1,0:T(4,128)(2,1)S(1)} concatenate(bf16[4,7168]{1,0:T(4,128)(2,1)} %param.6, bf16[4,4]{1,0:T(4,128)(2,1)S(1)} %convert_element_type.25, bf16[4,8]{1,0:T(4,128)(2,1)} %param.8, bf16[4,116]{1,0:T(4,128)(2,1)S(1)} %broadcast_in_dim.3), dimensions={1} | concatenate | bytes 116736 | tf_op jit(solution)/shard_map/concatenate | solution.py:55
  1.6 5.1 %collective-permute-start.2 = (bf16[4,7296]{1,0:T(4,128)(2,1)S(1)}, bf16[4,7296]{1,0:T(4,128)(2,1)S(1)}, u32[]{:S(2)}, u32[]{:S(2)}) collective-permute-start(bf16[4,7296]{1,0:T(4,128)(2,1)S(1)} %concatenate.14), channel_id=1, source_target_pairs={{0,12},{2,14},{4,0},{6,2},{8,4},{10,6},{12,8},{14,10},{1,13},{3,15... | collective-permute-start | bytes 175112 | tf_op jit(solution)/shard_map/ppermute | solution.py:13
  6.7 1.0 %collective-permute-start = (bf16[4,7296]{1,0:T(4,128)(2,1)S(1)}, bf16[4,7296]{1,0:T(4,128)(2,1)S(1)}, u32[]{:S(2)}, u32[]{:S(2)}) collective-permute-start(bf16[4,7296]{1,0:T(4,128)(2,1)S(1)} %concatenate.14), channel_id=1, source_target_pairs={{0,4},{2,6},{4,8},{6,10},{8,12},{10,14},{12,0},{14,2},{1,5},{3,7},... | collective-permute-start | bytes 175112 | tf_op jit(solution)/shard_map/ppermute | solution.py:13
  7.7 1.3 %collective-permute-done.2 = bf16[4,7296]{1,0:T(4,128)(2,1)S(1)} collective-permute-done((bf16[4,7296]{1,0:T(4,128)(2,1)S(1)}, bf16[4,7296]{1,0:T(4,128)(2,1)S(1)}, u32[]{:S(2)}, u32[]{:S(2)}) %collective-permute-start.2) | collective-permute-done | bytes 58400 | tf_op jit(solution)/shard_map/ppermute | solution.py:13
  9.0 2.9 %collective-permute-done.1 = bf16[4,7296]{1,0:T(4,128)(2,1)S(1)} collective-permute-done((bf16[4,7296]{1,0:T(4,128)(2,1)S(1)}, bf16[4,7296]{1,0:T(4,128)(2,1)S(1)}, u32[]{:S(2)}, u32[]{:S(2)}) %collective-permute-start.1) | collective-permute-done | bytes 58400 | tf_op jit(solution)/shard_map/ppermute | solution.py:13
  11.9 0.8 %collective-permute-done = bf16[4,7296]{1,0:T(4,128)(2,1)S(1)} collective-permute-done((bf16[4,7296]{1,0:T(4,128)(2,1)S(1)}, bf16[4,7296]{1,0:T(4,128)(2,1)S(1)}, u32[]{:S(2)}, u32[]{:S(2)}) %collective-permute-start) | collective-permute-done | bytes 58400 | tf_op jit(solution)/shard_map/ppermute | solution.py:13
  12.8 1.6 %collective-permute-start.3 = (bf16[16,7296]{1,0:T(8,128)(2,1)S(1)}, bf16[16,7296]{1,0:T(8,128)(2,1)S(1)}, u32[]{:S(2)}, u32[]{:S(2)}) collective-permute-start(bf16[16,7296]{1,0:T(8,128)(2,1)S(1)} %pad_maximum_fusion), channel_id=1, source_target_pairs={{0,1},{1,0},{2,3},{3,2},{4,5},{5,4},{6,7},{7,6},{8,9},{9,8},{10,11... | collective-permute-start | bytes 700424 | tf_op jit(solution)/shard_map/ppermute | solution.py:13
  14.4 4.5 %collective-permute-done.3 = bf16[16,7296]{1,0:T(8,128)(2,1)S(1)} collective-permute-done((bf16[16,7296]{1,0:T(8,128)(2,1)S(1)}, bf16[16,7296]{1,0:T(8,128)(2,1)S(1)}, u32[]{:S(2)}, u32[]{:S(2)}) %collective-permute-start.3) | collective-permute-done | bytes 233504 | tf_op jit(solution)/shard_map/ppermute | solution.py:13
  18.9 0.3 concatenate.16
  19.3 1.8 %collective-permute-done.4 = bf16[32,7296]{1,0:T(8,128)(2,1)S(1)} collective-permute-done((bf16[32,7296]{1,0:T(8,128)(2,1)S(1)}, bf16[32,7296]{1,0:T(8,128)(2,1)S(1)}, u32[]{:S(2)}, u32[]{:S(2)}) %collective-permute-start.4) | collective-permute-done | bytes 466976 | tf_op jit(solution)/shard_map/ppermute | solution.py:17
  21.1 0.4 concatenate.17.x_ref
  21.5 5.2 %copy-done = bf16[2,7168,512]{2,1,0:T(8,128)(2,1)S(1)} copy-done((bf16[2,7168,512]{2,1,0:T(8,128)(2,1)S(1)}, bf16[2,7168,512]{2,1,0:T(8,128)(2,1)}, u32[]{:S(2)}) %copy-start) | copy-done | bytes 14680088
  26.7 5.2 %copy-done.1 = bf16[2,7168,512]{2,1,0:T(8,128)(2,1)S(1)} copy-done((bf16[2,7168,512]{2,1,0:T(8,128)(2,1)S(1)}, bf16[2,7168,512]{2,1,0:T(8,128)(2,1)}, u32[]{:S(2)}) %copy-start.1) | copy-done | bytes 14680088
  31.9 5.2 %copy-done.2 = bf16[2,512,7168]{2,1,0:T(8,128)(2,1)S(1)} copy-done((bf16[2,512,7168]{2,1,0:T(8,128)(2,1)S(1)}, bf16[2,512,7168]{2,1,0:T(8,128)(2,1)}, u32[]{:S(2)}) %copy-start.2) | copy-done | bytes 14680088
  37.1 7.7 %shard_map.64 = (f32[32,7168]{1,0:T(8,128)S(1)}, bf16[32,7168]{1,0:T(8,128)(2,1)S(1)}) custom-call(bf16[64,7296]{1,0:T(8,128)(2,1)S(1)} %concatenate.17.x_ref, bf16[2,7168,512]{2,1,0:T(8,128)(2,1)S(1)} %copy-done, bf16[2,7168,512]{2,1,0:T(8,128)(2,1)S(1)} %copy-done.1, bf16[1024,7168]{1,0:T(8,128)(2,1)S(1)} %bitcast.1), custom_call_target="tpu_custom_call" | custom-call | tf_op jit(solution)/shard_map/pallas_call | solution.py:62
  45.0 1.7 %collective-permute-done.5 = bf16[32,7168]{1,0:T(8,128)(2,1)S(1)} collective-permute-done((bf16[32,7168]{1,0:T(8,128)(2,1)S(1)}, bf16[32,7168]{1,0:T(8,128)(2,1)S(1)}, u32[]{:S(2)}, u32[]{:S(2)}) %collective-permute-start.5) | collective-permute-done | bytes 458784 | tf_op jit(solution)/shard_map/ppermute | solution.py:17
  46.8 1.6 %collective-permute-start.6 = (bf16[16,7168]{1,0:T(8,128)(2,1)S(1)}, bf16[16,7168]{1,0:T(8,128)(2,1)S(1)}, u32[]{:S(2)}, u32[]{:S(2)}) collective-permute-start(bf16[16,7168]{1,0:T(8,128)(2,1)S(1)} %slice.49), channel_id=1, source_target_pairs={{0,1},{1,0},{2,3},{3,2},{4,5},{5,4},{6,7},{7,6},{8,9},{9,8},{10,11... | collective-permute-start | bytes 688136 | tf_op jit(solution)/shard_map/ppermute | solution.py:13
  48.4 6.1 %collective-permute-done.6 = bf16[16,7168]{1,0:T(8,128)(2,1)S(1)} collective-permute-done((bf16[16,7168]{1,0:T(8,128)(2,1)S(1)}, bf16[16,7168]{1,0:T(8,128)(2,1)S(1)}, u32[]{:S(2)}, u32[]{:S(2)}) %collective-permute-start.6) | collective-permute-done | bytes 229408 | tf_op jit(solution)/shard_map/ppermute | solution.py:13
  54.6 2.0 %collective-permute-start.7 = (bf16[4,7168]{1,0:T(4,128)(2,1)S(1)}, bf16[4,7168]{1,0:T(4,128)(2,1)S(1)}, u32[]{:S(2)}, u32[]{:S(2)}) collective-permute-start(bf16[4,7168]{1,0:T(4,128)(2,1)S(1)} %get-tuple-element.11), channel_id=1, source_target_pairs={{0,12},{2,14},{4,0},{6,2},{8,4},{10,6},{12,8},{14,10},{1,13},{3,15... | collective-permute-start | bytes 172040 | tf_op jit(solution)/shard_map/ppermute | solution.py:13
  56.7 2.8 %collective-permute-start.8 = (bf16[4,7168]{1,0:T(4,128)(2,1)S(1)}, bf16[4,7168]{1,0:T(4,128)(2,1)S(1)}, u32[]{:S(2)}, u32[]{:S(2)}) collective-permute-start(bf16[4,7168]{1,0:T(4,128)(2,1)S(1)} %get-tuple-element.13), channel_id=1, source_target_pairs={{0,8},{2,10},{4,12},{6,14},{8,0},{10,2},{12,4},{14,6},{1,9},{3,11}... | collective-permute-start | bytes 172040 | tf_op jit(solution)/shard_map/ppermute | solution.py:13
  59.5 3.1 %collective-permute-done.9 = bf16[4,7168]{1,0:T(4,128)(2,1)S(1)} collective-permute-done((bf16[4,7168]{1,0:T(4,128)(2,1)S(1)}, bf16[4,7168]{1,0:T(4,128)(2,1)S(1)}, u32[]{:S(2)}, u32[]{:S(2)}) %collective-permute-start.9) | collective-permute-done | bytes 57376 | tf_op jit(solution)/shard_map/ppermute | solution.py:13
  62.6 0.9 %collective-permute-done.8 = bf16[4,7168]{1,0:T(4,128)(2,1)S(1)} collective-permute-done((bf16[4,7168]{1,0:T(4,128)(2,1)S(1)}, bf16[4,7168]{1,0:T(4,128)(2,1)S(1)}, u32[]{:S(2)}, u32[]{:S(2)}) %collective-permute-start.8) | collective-permute-done | bytes 57376 | tf_op jit(solution)/shard_map/ppermute | solution.py:13
  63.5 0.7 %fusion.2 = bf16[4,7168]{1,0:T(4,128)(2,1)} fusion(f32[16,7168]{1,0:T(8,128)S(1)} %get-tuple-element.10, bf16[4,7168]{1,0:T(4,128)(2,1)S(1)} %collective-permute-done.9, bf16[4,7168]{1,0:T(4,128)(2,1)S(1)} %collective-permute-done.8, bf16[4,7168]{1,0:T(4,128)(2,1)S(1)} %collective-permute-done.7), kind=kLoop, calls=%fused_computation.7 | loop fusion | flops 200704 | bytes 344064 | tf_op jit(solution)/shard_map/convert_element_type | solution.py:81
  (14 shorter events, 0.8 us)
Async XLA Ops:
  1.6 7.4 %collective-permute-start.2 = (bf16[4,7296]{1,0:T(4,128)(2,1)S(1)}, bf16[4,7296]{1,0:T(4,128)(2,1)S(1)}, u32[]{:S(2)}, u32[]{:S(2)}) collective-permute-start(bf16[4,7296]{1,0:T(4,128)(2,1)S(1)} %concatenate.14), channel_id=1, source_target_pairs={{0,12},{2,14},{4,0},{6,2},{8,4},{10,6},{12,8},{14,10},{1,13},{3,15... | collective-permute-start | bytes 175112 | tf_op jit(solution)/shard_map/ppermute | solution.py:13
  6.7 5.2 %collective-permute-start.1 = (bf16[4,7296]{1,0:T(4,128)(2,1)S(1)}, bf16[4,7296]{1,0:T(4,128)(2,1)S(1)}, u32[]{:S(2)}, u32[]{:S(2)}) collective-permute-start(bf16[4,7296]{1,0:T(4,128)(2,1)S(1)} %concatenate.14), channel_id=1, source_target_pairs={{0,8},{2,10},{4,12},{6,14},{8,0},{10,2},{12,4},{14,6},{1,9},{3,11}... | collective-permute-start | bytes 175112 | tf_op jit(solution)/shard_map/ppermute | solution.py:13
  6.7 6.0 %collective-permute-start = (bf16[4,7296]{1,0:T(4,128)(2,1)S(1)}, bf16[4,7296]{1,0:T(4,128)(2,1)S(1)}, u32[]{:S(2)}, u32[]{:S(2)}) collective-permute-start(bf16[4,7296]{1,0:T(4,128)(2,1)S(1)} %concatenate.14), channel_id=1, source_target_pairs={{0,4},{2,6},{4,8},{6,10},{8,12},{10,14},{12,0},{14,2},{1,5},{3,7},... | collective-permute-start | bytes 175112 | tf_op jit(solution)/shard_map/ppermute | solution.py:13
  12.8 6.1 %collective-permute-start.3 = (bf16[16,7296]{1,0:T(8,128)(2,1)S(1)}, bf16[16,7296]{1,0:T(8,128)(2,1)S(1)}, u32[]{:S(2)}, u32[]{:S(2)}) collective-permute-start(bf16[16,7296]{1,0:T(8,128)(2,1)S(1)} %pad_maximum_fusion), channel_id=1, source_target_pairs={{0,1},{1,0},{2,3},{3,2},{4,5},{5,4},{6,7},{7,6},{8,9},{9,8},{10,11... | collective-permute-start | bytes 700424 | tf_op jit(solution)/shard_map/ppermute | solution.py:13
  19.2 1.9 %collective-permute-start.4 = (bf16[32,7296]{1,0:T(8,128)(2,1)S(1)}, bf16[32,7296]{1,0:T(8,128)(2,1)S(1)}, u32[]{:S(2)}, u32[]{:S(2)}) collective-permute-start(bf16[32,7296]{1,0:T(8,128)(2,1)S(1)} %concatenate.16), channel_id=1, source_target_pairs={{0,2},{2,0},{4,6},{6,4},{8,10},{10,8},{12,14},{14,12},{1,3},{3,1},... | collective-permute-start | bytes 1400840 | tf_op jit(solution)/shard_map/ppermute | solution.py:17
  21.5 5.2 %copy-start = (bf16[2,7168,512]{2,1,0:T(8,128)(2,1)S(1)}, bf16[2,7168,512]{2,1,0:T(8,128)(2,1)}, u32[]{:S(2)}) copy-start(bf16[2,7168,512]{2,1,0:T(8,128)(2,1)} %gate_ref.1) | copy-start | bytes 44040196
  26.7 5.2 %copy-start.1 = (bf16[2,7168,512]{2,1,0:T(8,128)(2,1)S(1)}, bf16[2,7168,512]{2,1,0:T(8,128)(2,1)}, u32[]{:S(2)}) copy-start(bf16[2,7168,512]{2,1,0:T(8,128)(2,1)} %up_ref.1) | copy-start | bytes 44040196
  31.9 5.2 %copy-start.2 = (bf16[2,512,7168]{2,1,0:T(8,128)(2,1)S(1)}, bf16[2,512,7168]{2,1,0:T(8,128)(2,1)}, u32[]{:S(2)}) copy-start(bf16[2,512,7168]{2,1,0:T(8,128)(2,1)} %param.11) | copy-start | bytes 44040196
  44.8 1.9 %collective-permute-start.5 = (bf16[32,7168]{1,0:T(8,128)(2,1)S(1)}, bf16[32,7168]{1,0:T(8,128)(2,1)S(1)}, u32[]{:S(2)}, u32[]{:S(2)}) collective-permute-start(bf16[32,7168]{1,0:T(8,128)(2,1)S(1)} %get-tuple-element.8), channel_id=1, source_target_pairs={{0,2},{2,0},{4,6},{6,4},{8,10},{10,8},{12,14},{14,12},{1,3},{3,1},... | collective-permute-start | bytes 1376264 | tf_op jit(solution)/shard_map/ppermute | solution.py:17
  46.8 7.7 %collective-permute-start.6 = (bf16[16,7168]{1,0:T(8,128)(2,1)S(1)}, bf16[16,7168]{1,0:T(8,128)(2,1)S(1)}, u32[]{:S(2)}, u32[]{:S(2)}) collective-permute-start(bf16[16,7168]{1,0:T(8,128)(2,1)S(1)} %slice.49), channel_id=1, source_target_pairs={{0,1},{1,0},{2,3},{3,2},{4,5},{5,4},{6,7},{7,6},{8,9},{9,8},{10,11... | collective-permute-start | bytes 688136 | tf_op jit(solution)/shard_map/ppermute | solution.py:13
  54.6 4.9 %collective-permute-start.7 = (bf16[4,7168]{1,0:T(4,128)(2,1)S(1)}, bf16[4,7168]{1,0:T(4,128)(2,1)S(1)}, u32[]{:S(2)}, u32[]{:S(2)}) collective-permute-start(bf16[4,7168]{1,0:T(4,128)(2,1)S(1)} %get-tuple-element.11), channel_id=1, source_target_pairs={{0,12},{2,14},{4,0},{6,2},{8,4},{10,6},{12,8},{14,10},{1,13},{3,15... | collective-permute-start | bytes 172040 | tf_op jit(solution)/shard_map/ppermute | solution.py:13
  56.6 6.0 %collective-permute-start.9 = (bf16[4,7168]{1,0:T(4,128)(2,1)S(1)}, bf16[4,7168]{1,0:T(4,128)(2,1)S(1)}, u32[]{:S(2)}, u32[]{:S(2)}) collective-permute-start(bf16[4,7168]{1,0:T(4,128)(2,1)S(1)} %get-tuple-element.12), channel_id=1, source_target_pairs={{0,4},{2,6},{4,8},{6,10},{8,12},{10,14},{12,0},{14,2},{1,5},{3,7},... | collective-permute-start | bytes 172040 | tf_op jit(solution)/shard_map/ppermute | solution.py:13
  56.7 6.8 %collective-permute-start.8 = (bf16[4,7168]{1,0:T(4,128)(2,1)S(1)}, bf16[4,7168]{1,0:T(4,128)(2,1)S(1)}, u32[]{:S(2)}, u32[]{:S(2)}) collective-permute-start(bf16[4,7168]{1,0:T(4,128)(2,1)S(1)} %get-tuple-element.13), channel_id=1, source_target_pairs={{0,8},{2,10},{4,12},{6,14},{8,0},{10,2},{12,4},{14,6},{1,9},{3,11}... | collective-permute-start | bytes 172040 | tf_op jit(solution)/shard_map/ppermute | solution.py:13

commit v2 on v1

v2 whole, which is shorter than its diff:
```python
import functools

import jax
import jax.numpy as jnp
from jax import lax
from jax.experimental import pallas as pl
from jax.experimental.pallas import tpu as pltpu
from jax.sharding import PartitionSpec as P

LANES = 128
GROUPS_ROW = 4


def rotate(value, axis, shift, stride):
    size = lax.axis_size(axis)
    return lax.ppermute(value, axis, [(i, (i + shift * stride) % size) for i in range(size)])


def other_core(value):
    return lax.ppermute(value, "group", [(i, i ^ 1) for i in range(lax.axis_size("group"))])


def pack_kernel(tokens_ref, routes_ref, weights_ref, out_ref):
    rows, width = tokens_ref.shape
    side = routes_ref.shape[1] + weights_ref.shape[1]
    out_ref[:, :width] = tokens_ref[...]
    out_ref[:, width:] = jnp.concatenate(
        [
            routes_ref[...].astype(jnp.float32),
            weights_ref[...].astype(jnp.float32),
            jnp.zeros((rows, LANES - side), jnp.float32),
        ],
        axis=1,
    ).astype(jnp.bfloat16)


def pack(tokens, routes, gate_weights):
    rows, width = tokens.shape
    return pl.pallas_call(
        pack_kernel,
        out_shape=jax.ShapeDtypeStruct((rows, width + LANES), jnp.bfloat16),
        compiler_params=pltpu.CompilerParams(vmem_limit_bytes=2 << 20),
    )(tokens, routes, gate_weights)


def fetch_kernel(source_ref, after_ref, out_ref, sem):
    copy = pltpu.make_async_copy(source_ref, out_ref, sem)
    copy.start()
    copy.wait()


def fetch(weights, after, limit):
    nbytes = weights.size * 2
    return pl.pallas_call(
        fetch_kernel,
        out_shape=jax.ShapeDtypeStruct(weights.shape, weights.dtype),
        in_specs=[pl.BlockSpec(memory_space=pl.ANY)] * 2,
        out_specs=pl.BlockSpec(memory_space=pltpu.VMEM),
        scratch_shapes=[pltpu.SemaphoreType.DMA],
        compiler_params=pltpu.CompilerParams(vmem_limit_bytes=limit << 20),
        cost_estimate=pl.CostEstimate(flops=0, bytes_accessed=nbytes, transcendentals=0),
    )(weights, after)


def experts_kernel(count, *refs):
    pieces, (gate_ref, up_ref, down_hbm, keep_ref, send_ref, down_ref, x_ref, acts_ref, sems) = refs[:count], refs[count:]
    depth, width = down_ref.shape
    pairs = gate_ref.shape[0]
    hidden_here = depth // pairs
    keep_rows = keep_ref.shape[0]
    chunks = sems.shape[0]
    step = width // chunks

    def piece(c):
        columns = pl.ds(pl.multiple_of(c * step, LANES), step)
        return columns, pltpu.make_async_copy(down_hbm.at[:, columns], down_ref.at[:, columns], sems.at[c])

    for c in range(chunks):
        piece(c)[1].start()
    group = lax.axis_index("group").astype(jnp.float32)
    first = 0
    for part in pieces:
        x_ref[first : first + part.shape[0], :] = part[:, :width]
        first += part.shape[0]
    side = jnp.concatenate([part[:, width:] for part in pieces], axis=0).astype(jnp.float32)
    rows = x_ref.shape[0]
    acts_ref[...] = jnp.zeros_like(acts_ref)

    def enter(c, carry):
        depths = pl.ds(pl.multiple_of(c * step, LANES), step)
        x = x_ref[:, depths]
        for e in range(pairs):
            acts_ref[e, 0] += jnp.dot(x, gate_ref[e, depths, :], preferred_element_type=jnp.float32)
            acts_ref[e, 1] += jnp.dot(x, up_ref[e, depths, :], preferred_element_type=jnp.float32)
        return carry

    lax.fori_loop(0, chunks, enter, 0)
    hidden, weight = [], []
    for e in range(pairs):
        total = jnp.zeros((rows, 1), jnp.float32)
        for k in range(GROUPS_ROW):
            column = GROUPS_ROW + k * pairs + e
            total = total + jnp.where(side[:, k : k + 1] == group, side[:, column : column + 1], 0.0)
        weight.append(total)
        gate_act = acts_ref[e, 0]
        hidden.append((gate_act / (1.0 + jnp.exp(-gate_act)) * acts_ref[e, 1]).astype(jnp.bfloat16))

    def down(c, carry):
        columns, copy = piece(c)
        copy.wait()
        y = jnp.zeros((rows, step), jnp.float32)
        for e in range(pairs):
            part = down_ref[e * hidden_here : (e + 1) * hidden_here, columns]
            y = y + weight[e] * jnp.dot(hidden[e], part, preferred_element_type=jnp.float32)
        keep_ref[:, columns] = y[:keep_rows]
        send_ref[:, columns] = y[keep_rows:].astype(jnp.bfloat16)
        return carry

    lax.fori_loop(0, chunks, down, 0)


def on_device(tokens, routes, gate_weights, w_gate, w_up, w_down):
    chips = lax.axis_size("group") // 2
    locals_ = lax.axis_size("local")
    rows_here, width = tokens.shape
    pairs, _, hidden_here = w_gate.shape
    mine = pack(tokens, routes, gate_weights)
    others = [rotate(mine, "group", k, 2) for k in range(1, chips)]
    gate_here, others = lax.optimization_barrier((fetch(w_gate, mine, 34), others))
    line = jnp.concatenate([mine] + others, axis=0)
    crossed = [rotate(line, "local", k, 1) for k in range(1, locals_)]
    across_line = other_core(line)
    up_here, crossed = lax.optimization_barrier((fetch(w_up, line, 18), crossed))
    pieces = [line] + crossed + [across_line] + [other_core(part) for part in crossed]
    half = locals_ * chips * rows_here
    keep, send = pl.pallas_call(
        functools.partial(experts_kernel, len(pieces)),
        out_shape=(
            jax.ShapeDtypeStruct((half, width), jnp.float32),
            jax.ShapeDtypeStruct((half, width), jnp.bfloat16),
        ),
        in_specs=[pl.BlockSpec(memory_space=pltpu.VMEM)] * (len(pieces) + 2) + [pl.BlockSpec(memory_space=pl.ANY)],
        scratch_shapes=[
            pltpu.VMEM((pairs * hidden_here, width), jnp.bfloat16),
            pltpu.VMEM((2 * half, width), jnp.bfloat16),
            pltpu.VMEM((pairs, 2, 2 * half, hidden_here), jnp.float32),
            pltpu.SemaphoreType.DMA((7,)),
        ],
        compiler_params=pltpu.CompilerParams(vmem_limit_bytes=18 << 20),
    )(*pieces, gate_here, up_here, w_down.reshape(pairs * hidden_here, width))
    total = keep + other_core(send).astype(jnp.float32)
    blocks = total.reshape(locals_, chips * rows_here, width)
    total = blocks[0]
    for k in range(1, locals_):
        back = rotate(blocks[k].astype(jnp.bfloat16), "local", -k, 1)
        total = total + back.astype(jnp.float32)
    blocks = total.reshape(chips, rows_here, width)
    total = blocks[0]
    for k in range(1, chips):
        back = rotate(blocks[k].astype(jnp.bfloat16), "group", -k, 2)
        total = total + back.astype(jnp.float32)
    return total.astype(jnp.bfloat16)


def solution(mesh):
    return jax.shard_map(
        on_device,
        mesh=mesh,
        in_specs=(
            P(("parts", "group", "local"), None),
            P(("parts", "group", "local"), None),
            P(("parts", "group", "local"), None),
            P("group", None, "local"),
            P("group", None, "local"),
            P("group", "local", None),
        ),
        out_specs=P(("parts", "group", "local"), None),
        check_vma=False,
    )
```

time: 64.5 us -> 53.7 us (0.83)
  local copies, waits for them, and re-layouts: 17.2 us -> 7.45 us
  Pallas kernels: 7.73 us -> 15.9 us
  waiting for transfers between devices: 23.1 us -> 15.8 us
  starting transfers between devices: 14.4 us -> 13.2 us
  other arithmetic: 1.64 us -> 0.96 us
    pallas_call x1 -> x4, Pallas kernels: 7.73 us -> 15.9 us  [the longest x1 9.67 us: on_device(): pl.pallas_call(functools.partial(experts_kernel, len(pieces)), out_shape=...]
    unnamed x6 -> x8, local copies, waits for them, and re-layouts: 15.5 us -> 7.35 us
    ppermute x8, waiting for transfers between devices: 19.6 us -> 13.2 us  [rotate(): lax.ppermute(value, axis, [(i, (i + shift * stride) % size) for i in rang...]
    ppermute x8, starting transfers between devices: 14.1 us -> 12.2 us  [rotate(): lax.ppermute(value, axis, [(i, (i + shift * stride) % size) for i in rang...]
    concatenate x3 -> x0, local copies, waits for them, and re-layouts: 1.58 us -> none  [the longest x1 0.91 us: on_device(): jnp.concatenate([tokens, routes.astype(jnp.bfloat16), gate_weights, jnp.z...]
    ppermute x2 -> x3, waiting for transfers between devices: 3.49 us -> 2.56 us  [other_core(): lax.ppermute(value, 'group', [(i, i ^ 1) for i in range(lax.axis_size('gr...]
    ppermute x2 -> x3, starting transfers between devices: 0.27 us -> 1.01 us  [other_core(): lax.ppermute(value, 'group', [(i, i ^ 1) for i in range(lax.axis_size('gr...]
    convert_element_type x1 -> x0, other arithmetic: 0.68 us -> none  [on_device(): routes.astype(jnp.bfloat16)]
  transfers between devices with their start and end apart: 10 -> 11, of which waited for: 9 -> 6; matrix products, arithmetic and copies ran while one was open for 0% -> 0% of each run, Pallas kernels for 0% -> 12%
where the time goes in v2:
time: 53.7 us; the launch traced here: 53.4 us
  Pallas kernels  15.9 us (30%)
  waiting for transfers between devices  15.8 us (29%)
  starting transfers between devices  13.2 us (25%)
  local copies, waits for them, and re-layouts  7.45 us (14%)
  other arithmetic  0.96 us (2%)
    ppermute x8, waiting for transfers between devices, rotate(): lax.ppermute(value, axis, [(i, (i + shift * stride) % size) for i in rang...  13.2 us
    ppermute x8, starting transfers between devices, rotate(): lax.ppermute(value, axis, [(i, (i + shift * stride) % size) for i in rang...  12.2 us
    pallas_call x1, Pallas kernels, on_device(): pl.pallas_call(functools.partial(experts_kernel, len(pieces)), out_shape=...  9.67 us
    unnamed x8, local copies, waits for them, and re-layouts  7.35 us
    pallas_call x2, Pallas kernels, fetch(): pl.pallas_call(fetch_kernel, out_shape=jax.ShapeDtypeStruct(weights.shape...  6.16 us
    ppermute x3, waiting for transfers between devices, other_core(): lax.ppermute(value, 'group', [(i, i ^ 1) for i in range(lax.axis_size('gr...  2.56 us
  transfers between devices with their start and end apart: 11, of which 6 were waited for; matrix products, arithmetic and copies ran while one was open for 0% of the time, Pallas kernels for 12%

profile of v2, /device:TPU:0, one launch (start us, length us, event | category | flops | bytes accessed | tf_op | source)
XLA Modules:
  0.0 53.4 jit_solution(14455864984380410116)
XLA Ops:
  0.0 0.8 %copy-done.1 = bf16[4,7168]{1,0:T(4,128)(2,1)S(1)} copy-done((bf16[4,7168]{1,0:T(4,128)(2,1)S(1)}, bf16[4,7168]{1,0:T(4,128)(2,1)}, u32[]{:S(2)}) %copy-start.1) | copy-done | bytes 57368
  0.8 0.7 %copy-done.2 = s32[4,4]{1,0:T(4,128)S(1)} copy-done((s32[4,4]{1,0:T(4,128)S(1)}, s32[4,4]{1,0:T(4,128)}, u32[]{:S(2)}) %copy-start.2) | copy-done | bytes 88
  1.5 0.7 %copy-done.3 = bf16[4,8]{1,0:T(4,128)(2,1)S(1)} copy-done((bf16[4,8]{1,0:T(4,128)(2,1)S(1)}, bf16[4,8]{1,0:T(4,128)(2,1)}, u32[]{:S(2)}) %copy-start.3) | copy-done | bytes 88
  2.3 5.0 %collective-permute-start.2 = (bf16[4,7296]{1,0:T(4,128)(2,1)S(1)}, bf16[4,7296]{1,0:T(4,128)(2,1)S(1)}, u32[]{:S(2)}, u32[]{:S(2)}) collective-permute-start(bf16[4,7296]{1,0:T(4,128)(2,1)S(1)} %shard_map.64.after_ref), channel_id=1, source_target_pairs={{0,12},{2,14},{4,0},{6,2},{8,4},{10,6},{12,8},{14,10},{1,13},{3,15... | collective-permute-start | bytes 175112 | tf_op jit(solution)/shard_map/ppermute | solution.py:16
  7.3 1.0 %collective-permute-start = (bf16[4,7296]{1,0:T(4,128)(2,1)S(1)}, bf16[4,7296]{1,0:T(4,128)(2,1)S(1)}, u32[]{:S(2)}, u32[]{:S(2)}) collective-permute-start(bf16[4,7296]{1,0:T(4,128)(2,1)S(1)} %shard_map.64.after_ref), channel_id=1, source_target_pairs={{0,4},{2,6},{4,8},{6,10},{8,12},{10,14},{12,0},{14,2},{1,5},{3,7},... | collective-permute-start | bytes 175112 | tf_op jit(solution)/shard_map/ppermute | solution.py:16
  8.3 5.2 %shard_map.65.refs_4_ = bf16[2,7168,512]{2,1,0:T(8,128)(2,1)S(1)} custom-call(bf16[2,7168,512]{2,1,0:T(8,128)(2,1)} %source_ref.2, bf16[4,7296]{1,0:T(4,128)(2,1)S(1)} %shard_map.64.after_ref), custom_call_target="tpu_custom_call" | custom-call | bytes 14680064 | tf_op jit(solution)/shard_map/pallas_call | solution.py:54
  13.5 0.1 pad_maximum_fusion.after_ref.refs_0_
  13.7 1.6 %collective-permute-start.3 = (bf16[16,7296]{1,0:T(8,128)(2,1)S(1)}, bf16[16,7296]{1,0:T(8,128)(2,1)S(1)}, u32[]{:S(2)}, u32[]{:S(2)}) collective-permute-start(bf16[16,7296]{1,0:T(8,128)(2,1)S(1)} %pad_maximum_fusion.after_ref.refs_0_), channel_id=1, source_target_pairs={{0,1},{1,0},{2,3},{3,2},{4,5},{5,4},{6,7},{7,6},{8,9},{9,8},{10,11... | collective-permute-start | bytes 700424 | tf_op jit(solution)/shard_map/ppermute | solution.py:16
  15.3 5.2 %copy-done = bf16[2,7168,512]{2,1,0:T(8,128)(2,1)S(1)} copy-done((bf16[2,7168,512]{2,1,0:T(8,128)(2,1)S(1)}, bf16[2,7168,512]{2,1,0:T(8,128)(2,1)}, u32[]{:S(2)}) %copy-start) | copy-done | bytes 14680088
  20.4 1.0 %shard_map.66.refs_5_ = bf16[2,7168,512]{2,1,0:T(8,128)(2,1)S(1)} custom-call(bf16[2,7168,512]{2,1,0:T(8,128)(2,1)S(1)} %copy-done, bf16[16,7296]{1,0:T(8,128)(2,1)S(1)} %pad_maximum_fusion.after_ref.refs_0_), custom_call_target="tpu_custom_call" | custom-call | bytes 14680064 | tf_op jit(solution)/shard_map/pallas_call | solution.py:54
  21.5 0.6 %collective-permute-start.5 = (bf16[16,7296]{1,0:T(8,128)(2,1)S(1)}, bf16[16,7296]{1,0:T(8,128)(2,1)S(1)}, u32[]{:S(2)}, u32[]{:S(2)}) collective-permute-start(bf16[16,7296]{1,0:T(8,128)(2,1)S(1)} %collective-permute-done.3.refs_1_), channel_id=1, source_target_pairs={{0,2},{2,0},{4,6},{6,4},{8,10},{10,8},{12,14},{14,12},{1,3},{3,1},... | collective-permute-start | bytes 700424 | tf_op jit(solution)/shard_map/ppermute | solution.py:20
  22.0 1.1 %collective-permute-done.5.refs_3_ = bf16[16,7296]{1,0:T(8,128)(2,1)S(1)} collective-permute-done((bf16[16,7296]{1,0:T(8,128)(2,1)S(1)}, bf16[16,7296]{1,0:T(8,128)(2,1)S(1)}, u32[]{:S(2)}, u32[]{:S(2)}) %collective-permute-start.5) | collective-permute-done | bytes 233504 | tf_op jit(solution)/shard_map/ppermute | solution.py:20
  23.1 9.7 %shard_map.67 = (f32[32,7168]{1,0:T(8,128)S(1)}, bf16[32,7168]{1,0:T(8,128)(2,1)S(1)}) custom-call(bf16[16,7296]{1,0:T(8,128)(2,1)S(1)} %pad_maximum_fusion.after_ref.refs_0_, bf16[16,7296]{1,0:T(8,128)(2,1)S(1)} %collective-permute-done.3.refs_1_, bf16[16,7296]{1,0:T(8,128)(2,1)S(1)} %collective-permute-done.4.refs_2_, ...), custom_call_target="tpu_custom_call" | custom-call | tf_op jit(solution)/shard_map/pallas_call | solution.py:136
  32.8 0.4 collective-permute-start.6
  33.3 1.4 %collective-permute-done.6 = bf16[32,7168]{1,0:T(8,128)(2,1)S(1)} collective-permute-done((bf16[32,7168]{1,0:T(8,128)(2,1)S(1)}, bf16[32,7168]{1,0:T(8,128)(2,1)S(1)}, u32[]{:S(2)}, u32[]{:S(2)}) %collective-permute-start.6) | collective-permute-done | bytes 458784 | tf_op jit(solution)/shard_map/ppermute | solution.py:20
  34.7 0.1 convert_add_fusion
  34.8 0.6 %collective-permute-start.7 = (bf16[16,7168]{1,0:T(8,128)(2,1)S(1)}, bf16[16,7168]{1,0:T(8,128)(2,1)S(1)}, u32[]{:S(2)}, u32[]{:S(2)}) collective-permute-start(bf16[16,7168]{1,0:T(8,128)(2,1)S(1)} %slice.49), channel_id=1, source_target_pairs={{0,1},{1,0},{2,3},{3,2},{4,5},{5,4},{6,7},{7,6},{8,9},{9,8},{10,11... | collective-permute-start | bytes 688136 | tf_op jit(solution)/shard_map/ppermute | solution.py:16
  35.4 7.4 %collective-permute-done.7 = bf16[16,7168]{1,0:T(8,128)(2,1)S(1)} collective-permute-done((bf16[16,7168]{1,0:T(8,128)(2,1)S(1)}, bf16[16,7168]{1,0:T(8,128)(2,1)S(1)}, u32[]{:S(2)}, u32[]{:S(2)}) %collective-permute-start.7) | collective-permute-done | bytes 229408 | tf_op jit(solution)/shard_map/ppermute | solution.py:16
  42.9 2.9 %collective-permute-start.8 = (bf16[4,7168]{1,0:T(4,128)(2,1)S(1)}, bf16[4,7168]{1,0:T(4,128)(2,1)S(1)}, u32[]{:S(2)}, u32[]{:S(2)}) collective-permute-start(bf16[4,7168]{1,0:T(4,128)(2,1)S(1)} %get-tuple-element.23), channel_id=1, source_target_pairs={{0,12},{2,14},{4,0},{6,2},{8,4},{10,6},{12,8},{14,10},{1,13},{3,15... | collective-permute-start | bytes 172040 | tf_op jit(solution)/shard_map/ppermute | solution.py:16
  45.8 1.1 %collective-permute-start.9 = (bf16[4,7168]{1,0:T(4,128)(2,1)S(1)}, bf16[4,7168]{1,0:T(4,128)(2,1)S(1)}, u32[]{:S(2)}, u32[]{:S(2)}) collective-permute-start(bf16[4,7168]{1,0:T(4,128)(2,1)S(1)} %get-tuple-element.25), channel_id=1, source_target_pairs={{0,8},{2,10},{4,12},{6,14},{8,0},{10,2},{12,4},{14,6},{1,9},{3,11}... | collective-permute-start | bytes 172040 | tf_op jit(solution)/shard_map/ppermute | solution.py:16
  46.9 1.0 %collective-permute-done.8 = bf16[4,7168]{1,0:T(4,128)(2,1)S(1)} collective-permute-done((bf16[4,7168]{1,0:T(4,128)(2,1)S(1)}, bf16[4,7168]{1,0:T(4,128)(2,1)S(1)}, u32[]{:S(2)}, u32[]{:S(2)}) %collective-permute-start.8) | collective-permute-done | bytes 57376 | tf_op jit(solution)/shard_map/ppermute | solution.py:16
  47.9 3.9 %collective-permute-done.10 = bf16[4,7168]{1,0:T(4,128)(2,1)S(1)} collective-permute-done((bf16[4,7168]{1,0:T(4,128)(2,1)S(1)}, bf16[4,7168]{1,0:T(4,128)(2,1)S(1)}, u32[]{:S(2)}, u32[]{:S(2)}) %collective-permute-start.10) | collective-permute-done | bytes 57376 | tf_op jit(solution)/shard_map/ppermute | solution.py:16
  51.8 1.0 %collective-permute-done.9 = bf16[4,7168]{1,0:T(4,128)(2,1)S(1)} collective-permute-done((bf16[4,7168]{1,0:T(4,128)(2,1)S(1)}, bf16[4,7168]{1,0:T(4,128)(2,1)S(1)}, u32[]{:S(2)}, u32[]{:S(2)}) %collective-permute-start.9) | collective-permute-done | bytes 57376 | tf_op jit(solution)/shard_map/ppermute | solution.py:16
  52.7 0.7 %fusion.2 = bf16[4,7168]{1,0:T(4,128)(2,1)} fusion(f32[16,7168]{1,0:T(8,128)S(1)} %get-tuple-element.22, bf16[4,7168]{1,0:T(4,128)(2,1)S(1)} %collective-permute-done.10, bf16[4,7168]{1,0:T(4,128)(2,1)S(1)} %collective-permute-done.9, bf16[4,7168]{1,0:T(4,128)(2,1)S(1)} %collective-permute-done.8), kind=kLoop, calls=%fused_computation.7 | loop fusion | flops 200704 | bytes 344064 | tf_op jit(solution)/shard_map/convert_element_type | solution.py:162
  (16 shorter events, 0.3 us)
Async XLA Ops:
  0.0 0.8 %copy-start.1 = (bf16[4,7168]{1,0:T(4,128)(2,1)S(1)}, bf16[4,7168]{1,0:T(4,128)(2,1)}, u32[]{:S(2)}) copy-start(bf16[4,7168]{1,0:T(4,128)(2,1)} %tokens_ref.1) | copy-start | bytes 172036
  0.8 0.7 %copy-start.2 = (s32[4,4]{1,0:T(4,128)S(1)}, s32[4,4]{1,0:T(4,128)}, u32[]{:S(2)}) copy-start(s32[4,4]{1,0:T(4,128)} %routes_ref.1) | copy-start | bytes 196
  1.5 0.7 %copy-start.3 = (bf16[4,8]{1,0:T(4,128)(2,1)S(1)}, bf16[4,8]{1,0:T(4,128)(2,1)}, u32[]{:S(2)}) copy-start(bf16[4,8]{1,0:T(4,128)(2,1)} %weights_ref.1) | copy-start | bytes 196
  2.3 11.3 %collective-permute-start.2 = (bf16[4,7296]{1,0:T(4,128)(2,1)S(1)}, bf16[4,7296]{1,0:T(4,128)(2,1)S(1)}, u32[]{:S(2)}, u32[]{:S(2)}) collective-permute-start(bf16[4,7296]{1,0:T(4,128)(2,1)S(1)} %shard_map.64.after_ref), channel_id=1, source_target_pairs={{0,12},{2,14},{4,0},{6,2},{8,4},{10,6},{12,8},{14,10},{1,13},{3,15... | collective-permute-start | bytes 175112 | tf_op jit(solution)/shard_map/ppermute | solution.py:16
  7.3 6.2 %collective-permute-start.1 = (bf16[4,7296]{1,0:T(4,128)(2,1)S(1)}, bf16[4,7296]{1,0:T(4,128)(2,1)S(1)}, u32[]{:S(2)}, u32[]{:S(2)}) collective-permute-start(bf16[4,7296]{1,0:T(4,128)(2,1)S(1)} %shard_map.64.after_ref), channel_id=1, source_target_pairs={{0,8},{2,10},{4,12},{6,14},{8,0},{10,2},{12,4},{14,6},{1,9},{3,11}... | collective-permute-start | bytes 175112 | tf_op jit(solution)/shard_map/ppermute | solution.py:16
  7.3 6.2 %collective-permute-start = (bf16[4,7296]{1,0:T(4,128)(2,1)S(1)}, bf16[4,7296]{1,0:T(4,128)(2,1)S(1)}, u32[]{:S(2)}, u32[]{:S(2)}) collective-permute-start(bf16[4,7296]{1,0:T(4,128)(2,1)S(1)} %shard_map.64.after_ref), channel_id=1, source_target_pairs={{0,4},{2,6},{4,8},{6,10},{8,12},{10,14},{12,0},{14,2},{1,5},{3,7},... | collective-permute-start | bytes 175112 | tf_op jit(solution)/shard_map/ppermute | solution.py:16
  13.7 7.8 %collective-permute-start.3 = (bf16[16,7296]{1,0:T(8,128)(2,1)S(1)}, bf16[16,7296]{1,0:T(8,128)(2,1)S(1)}, u32[]{:S(2)}, u32[]{:S(2)}) collective-permute-start(bf16[16,7296]{1,0:T(8,128)(2,1)S(1)} %pad_maximum_fusion.after_ref.refs_0_), channel_id=1, source_target_pairs={{0,1},{1,0},{2,3},{3,2},{4,5},{5,4},{6,7},{7,6},{8,9},{9,8},{10,11... | collective-permute-start | bytes 700424 | tf_op jit(solution)/shard_map/ppermute | solution.py:16
  15.3 6.8 %collective-permute-start.4 = (bf16[16,7296]{1,0:T(8,128)(2,1)S(1)}, bf16[16,7296]{1,0:T(8,128)(2,1)S(1)}, u32[]{:S(2)}, u32[]{:S(2)}) collective-permute-start(bf16[16,7296]{1,0:T(8,128)(2,1)S(1)} %pad_maximum_fusion.after_ref.refs_0_), channel_id=1, source_target_pairs={{0,2},{2,0},{4,6},{6,4},{8,10},{10,8},{12,14},{14,12},{1,3},{3,1},... | collective-permute-start | bytes 700424 | tf_op jit(solution)/shard_map/ppermute | solution.py:20
  15.3 5.2 %copy-start = (bf16[2,7168,512]{2,1,0:T(8,128)(2,1)S(1)}, bf16[2,7168,512]{2,1,0:T(8,128)(2,1)}, u32[]{:S(2)}) copy-start(bf16[2,7168,512]{2,1,0:T(8,128)(2,1)} %source_ref.3) | copy-start | bytes 44040196
  21.5 1.7 %collective-permute-start.5 = (bf16[16,7296]{1,0:T(8,128)(2,1)S(1)}, bf16[16,7296]{1,0:T(8,128)(2,1)S(1)}, u32[]{:S(2)}, u32[]{:S(2)}) collective-permute-start(bf16[16,7296]{1,0:T(8,128)(2,1)S(1)} %collective-permute-done.3.refs_1_), channel_id=1, source_target_pairs={{0,2},{2,0},{4,6},{6,4},{8,10},{10,8},{12,14},{14,12},{1,3},{3,1},... | collective-permute-start | bytes 700424 | tf_op jit(solution)/shard_map/ppermute | solution.py:20
  32.8 1.9 %collective-permute-start.6 = (bf16[32,7168]{1,0:T(8,128)(2,1)S(1)}, bf16[32,7168]{1,0:T(8,128)(2,1)S(1)}, u32[]{:S(2)}, u32[]{:S(2)}) collective-permute-start(bf16[32,7168]{1,0:T(8,128)(2,1)S(1)} %get-tuple-element.20), channel_id=1, source_target_pairs={{0,2},{2,0},{4,6},{6,4},{8,10},{10,8},{12,14},{14,12},{1,3},{3,1},... | collective-permute-start | bytes 1376264 | tf_op jit(solution)/shard_map/ppermute | solution.py:20
  34.8 7.9 %collective-permute-start.7 = (bf16[16,7168]{1,0:T(8,128)(2,1)S(1)}, bf16[16,7168]{1,0:T(8,128)(2,1)S(1)}, u32[]{:S(2)}, u32[]{:S(2)}) collective-permute-start(bf16[16,7168]{1,0:T(8,128)(2,1)S(1)} %slice.49), channel_id=1, source_target_pairs={{0,1},{1,0},{2,3},{3,2},{4,5},{5,4},{6,7},{7,6},{8,9},{9,8},{10,11... | collective-permute-start | bytes 688136 | tf_op jit(solution)/shard_map/ppermute | solution.py:16
  42.9 5.0 %collective-permute-start.8 = (bf16[4,7168]{1,0:T(4,128)(2,1)S(1)}, bf16[4,7168]{1,0:T(4,128)(2,1)S(1)}, u32[]{:S(2)}, u32[]{:S(2)}) collective-permute-start(bf16[4,7168]{1,0:T(4,128)(2,1)S(1)} %get-tuple-element.23), channel_id=1, source_target_pairs={{0,12},{2,14},{4,0},{6,2},{8,4},{10,6},{12,8},{14,10},{1,13},{3,15... | collective-permute-start | bytes 172040 | tf_op jit(solution)/shard_map/ppermute | solution.py:16
  45.8 6.0 %collective-permute-start.10 = (bf16[4,7168]{1,0:T(4,128)(2,1)S(1)}, bf16[4,7168]{1,0:T(4,128)(2,1)S(1)}, u32[]{:S(2)}, u32[]{:S(2)}) collective-permute-start(bf16[4,7168]{1,0:T(4,128)(2,1)S(1)} %get-tuple-element.24), channel_id=1, source_target_pairs={{0,4},{2,6},{4,8},{6,10},{8,12},{10,14},{12,0},{14,2},{1,5},{3,7},... | collective-permute-start | bytes 172040 | tf_op jit(solution)/shard_map/ppermute | solution.py:16
  45.8 7.0 %collective-permute-start.9 = (bf16[4,7168]{1,0:T(4,128)(2,1)S(1)}, bf16[4,7168]{1,0:T(4,128)(2,1)S(1)}, u32[]{:S(2)}, u32[]{:S(2)}) collective-permute-start(bf16[4,7168]{1,0:T(4,128)(2,1)S(1)} %get-tuple-element.25), channel_id=1, source_target_pairs={{0,8},{2,10},{4,12},{6,14},{8,0},{10,2},{12,4},{14,6},{1,9},{3,11}... | collective-permute-start | bytes 172040 | tf_op jit(solution)/shard_map/ppermute | solution.py:16

commit v3 on v2

v3 whole, which is shorter than its diff:
```python
import functools

import jax
import jax.numpy as jnp
from jax import lax
from jax.experimental import pallas as pl
from jax.experimental.pallas import tpu as pltpu
from jax.sharding import PartitionSpec as P

LANES = 128
LEAST_ROWS = 128
GROUPS_ROW = 4


def rotate(value, axis, shift, stride):
    size = lax.axis_size(axis)
    return lax.ppermute(value, axis, [(i, (i + shift * stride) % size) for i in range(size)])


def other_core(value):
    return lax.ppermute(value, "group", [(i, i ^ 1) for i in range(lax.axis_size("group"))])


def pack(tokens, routes, gate_weights):
    zero = jnp.zeros((), jnp.bfloat16)
    width = tokens.shape[1]
    packed = lax.pad(tokens, zero, ((0, 0, 0), (0, LANES, 0)))
    first = width
    for side in (routes, gate_weights):
        last = first + side.shape[1]
        side = lax.pad(side, jnp.zeros((), side.dtype), ((0, 0, 0), (first, width + LANES - last, 0)))
        packed = packed + side.astype(jnp.bfloat16)
        first = last
    return packed


def fetch_kernel(source_ref, after_ref, out_ref, sem):
    copy = pltpu.make_async_copy(source_ref, out_ref, sem)
    copy.start()
    copy.wait()


def fetch(weights, after, limit):
    nbytes = weights.size * 2
    return pl.pallas_call(
        fetch_kernel,
        out_shape=jax.ShapeDtypeStruct(weights.shape, weights.dtype),
        in_specs=[pl.BlockSpec(memory_space=pl.ANY)] * 2,
        out_specs=pl.BlockSpec(memory_space=pltpu.VMEM),
        scratch_shapes=[pltpu.SemaphoreType.DMA],
        compiler_params=pltpu.CompilerParams(vmem_limit_bytes=limit << 20),
        cost_estimate=pl.CostEstimate(flops=0, bytes_accessed=nbytes, transcendentals=0),
    )(weights, after)


def experts_kernel(count, *refs):
    pieces, (gate_ref, up_ref, down_hbm), outs = refs[:count], refs[count : count + 3], refs[count + 3 : -4]
    down_ref, x_ref, acts_ref, sems = refs[-4:]
    depth, width = down_ref.shape
    pairs = gate_ref.shape[0]
    hidden_here = depth // pairs
    block = outs[0].shape[0]
    chunks = sems.shape[0]
    step = width // chunks

    def piece(c):
        columns = pl.ds(pl.multiple_of(c * step, LANES), step)
        return columns, pltpu.make_async_copy(down_hbm.at[:, columns], down_ref.at[:, columns], sems.at[c])

    for c in range(chunks):
        piece(c)[1].start()
    group = lax.axis_index("group").astype(jnp.float32)
    first = 0
    while first < x_ref.shape[0]:
        for part in pieces:
            x_ref[first : first + part.shape[0], :] = part[:, :width]
            first += part.shape[0]
    side = jnp.concatenate([part[:, width:] for part in pieces], axis=0).astype(jnp.float32)
    rows = side.shape[0]
    acts_ref[...] = jnp.zeros_like(acts_ref)

    half = width // 2

    def enter(c, carry):
        depths = pl.ds(pl.multiple_of(c * half, LANES), half)
        x = x_ref[:, depths]
        for e in range(pairs):
            acts_ref[e, 0] += jnp.dot(x, gate_ref[e, depths, :], preferred_element_type=jnp.float32)
            acts_ref[e, 1] += jnp.dot(x, up_ref[e, depths, :], preferred_element_type=jnp.float32)
        return carry

    lax.fori_loop(0, 2, enter, 0)
    hidden, weight = [], []
    for e in range(pairs):
        total = jnp.zeros((rows, 1), jnp.float32)
        for k in range(GROUPS_ROW):
            column = GROUPS_ROW + k * pairs + e
            total = total + jnp.where(side[:, k : k + 1] == group, side[:, column : column + 1], 0.0)
        weight.append(total)
        gate_act = acts_ref[e, 0]
        hidden.append((gate_act / (1.0 + jnp.exp(-gate_act)) * acts_ref[e, 1]).astype(jnp.bfloat16))

    def down(c, carry):
        columns, copy = piece(c)
        copy.wait()
        y = jnp.zeros((rows, step), jnp.float32)
        for e in range(pairs):
            part = down_ref[e * hidden_here : (e + 1) * hidden_here, columns]
            y = y + weight[e] * jnp.dot(hidden[e], part, preferred_element_type=jnp.float32)[:rows]
        for i, out in enumerate(outs):
            out[:, columns] = y[i * block : (i + 1) * block].astype(out.dtype)
        return carry

    lax.fori_loop(0, chunks, down, 0)


def join_kernel(blocks, *refs):
    total = refs[0][...]
    for ref in refs[1:-blocks]:
        total = total + ref[...].astype(jnp.float32)
    height = total.shape[0] // blocks
    for i, out in enumerate(refs[-blocks:]):
        out[...] = total[i * height : (i + 1) * height].astype(out.dtype)


def join(values, blocks, first):
    shape = (values[0].shape[0] // blocks, values[0].shape[1])
    return pl.pallas_call(
        functools.partial(join_kernel, blocks),
        out_shape=[
            jax.ShapeDtypeStruct(shape, jnp.bfloat16 if first + i else jnp.float32) for i in range(blocks)
        ],
        compiler_params=pltpu.CompilerParams(vmem_limit_bytes=4 << 20),
    )(*values)


def on_device(tokens, routes, gate_weights, w_gate, w_up, w_down):
    chips = lax.axis_size("group") // 2
    locals_ = lax.axis_size("local")
    rows_here, width = tokens.shape
    pairs, _, hidden_here = w_gate.shape
    mine = pack(tokens, routes, gate_weights)
    others = [rotate(mine, "group", k, 2) for k in range(1, chips)]
    gate_here, others = lax.optimization_barrier((fetch(w_gate, mine, 34), others))
    line = jnp.concatenate([mine] + others, axis=0)
    crossed = [rotate(line, "local", k, 1) for k in range(1, locals_)]
    across_line = other_core(line)
    up_here, crossed = lax.optimization_barrier((fetch(w_up, line, 26), crossed))
    pieces = [line] + crossed + [across_line] + [other_core(part) for part in crossed]
    block = chips * rows_here
    rows = 2 * locals_ * block
    padded = rows * max(1, LEAST_ROWS // rows)
    outs = pl.pallas_call(
        functools.partial(experts_kernel, len(pieces)),
        out_shape=[jax.ShapeDtypeStruct((block, width), jnp.float32)] * locals_
        + [jax.ShapeDtypeStruct((block, width), jnp.bfloat16)] * locals_,
        in_specs=[pl.BlockSpec(memory_space=pltpu.VMEM)] * (len(pieces) + 2) + [pl.BlockSpec(memory_space=pl.ANY)],
        scratch_shapes=[
            pltpu.VMEM((pairs * hidden_here, width), jnp.bfloat16),
            pltpu.VMEM((padded, width), jnp.bfloat16),
            pltpu.VMEM((pairs, 2, padded, hidden_here), jnp.float32),
            pltpu.SemaphoreType.DMA((7,)),
        ],
        compiler_params=pltpu.CompilerParams(vmem_limit_bytes=18 << 20),
    )(*pieces, gate_here, up_here, w_down.reshape(pairs * hidden_here, width))
    totals = [None] * locals_
    for k in reversed(range(locals_)):
        totals[k] = outs[k] + other_core(outs[locals_ + k]).astype(jnp.float32)
    home = [None] * chips
    backs = None
    for low, high in ((chips // 2, chips), (0, chips // 2)):
        if low == high:
            continue
        part = slice(low * rows_here, high * rows_here)
        sent = [totals[k][part].astype(jnp.bfloat16) for k in range(1, locals_)]
        if backs is not None:
            sent, backs = lax.optimization_barrier((sent, backs))
        backs = [rotate(sent[k - 1], "local", -k, 1) for k in range(1, locals_)]
        home[low:high] = join([totals[0][part]] + backs, high - low, low)
    result = home[0]
    for c in range(1, chips):
        result = result + rotate(home[c], "group", -c, 2).astype(jnp.float32)
    return result.astype(jnp.bfloat16)


def solution(mesh):
    return jax.shard_map(
        on_device,
        mesh=mesh,
        in_specs=(
            P(("parts", "group", "local"), None),
            P(("parts", "group", "local"), None),
            P(("parts", "group", "local"), None),
            P("group", None, "local"),
            P("group", None, "local"),
            P("group", "local", None),
        ),
        out_specs=P(("parts", "group", "local"), None),
        check_vma=False,
    )
```

time: 53.7 us -> 47.4 us (0.88)
  local copies, waits for them, and re-layouts: 7.45 us -> 0.05 us
  waiting for transfers between devices: 15.8 us -> 8.53 us
  starting transfers between devices: 13.2 us -> 17.6 us
  Pallas kernels: 15.9 us -> 18.3 us
  other arithmetic: 0.96 us -> 2.54 us
    unnamed x8 -> x0, local copies, waits for them, and re-layouts: 7.35 us -> none
    ppermute x8 -> x9, waiting for transfers between devices: 13.2 us -> 6.43 us  [rotate(): lax.ppermute(value, axis, [(i, (i + shift * stride) % size) for i in rang...]
    ppermute x8 -> x9, starting transfers between devices: 12.2 us -> 16.5 us  [rotate(): lax.ppermute(value, axis, [(i, (i + shift * stride) % size) for i in rang...]
    pallas_call x2, Pallas kernels: 6.16 us -> 10.4 us  [fetch(): pl.pallas_call(fetch_kernel, out_shape=jax.ShapeDtypeStruct(weights.shape...]
    pallas_call x1, Pallas kernels: 9.67 us -> 7.92 us  [on_device(): pl.pallas_call(functools.partial(experts_kernel, len(pieces)), out_shape=...]
    add x1 -> x2, other arithmetic: 0.08 us -> 0.98 us  [the longest x1 0.93 us: pack(): packed = packed + side.astype(jnp.bfloat16)]
    another operation x1 -> x2, other arithmetic: 0.06 us -> 0.74 us
    ppermute x3 -> x4, waiting for transfers between devices: 2.56 us -> 2.1 us  [other_core(): lax.ppermute(value, 'group', [(i, i ^ 1) for i in range(lax.axis_size('gr...]
  transfers between devices with their start and end apart: 11 -> 13, of which waited for: 6 -> 5; matrix products, arithmetic and copies ran while one was open for 0% -> 0% of each run, Pallas kernels for 12% -> 22%
where the time goes in v3:
time: 47.4 us; the launch traced here: 47.2 us
  Pallas kernels  18.3 us (39%)
  starting transfers between devices  17.6 us (37%)
  waiting for transfers between devices  8.53 us (18%)
  other arithmetic  2.54 us (5%)
    ppermute x9, starting transfers between devices, rotate(): lax.ppermute(value, axis, [(i, (i + shift * stride) % size) for i in rang...  16.5 us
    pallas_call x2, Pallas kernels, fetch(): pl.pallas_call(fetch_kernel, out_shape=jax.ShapeDtypeStruct(weights.shape...  10.4 us
    pallas_call x1, Pallas kernels, on_device(): pl.pallas_call(functools.partial(experts_kernel, len(pieces)), out_shape=...  7.92 us
    ppermute x9, waiting for transfers between devices, rotate(): lax.ppermute(value, axis, [(i, (i + shift * stride) % size) for i in rang...  6.43 us
    ppermute x4, waiting for transfers between devices, other_core(): lax.ppermute(value, 'group', [(i, i ^ 1) for i in range(lax.axis_size('gr...  2.1 us
    ppermute x4, starting transfers between devices, other_core(): lax.ppermute(value, 'group', [(i, i ^ 1) for i in range(lax.axis_size('gr...  1.15 us
  transfers between devices with their start and end apart: 13, of which 5 were waited for; matrix products, arithmetic and copies ran while one was open for 0% of the time, Pallas kernels for 22%

profile of v3, /device:TPU:0, one launch (start us, length us, event | category | flops | bytes accessed | tf_op | source)
XLA Modules:
  0.0 47.2 jit_solution(14344621716915462310)
XLA Ops:
  0.0 0.7 %convert.8 = bf16[4,4]{1,0:T(4,128)(2,1)S(1)} convert(s32[4,4]{1,0:T(4,128)} %param.7) | non-fusion elementwise | flops 16 | bytes 96 | tf_op jit(solution)/shard_map/convert.2
  0.7 0.9 %pad_add_fusion.after_ref = bf16[4,7296]{1,0:T(4,128)(2,1)S(1)} fusion(bf16[4,8]{1,0:T(4,128)(2,1)} %param.8, bf16[4,4]{1,0:T(4,128)(2,1)S(1)} %convert.8, bf16[4,7168]{1,0:T(4,128)(2,1)} %param.6), kind=kLoop, calls=%fused_computation.4 | loop fusion | flops 175104 | bytes 115808 | tf_op jit(solution)/shard_map/add | solution.py:32
  1.6 5.0 %collective-permute-start.2 = (bf16[4,7296]{1,0:T(4,128)(2,1)S(1)}, bf16[4,7296]{1,0:T(4,128)(2,1)S(1)}, u32[]{:S(2)}, u32[]{:S(2)}) collective-permute-start(bf16[4,7296]{1,0:T(4,128)(2,1)S(1)} %pad_add_fusion.after_ref), channel_id=1, source_target_pairs={{0,12},{2,14},{4,0},{6,2},{8,4},{10,6},{12,8},{14,10},{1,13},{3,15... | collective-permute-start | bytes 175112 | tf_op jit(solution)/shard_map/ppermute | solution.py:17
  6.7 1.0 %collective-permute-start = (bf16[4,7296]{1,0:T(4,128)(2,1)S(1)}, bf16[4,7296]{1,0:T(4,128)(2,1)S(1)}, u32[]{:S(2)}, u32[]{:S(2)}) collective-permute-start(bf16[4,7296]{1,0:T(4,128)(2,1)S(1)} %pad_add_fusion.after_ref), channel_id=1, source_target_pairs={{0,4},{2,6},{4,8},{6,10},{8,12},{10,14},{12,0},{14,2},{1,5},{3,7},... | collective-permute-start | bytes 175112 | tf_op jit(solution)/shard_map/ppermute | solution.py:17
  7.7 5.2 %shard_map.64.refs_4_ = bf16[2,7168,512]{2,1,0:T(8,128)(2,1)S(1)} custom-call(bf16[2,7168,512]{2,1,0:T(8,128)(2,1)} %source_ref.2, bf16[4,7296]{1,0:T(4,128)(2,1)S(1)} %pad_add_fusion.after_ref), custom_call_target="tpu_custom_call" | custom-call | bytes 14680064 | tf_op jit(solution)/shard_map/pallas_call | solution.py:45
  12.9 0.1 pad_maximum_fusion.after_ref.refs_0_
  13.1 1.6 %collective-permute-start.3 = (bf16[16,7296]{1,0:T(8,128)(2,1)S(1)}, bf16[16,7296]{1,0:T(8,128)(2,1)S(1)}, u32[]{:S(2)}, u32[]{:S(2)}) collective-permute-start(bf16[16,7296]{1,0:T(8,128)(2,1)S(1)} %pad_maximum_fusion.after_ref.refs_0_), channel_id=1, source_target_pairs={{0,1},{1,0},{2,3},{3,2},{4,5},{5,4},{6,7},{7,6},{8,9},{9,8},{10,11... | collective-permute-start | bytes 700424 | tf_op jit(solution)/shard_map/ppermute | solution.py:17
  14.6 5.2 %shard_map.65.refs_5_ = bf16[2,7168,512]{2,1,0:T(8,128)(2,1)S(1)} custom-call(bf16[2,7168,512]{2,1,0:T(8,128)(2,1)} %source_ref.3, bf16[16,7296]{1,0:T(8,128)(2,1)S(1)} %pad_maximum_fusion.after_ref.refs_0_), custom_call_target="tpu_custom_call" | custom-call | bytes 14680064 | tf_op jit(solution)/shard_map/pallas_call | solution.py:45
  19.8 0.6 %collective-permute-start.5 = (bf16[16,7296]{1,0:T(8,128)(2,1)S(1)}, bf16[16,7296]{1,0:T(8,128)(2,1)S(1)}, u32[]{:S(2)}, u32[]{:S(2)}) collective-permute-start(bf16[16,7296]{1,0:T(8,128)(2,1)S(1)} %collective-permute-done.3.refs_1_), channel_id=1, source_target_pairs={{0,2},{2,0},{4,6},{6,4},{8,10},{10,8},{12,14},{14,12},{1,3},{3,1},... | collective-permute-start | bytes 700424 | tf_op jit(solution)/shard_map/ppermute | solution.py:21
  20.4 1.1 %collective-permute-done.5.refs_3_ = bf16[16,7296]{1,0:T(8,128)(2,1)S(1)} collective-permute-done((bf16[16,7296]{1,0:T(8,128)(2,1)S(1)}, bf16[16,7296]{1,0:T(8,128)(2,1)S(1)}, u32[]{:S(2)}, u32[]{:S(2)}) %collective-permute-start.5) | collective-permute-done | bytes 233504 | tf_op jit(solution)/shard_map/ppermute | solution.py:21
  21.5 7.9 %shard_map.66 = (f32[16,7168]{1,0:T(8,128)S(1)}, f32[16,7168]{1,0:T(8,128)S(1)}, bf16[16,7168]{1,0:T(8,128)(2,1)S(1)}, bf16[16,7168]{1,0:T(8,128)(2,1)S(1)}) custom-call(bf16[16,7296]{1,0:T(8,128)(2,1)S(1)} %pad_maximum_fusion.after_ref.refs_0_, bf16[16,7296]{1,0:T(8,128)(2,1)S(1)} %collective-permute-done.3.refs_1_, ...), custom_call_target="tpu_custom_call" | custom-call | tf_op jit(solution)/shard_map/pallas_call | solution.py:153
  29.5 0.4 collective-permute-start.7
  29.9 0.1 collective-permute-start.6
  30.0 1.0 %collective-permute-done.7 = bf16[16,7168]{1,0:T(8,128)(2,1)S(1)} collective-permute-done((bf16[16,7168]{1,0:T(8,128)(2,1)S(1)}, bf16[16,7168]{1,0:T(8,128)(2,1)S(1)}, u32[]{:S(2)}, u32[]{:S(2)}) %collective-permute-start.7) | collective-permute-done | bytes 229408 | tf_op jit(solution)/shard_map/ppermute | solution.py:21
  31.0 0.1 add_convert_fusion
  31.1 1.3 %collective-permute-start.8 = (bf16[8,7168]{1,0:T(8,128)(2,1)S(1)}, bf16[8,7168]{1,0:T(8,128)(2,1)S(1)}, u32[]{:S(2)}, u32[]{:S(2)}) collective-permute-start(bf16[8,7168]{1,0:T(8,128)(2,1)S(1)} %get-tuple-element.38), channel_id=1, source_target_pairs={{0,1},{1,0},{2,3},{3,2},{4,5},{5,4},{6,7},{7,6},{8,9},{9,8},{10,11... | collective-permute-start | bytes 344072 | tf_op jit(solution)/shard_map/ppermute | solution.py:17
  32.4 4.2 %collective-permute-done.8.refs_1_ = bf16[8,7168]{1,0:T(8,128)(2,1)S(1)} collective-permute-done((bf16[8,7168]{1,0:T(8,128)(2,1)S(1)}, bf16[8,7168]{1,0:T(8,128)(2,1)S(1)}, u32[]{:S(2)}, u32[]{:S(2)}) %collective-permute-start.8) | collective-permute-done | bytes 114720 | tf_op jit(solution)/shard_map/ppermute | solution.py:17
  36.6 1.0 %collective-permute-start.9 = (bf16[8,7168]{1,0:T(8,128)(2,1)S(1)}, bf16[8,7168]{1,0:T(8,128)(2,1)S(1)}, u32[]{:S(2)}, u32[]{:S(2)}) collective-permute-start(bf16[8,7168]{1,0:T(8,128)(2,1)S(1)} %get-tuple-element.30), channel_id=1, source_target_pairs={{0,1},{1,0},{2,3},{3,2},{4,5},{5,4},{6,7},{7,6},{8,9},{9,8},{10,11... | collective-permute-start | bytes 344072 | tf_op jit(solution)/shard_map/ppermute | solution.py:17
  37.6 2.3 %collective-permute-start.11 = (bf16[4,7168]{1,0:T(4,128)(2,1)S(1)}, bf16[4,7168]{1,0:T(4,128)(2,1)S(1)}, u32[]{:S(2)}, u32[]{:S(2)}) collective-permute-start(bf16[4,7168]{1,0:T(4,128)(2,1)S(1)} %get-tuple-element.33), channel_id=1, source_target_pairs={{0,8},{2,10},{4,12},{6,14},{8,0},{10,2},{12,4},{14,6},{1,9},{3,11}... | collective-permute-start | bytes 172040 | tf_op jit(solution)/shard_map/ppermute | solution.py:17
  39.9 1.5 %collective-permute-start.12 = (bf16[4,7168]{1,0:T(4,128)(2,1)S(1)}, bf16[4,7168]{1,0:T(4,128)(2,1)S(1)}, u32[]{:S(2)}, u32[]{:S(2)}) collective-permute-start(bf16[4,7168]{1,0:T(4,128)(2,1)S(1)} %get-tuple-element.34), channel_id=1, source_target_pairs={{0,4},{2,6},{4,8},{6,10},{8,12},{10,14},{12,0},{14,2},{1,5},{3,7},... | collective-permute-start | bytes 172040 | tf_op jit(solution)/shard_map/ppermute | solution.py:17
  41.4 2.9 %collective-permute-start.10 = (bf16[4,7168]{1,0:T(4,128)(2,1)S(1)}, bf16[4,7168]{1,0:T(4,128)(2,1)S(1)}, u32[]{:S(2)}, u32[]{:S(2)}) collective-permute-start(bf16[4,7168]{1,0:T(4,128)(2,1)S(1)} %get-tuple-element.32), channel_id=1, source_target_pairs={{0,12},{2,14},{4,0},{6,2},{8,4},{10,6},{12,8},{14,10},{1,13},{3,15... | collective-permute-start | bytes 172040 | tf_op jit(solution)/shard_map/ppermute | solution.py:17
  44.3 1.6 %collective-permute-done.12 = bf16[4,7168]{1,0:T(4,128)(2,1)S(1)} collective-permute-done((bf16[4,7168]{1,0:T(4,128)(2,1)S(1)}, bf16[4,7168]{1,0:T(4,128)(2,1)S(1)}, u32[]{:S(2)}, u32[]{:S(2)}) %collective-permute-start.12) | collective-permute-done | bytes 57376 | tf_op jit(solution)/shard_map/ppermute | solution.py:17
  45.9 0.6 %collective-permute-done.10 = bf16[4,7168]{1,0:T(4,128)(2,1)S(1)} collective-permute-done((bf16[4,7168]{1,0:T(4,128)(2,1)S(1)}, bf16[4,7168]{1,0:T(4,128)(2,1)S(1)}, u32[]{:S(2)}, u32[]{:S(2)}) %collective-permute-start.10) | collective-permute-done | bytes 57376 | tf_op jit(solution)/shard_map/ppermute | solution.py:17
  46.5 0.7 %add_convert_fusion.1 = bf16[4,7168]{1,0:T(4,128)(2,1)} fusion(bf16[4,7168]{1,0:T(4,128)(2,1)S(1)} %collective-permute-done.12, bf16[4,7168]{1,0:T(4,128)(2,1)S(1)} %collective-permute-done.11, f32[4,7168]{1,0:T(4,128)S(1)} %get-tuple-element.31, bf16[4,7168]{1,0:T(4,128)(2,1)S(1)} %collective-permute-done.10), kind=kLoop, calls=%fused_computation.3 | loop fusion | flops 200704 | bytes 344064 | tf_op jit(solution)/shard_map/convert_element_type | solution.py:183
  (15 shorter events, 0.2 us)
Async XLA Ops:
  1.6 11.3 %collective-permute-start.2 = (bf16[4,7296]{1,0:T(4,128)(2,1)S(1)}, bf16[4,7296]{1,0:T(4,128)(2,1)S(1)}, u32[]{:S(2)}, u32[]{:S(2)}) collective-permute-start(bf16[4,7296]{1,0:T(4,128)(2,1)S(1)} %pad_add_fusion.after_ref), channel_id=1, source_target_pairs={{0,12},{2,14},{4,0},{6,2},{8,4},{10,6},{12,8},{14,10},{1,13},{3,15... | collective-permute-start | bytes 175112 | tf_op jit(solution)/shard_map/ppermute | solution.py:17
  6.7 6.2 %collective-permute-start.1 = (bf16[4,7296]{1,0:T(4,128)(2,1)S(1)}, bf16[4,7296]{1,0:T(4,128)(2,1)S(1)}, u32[]{:S(2)}, u32[]{:S(2)}) collective-permute-start(bf16[4,7296]{1,0:T(4,128)(2,1)S(1)} %pad_add_fusion.after_ref), channel_id=1, source_target_pairs={{0,8},{2,10},{4,12},{6,14},{8,0},{10,2},{12,4},{14,6},{1,9},{3,11}... | collective-permute-start | bytes 175112 | tf_op jit(solution)/shard_map/ppermute | solution.py:17
  6.7 6.2 %collective-permute-start = (bf16[4,7296]{1,0:T(4,128)(2,1)S(1)}, bf16[4,7296]{1,0:T(4,128)(2,1)S(1)}, u32[]{:S(2)}, u32[]{:S(2)}) collective-permute-start(bf16[4,7296]{1,0:T(4,128)(2,1)S(1)} %pad_add_fusion.after_ref), channel_id=1, source_target_pairs={{0,4},{2,6},{4,8},{6,10},{8,12},{10,14},{12,0},{14,2},{1,5},{3,7},... | collective-permute-start | bytes 175112 | tf_op jit(solution)/shard_map/ppermute | solution.py:17
  13.1 6.8 %collective-permute-start.3 = (bf16[16,7296]{1,0:T(8,128)(2,1)S(1)}, bf16[16,7296]{1,0:T(8,128)(2,1)S(1)}, u32[]{:S(2)}, u32[]{:S(2)}) collective-permute-start(bf16[16,7296]{1,0:T(8,128)(2,1)S(1)} %pad_maximum_fusion.after_ref.refs_0_), channel_id=1, source_target_pairs={{0,1},{1,0},{2,3},{3,2},{4,5},{5,4},{6,7},{7,6},{8,9},{9,8},{10,11... | collective-permute-start | bytes 700424 | tf_op jit(solution)/shard_map/ppermute | solution.py:17
  14.6 5.8 %collective-permute-start.4 = (bf16[16,7296]{1,0:T(8,128)(2,1)S(1)}, bf16[16,7296]{1,0:T(8,128)(2,1)S(1)}, u32[]{:S(2)}, u32[]{:S(2)}) collective-permute-start(bf16[16,7296]{1,0:T(8,128)(2,1)S(1)} %pad_maximum_fusion.after_ref.refs_0_), channel_id=1, source_target_pairs={{0,2},{2,0},{4,6},{6,4},{8,10},{10,8},{12,14},{14,12},{1,3},{3,1},... | collective-permute-start | bytes 700424 | tf_op jit(solution)/shard_map/ppermute | solution.py:21
  19.8 1.7 %collective-permute-start.5 = (bf16[16,7296]{1,0:T(8,128)(2,1)S(1)}, bf16[16,7296]{1,0:T(8,128)(2,1)S(1)}, u32[]{:S(2)}, u32[]{:S(2)}) collective-permute-start(bf16[16,7296]{1,0:T(8,128)(2,1)S(1)} %collective-permute-done.3.refs_1_), channel_id=1, source_target_pairs={{0,2},{2,0},{4,6},{6,4},{8,10},{10,8},{12,14},{14,12},{1,3},{3,1},... | collective-permute-start | bytes 700424 | tf_op jit(solution)/shard_map/ppermute | solution.py:21
  29.5 1.6 %collective-permute-start.7 = (bf16[16,7168]{1,0:T(8,128)(2,1)S(1)}, bf16[16,7168]{1,0:T(8,128)(2,1)S(1)}, u32[]{:S(2)}, u32[]{:S(2)}) collective-permute-start(bf16[16,7168]{1,0:T(8,128)(2,1)S(1)} %get-tuple-element.29), channel_id=1, source_target_pairs={{0,2},{2,0},{4,6},{6,4},{8,10},{10,8},{12,14},{14,12},{1,3},{3,1},... | collective-permute-start | bytes 688136 | tf_op jit(solution)/shard_map/ppermute | solution.py:21
  29.9 2.5 %collective-permute-start.6 = (bf16[16,7168]{1,0:T(8,128)(2,1)S(1)}, bf16[16,7168]{1,0:T(8,128)(2,1)S(1)}, u32[]{:S(2)}, u32[]{:S(2)}) collective-permute-start(bf16[16,7168]{1,0:T(8,128)(2,1)S(1)} %get-tuple-element.27), channel_id=1, source_target_pairs={{0,2},{2,0},{4,6},{6,4},{8,10},{10,8},{12,14},{14,12},{1,3},{3,1},... | collective-permute-start | bytes 688136 | tf_op jit(solution)/shard_map/ppermute | solution.py:21
  31.1 5.5 %collective-permute-start.8 = (bf16[8,7168]{1,0:T(8,128)(2,1)S(1)}, bf16[8,7168]{1,0:T(8,128)(2,1)S(1)}, u32[]{:S(2)}, u32[]{:S(2)}) collective-permute-start(bf16[8,7168]{1,0:T(8,128)(2,1)S(1)} %get-tuple-element.38), channel_id=1, source_target_pairs={{0,1},{1,0},{2,3},{3,2},{4,5},{5,4},{6,7},{7,6},{8,9},{9,8},{10,11... | collective-permute-start | bytes 344072 | tf_op jit(solution)/shard_map/ppermute | solution.py:17
  36.6 4.8 %collective-permute-start.9 = (bf16[8,7168]{1,0:T(8,128)(2,1)S(1)}, bf16[8,7168]{1,0:T(8,128)(2,1)S(1)}, u32[]{:S(2)}, u32[]{:S(2)}) collective-permute-start(bf16[8,7168]{1,0:T(8,128)(2,1)S(1)} %get-tuple-element.30), channel_id=1, source_target_pairs={{0,1},{1,0},{2,3},{3,2},{4,5},{5,4},{6,7},{7,6},{8,9},{9,8},{10,11... | collective-permute-start | bytes 344072 | tf_op jit(solution)/shard_map/ppermute | solution.py:17
  37.6 6.7 %collective-permute-start.11 = (bf16[4,7168]{1,0:T(4,128)(2,1)S(1)}, bf16[4,7168]{1,0:T(4,128)(2,1)S(1)}, u32[]{:S(2)}, u32[]{:S(2)}) collective-permute-start(bf16[4,7168]{1,0:T(4,128)(2,1)S(1)} %get-tuple-element.33), channel_id=1, source_target_pairs={{0,8},{2,10},{4,12},{6,14},{8,0},{10,2},{12,4},{14,6},{1,9},{3,11}... | collective-permute-start | bytes 172040 | tf_op jit(solution)/shard_map/ppermute | solution.py:17
  39.9 6.0 %collective-permute-start.12 = (bf16[4,7168]{1,0:T(4,128)(2,1)S(1)}, bf16[4,7168]{1,0:T(4,128)(2,1)S(1)}, u32[]{:S(2)}, u32[]{:S(2)}) collective-permute-start(bf16[4,7168]{1,0:T(4,128)(2,1)S(1)} %get-tuple-element.34), channel_id=1, source_target_pairs={{0,4},{2,6},{4,8},{6,10},{8,12},{10,14},{12,0},{14,2},{1,5},{3,7},... | collective-permute-start | bytes 172040 | tf_op jit(solution)/shard_map/ppermute | solution.py:17
  41.4 5.1 %collective-permute-start.10 = (bf16[4,7168]{1,0:T(4,128)(2,1)S(1)}, bf16[4,7168]{1,0:T(4,128)(2,1)S(1)}, u32[]{:S(2)}, u32[]{:S(2)}) collective-permute-start(bf16[4,7168]{1,0:T(4,128)(2,1)S(1)} %get-tuple-element.32), channel_id=1, source_target_pairs={{0,12},{2,14},{4,0},{6,2},{8,4},{10,6},{12,8},{14,10},{1,13},{3,15... | collective-permute-start | bytes 172040 | tf_op jit(solution)/shard_map/ppermute | solution.py:17

commit v4 on v3

--- a/solution.py
+++ b/solution.py
@@ -17,6 +17,14 @@
     return lax.ppermute(value, axis, [(i, (i + shift * stride) % size) for i in range(size)])
 
 
+def chip_shift(value, k, back):
+    size = lax.axis_size("group")
+    chips = size // 2
+    if chips & (chips - 1):
+        return rotate(value, "group", -k if back else k, 2)
+    return lax.ppermute(value, "group", [(i, i ^ (2 * k)) for i in range(size)])
+
+
 def other_core(value):
     return lax.ppermute(value, "group", [(i, i ^ 1) for i in range(lax.axis_size("group"))])
 
@@ -24,12 +32,16 @@
 def pack(tokens, routes, gate_weights):
     zero = jnp.zeros((), jnp.bfloat16)
     width = tokens.shape[1]
+    column = lax.broadcasted_iota(jnp.int32, (tokens.shape[0], width + LANES), 1)
+    inside = jnp.where(column < width, 0, 1)
     packed = lax.pad(tokens, zero, ((0, 0, 0), (0, LANES, 0)))
     first = width
     for side in (routes, gate_weights):
         last = first + side.shape[1]
         side = lax.pad(side, jnp.zeros((), side.dtype), ((0, 0, 0), (first, width + LANES - last, 0)))
-        packed = packed + side.astype(jnp.bfloat16)
+        if side.dtype == jnp.int32:
+            side = (side * inside).astype(jnp.bfloat16)
+        packed = packed + side
         first = last
     return packed
 
@@ -140,7 +152,7 @@
     rows_here, width = tokens.shape
     pairs, _, hidden_here = w_gate.shape
     mine = pack(tokens, routes, gate_weights)
-    others = [rotate(mine, "group", k, 2) for k in range(1, chips)]
+    others = [chip_shift(mine, k, False) for k in range(1, chips)]
     gate_here, others = lax.optimization_barrier((fetch(w_gate, mine, 34), others))
     line = jnp.concatenate([mine] + others, axis=0)
     crossed = [rotate(line, "local", k, 1) for k in range(1, locals_)]
@@ -179,7 +191,7 @@
         home[low:high] = join([totals[0][part]] + backs, high - low, low)
     result = home[0]
     for c in range(1, chips):
-        result = result + rotate(home[c], "group", -c, 2).astype(jnp.float32)
+        result = result + chip_shift(home[c], c, True).astype(jnp.float32)
     return result.astype(jnp.bfloat16)
 
 

time: 47.4 us -> 46.5 us (0.981)
  starting transfers between devices: 17.6 us -> 16 us
  waiting for transfers between devices: 8.53 us -> 9.9 us
  other arithmetic: 2.54 us -> 1.88 us
    ppermute x9 -> x3, starting transfers between devices: 16.5 us -> 4.23 us  [rotate(): lax.ppermute(value, axis, [(i, (i + shift * stride) % size) for i in rang...]
    ppermute x0 -> x6, starting transfers between devices: none -> 10.6 us  [chip_shift(): return lax.ppermute(value, 'group', [(i, i ^ 2 * k) for i in range(size)])]
    ppermute x0 -> x6, waiting for transfers between devices: none -> 3.74 us  [chip_shift(): return lax.ppermute(value, 'group', [(i, i ^ 2 * k) for i in range(size)])]
    ppermute x9 -> x3, waiting for transfers between devices: 6.43 us -> 4.05 us  [rotate(): lax.ppermute(value, axis, [(i, (i + shift * stride) % size) for i in rang...]
    another operation x2 -> x1, other arithmetic: 0.74 us -> 0.05 us
  transfers between devices with their start and end apart: 13 -> 13, of which waited for: 5 -> 6; matrix products, arithmetic and copies ran while one was open for 0% -> 0% of each run, Pallas kernels for 22% -> 23%
where the time goes in v4:
time: 46.5 us; the launch traced here: 46.3 us
  Pallas kernels  18.3 us (39%)
  starting transfers between devices  16 us (34%)
  waiting for transfers between devices  9.9 us (21%)
  other arithmetic  1.88 us (4%)
    ppermute x6, starting transfers between devices, chip_shift(): return lax.ppermute(value, 'group', [(i, i ^ 2 * k) for i in range(size)])  10.6 us
    pallas_call x2, Pallas kernels, fetch(): pl.pallas_call(fetch_kernel, out_shape=jax.ShapeDtypeStruct(weights.shape...  10.4 us
    pallas_call x1, Pallas kernels, on_device(): pl.pallas_call(functools.partial(experts_kernel, len(pieces)), out_shape=...  7.91 us
    ppermute x3, starting transfers between devices, rotate(): lax.ppermute(value, axis, [(i, (i + shift * stride) % size) for i in rang...  4.23 us
    ppermute x3, waiting for transfers between devices, rotate(): lax.ppermute(value, axis, [(i, (i + shift * stride) % size) for i in rang...  4.05 us
    ppermute x6, waiting for transfers between devices, chip_shift(): return lax.ppermute(value, 'group', [(i, i ^ 2 * k) for i in range(size)])  3.74 us
    ppermute x4, waiting for transfers between devices, other_core(): lax.ppermute(value, 'group', [(i, i ^ 1) for i in range(lax.axis_size('gr...  2.1 us
    ppermute x4, starting transfers between devices, other_core(): lax.ppermute(value, 'group', [(i, i ^ 1) for i in range(lax.axis_size('gr...  1.14 us
  transfers between devices with their start and end apart: 13, of which 6 were waited for; matrix products, arithmetic and copies ran while one was open for 0% of the time, Pallas kernels for 23%

profile of v4, /device:TPU:0, one launch (start us, length us, event | category | flops | bytes accessed | tf_op | source)
XLA Modules:
  0.0 46.3 jit_solution(7626742162461617530)
XLA Ops:
  0.0 0.9 %fusion.1.after_ref = bf16[4,7296]{1,0:T(4,128)(2,1)S(1)} fusion(s32[4,4]{1,0:T(4,128)} %param.7, bf16[4,8]{1,0:T(4,128)(2,1)} %param.8, s32[7296]{0:T(1024)S(1)} %fusion.2, bf16[4,7168]{1,0:T(4,128)(2,1)} %param.6), kind=kLoop, calls=%fused_computation.6 | loop fusion | flops 233472 | bytes 145024 | tf_op jit(solution)/shard_map/add | solution.py:44
  1.0 5.1 %collective-permute-start.2 = (bf16[4,7296]{1,0:T(4,128)(2,1)S(1)}, bf16[4,7296]{1,0:T(4,128)(2,1)S(1)}, u32[]{:S(2)}, u32[]{:S(2)}) collective-permute-start(bf16[4,7296]{1,0:T(4,128)(2,1)S(1)} %fusion.1.after_ref), channel_id=1, source_target_pairs={{0,12},{2,14},{4,8},{6,10},{8,4},{10,6},{12,0},{14,2},{1,13},{3,15... | collective-permute-start | bytes 175112 | tf_op jit(solution)/shard_map/ppermute | solution.py:25
  6.0 0.6 %collective-permute-start = (bf16[4,7296]{1,0:T(4,128)(2,1)S(1)}, bf16[4,7296]{1,0:T(4,128)(2,1)S(1)}, u32[]{:S(2)}, u32[]{:S(2)}) collective-permute-start(bf16[4,7296]{1,0:T(4,128)(2,1)S(1)} %fusion.1.after_ref), channel_id=1, source_target_pairs={{0,4},{2,6},{4,0},{6,2},{8,12},{10,14},{12,8},{14,10},{1,5},{3,7},... | collective-permute-start | bytes 175112 | tf_op jit(solution)/shard_map/ppermute | solution.py:25
  6.6 5.2 %shard_map.64.refs_4_ = bf16[2,7168,512]{2,1,0:T(8,128)(2,1)S(1)} custom-call(bf16[2,7168,512]{2,1,0:T(8,128)(2,1)} %source_ref.2, bf16[4,7296]{1,0:T(4,128)(2,1)S(1)} %fusion.1.after_ref), custom_call_target="tpu_custom_call" | custom-call | bytes 14680064 | tf_op jit(solution)/shard_map/pallas_call | solution.py:57
  11.9 0.1 pad_maximum_fusion.after_ref.refs_0_
  12.0 1.7 %collective-permute-start.3 = (bf16[16,7296]{1,0:T(8,128)(2,1)S(1)}, bf16[16,7296]{1,0:T(8,128)(2,1)S(1)}, u32[]{:S(2)}, u32[]{:S(2)}) collective-permute-start(bf16[16,7296]{1,0:T(8,128)(2,1)S(1)} %pad_maximum_fusion.after_ref.refs_0_), channel_id=1, source_target_pairs={{0,1},{1,0},{2,3},{3,2},{4,5},{5,4},{6,7},{7,6},{8,9},{9,8},{10,11... | collective-permute-start | bytes 700424 | tf_op jit(solution)/shard_map/ppermute | solution.py:17
  13.7 5.2 %shard_map.65.refs_5_ = bf16[2,7168,512]{2,1,0:T(8,128)(2,1)S(1)} custom-call(bf16[2,7168,512]{2,1,0:T(8,128)(2,1)} %source_ref.3, bf16[16,7296]{1,0:T(8,128)(2,1)S(1)} %pad_maximum_fusion.after_ref.refs_0_), custom_call_target="tpu_custom_call" | custom-call | bytes 14680064 | tf_op jit(solution)/shard_map/pallas_call | solution.py:57
  19.0 0.6 %collective-permute-start.5 = (bf16[16,7296]{1,0:T(8,128)(2,1)S(1)}, bf16[16,7296]{1,0:T(8,128)(2,1)S(1)}, u32[]{:S(2)}, u32[]{:S(2)}) collective-permute-start(bf16[16,7296]{1,0:T(8,128)(2,1)S(1)} %collective-permute-done.3.refs_1_), channel_id=1, source_target_pairs={{0,2},{2,0},{4,6},{6,4},{8,10},{10,8},{12,14},{14,12},{1,3},{3,1},... | collective-permute-start | bytes 700424 | tf_op jit(solution)/shard_map/ppermute | solution.py:29
  19.5 1.1 %collective-permute-done.5.refs_3_ = bf16[16,7296]{1,0:T(8,128)(2,1)S(1)} collective-permute-done((bf16[16,7296]{1,0:T(8,128)(2,1)S(1)}, bf16[16,7296]{1,0:T(8,128)(2,1)S(1)}, u32[]{:S(2)}, u32[]{:S(2)}) %collective-permute-start.5) | collective-permute-done | bytes 233504 | tf_op jit(solution)/shard_map/ppermute | solution.py:29
  20.6 7.9 %shard_map.66 = (f32[16,7168]{1,0:T(8,128)S(1)}, f32[16,7168]{1,0:T(8,128)S(1)}, bf16[16,7168]{1,0:T(8,128)(2,1)S(1)}, bf16[16,7168]{1,0:T(8,128)(2,1)S(1)}) custom-call(bf16[16,7296]{1,0:T(8,128)(2,1)S(1)} %pad_maximum_fusion.after_ref.refs_0_, bf16[16,7296]{1,0:T(8,128)(2,1)S(1)} %collective-permute-done.3.refs_1_, ...), custom_call_target="tpu_custom_call" | custom-call | tf_op jit(solution)/shard_map/pallas_call | solution.py:165
  28.6 0.4 collective-permute-start.7
  29.0 0.1 collective-permute-start.6
  29.1 1.0 %collective-permute-done.7 = bf16[16,7168]{1,0:T(8,128)(2,1)S(1)} collective-permute-done((bf16[16,7168]{1,0:T(8,128)(2,1)S(1)}, bf16[16,7168]{1,0:T(8,128)(2,1)S(1)}, u32[]{:S(2)}, u32[]{:S(2)}) %collective-permute-start.7) | collective-permute-done | bytes 229408 | tf_op jit(solution)/shard_map/ppermute | solution.py:29
  30.1 0.1 add_convert_fusion
  30.2 1.4 %collective-permute-start.8 = (bf16[8,7168]{1,0:T(8,128)(2,1)S(1)}, bf16[8,7168]{1,0:T(8,128)(2,1)S(1)}, u32[]{:S(2)}, u32[]{:S(2)}) collective-permute-start(bf16[8,7168]{1,0:T(8,128)(2,1)S(1)} %get-tuple-element.38), channel_id=1, source_target_pairs={{0,1},{1,0},{2,3},{3,2},{4,5},{5,4},{6,7},{7,6},{8,9},{9,8},{10,11... | collective-permute-start | bytes 344072 | tf_op jit(solution)/shard_map/ppermute | solution.py:17
  31.7 4.0 %collective-permute-done.8.refs_1_ = bf16[8,7168]{1,0:T(8,128)(2,1)S(1)} collective-permute-done((bf16[8,7168]{1,0:T(8,128)(2,1)S(1)}, bf16[8,7168]{1,0:T(8,128)(2,1)S(1)}, u32[]{:S(2)}, u32[]{:S(2)}) %collective-permute-start.8) | collective-permute-done | bytes 114720 | tf_op jit(solution)/shard_map/ppermute | solution.py:17
  35.7 1.1 %collective-permute-start.9 = (bf16[8,7168]{1,0:T(8,128)(2,1)S(1)}, bf16[8,7168]{1,0:T(8,128)(2,1)S(1)}, u32[]{:S(2)}, u32[]{:S(2)}) collective-permute-start(bf16[8,7168]{1,0:T(8,128)(2,1)S(1)} %get-tuple-element.30), channel_id=1, source_target_pairs={{0,1},{1,0},{2,3},{3,2},{4,5},{5,4},{6,7},{7,6},{8,9},{9,8},{10,11... | collective-permute-start | bytes 344072 | tf_op jit(solution)/shard_map/ppermute | solution.py:17
  36.9 2.4 %collective-permute-start.11 = (bf16[4,7168]{1,0:T(4,128)(2,1)S(1)}, bf16[4,7168]{1,0:T(4,128)(2,1)S(1)}, u32[]{:S(2)}, u32[]{:S(2)}) collective-permute-start(bf16[4,7168]{1,0:T(4,128)(2,1)S(1)} %get-tuple-element.33), channel_id=1, source_target_pairs={{0,8},{2,10},{4,12},{6,14},{8,0},{10,2},{12,4},{14,6},{1,9},{3,11}... | collective-permute-start | bytes 172040 | tf_op jit(solution)/shard_map/ppermute | solution.py:25
  39.2 1.5 %collective-permute-start.12 = (bf16[4,7168]{1,0:T(4,128)(2,1)S(1)}, bf16[4,7168]{1,0:T(4,128)(2,1)S(1)}, u32[]{:S(2)}, u32[]{:S(2)}) collective-permute-start(bf16[4,7168]{1,0:T(4,128)(2,1)S(1)} %get-tuple-element.34), channel_id=1, source_target_pairs={{0,12},{2,14},{4,8},{6,10},{8,4},{10,6},{12,0},{14,2},{1,13},{3,15... | collective-permute-start | bytes 172040 | tf_op jit(solution)/shard_map/ppermute | solution.py:25
  40.7 1.1 %collective-permute-start.10 = (bf16[4,7168]{1,0:T(4,128)(2,1)S(1)}, bf16[4,7168]{1,0:T(4,128)(2,1)S(1)}, u32[]{:S(2)}, u32[]{:S(2)}) collective-permute-start(bf16[4,7168]{1,0:T(4,128)(2,1)S(1)} %get-tuple-element.32), channel_id=1, source_target_pairs={{0,4},{2,6},{4,0},{6,2},{8,12},{10,14},{12,8},{14,10},{1,5},{3,7},... | collective-permute-start | bytes 172040 | tf_op jit(solution)/shard_map/ppermute | solution.py:25
  41.8 1.8 %collective-permute-done.11 = bf16[4,7168]{1,0:T(4,128)(2,1)S(1)} collective-permute-done((bf16[4,7168]{1,0:T(4,128)(2,1)S(1)}, bf16[4,7168]{1,0:T(4,128)(2,1)S(1)}, u32[]{:S(2)}, u32[]{:S(2)}) %collective-permute-start.11) | collective-permute-done | bytes 57376 | tf_op jit(solution)/shard_map/ppermute | solution.py:25
  43.6 1.7 %collective-permute-done.12 = bf16[4,7168]{1,0:T(4,128)(2,1)S(1)} collective-permute-done((bf16[4,7168]{1,0:T(4,128)(2,1)S(1)}, bf16[4,7168]{1,0:T(4,128)(2,1)S(1)}, u32[]{:S(2)}, u32[]{:S(2)}) %collective-permute-start.12) | collective-permute-done | bytes 57376 | tf_op jit(solution)/shard_map/ppermute | solution.py:25
  45.3 0.3 collective-permute-done.10
  45.6 0.7 %add_convert_fusion.1 = bf16[4,7168]{1,0:T(4,128)(2,1)} fusion(bf16[4,7168]{1,0:T(4,128)(2,1)S(1)} %collective-permute-done.12, bf16[4,7168]{1,0:T(4,128)(2,1)S(1)} %collective-permute-done.11, f32[4,7168]{1,0:T(4,128)S(1)} %get-tuple-element.31, bf16[4,7168]{1,0:T(4,128)(2,1)S(1)} %collective-permute-done.10), kind=kLoop, calls=%fused_computation.4 | loop fusion | flops 200704 | bytes 344064 | tf_op jit(solution)/shard_map/convert_element_type | solution.py:195
  (15 shorter events, 0.2 us)
Async XLA Ops:
  1.0 10.9 %collective-permute-start.2 = (bf16[4,7296]{1,0:T(4,128)(2,1)S(1)}, bf16[4,7296]{1,0:T(4,128)(2,1)S(1)}, u32[]{:S(2)}, u32[]{:S(2)}) collective-permute-start(bf16[4,7296]{1,0:T(4,128)(2,1)S(1)} %fusion.1.after_ref), channel_id=1, source_target_pairs={{0,12},{2,14},{4,8},{6,10},{8,4},{10,6},{12,0},{14,2},{1,13},{3,15... | collective-permute-start | bytes 175112 | tf_op jit(solution)/shard_map/ppermute | solution.py:25
  6.0 5.8 %collective-permute-start.1 = (bf16[4,7296]{1,0:T(4,128)(2,1)S(1)}, bf16[4,7296]{1,0:T(4,128)(2,1)S(1)}, u32[]{:S(2)}, u32[]{:S(2)}) collective-permute-start(bf16[4,7296]{1,0:T(4,128)(2,1)S(1)} %fusion.1.after_ref), channel_id=1, source_target_pairs={{0,8},{2,10},{4,12},{6,14},{8,0},{10,2},{12,4},{14,6},{1,9},{3,11}... | collective-permute-start | bytes 175112 | tf_op jit(solution)/shard_map/ppermute | solution.py:25
  6.0 5.9 %collective-permute-start = (bf16[4,7296]{1,0:T(4,128)(2,1)S(1)}, bf16[4,7296]{1,0:T(4,128)(2,1)S(1)}, u32[]{:S(2)}, u32[]{:S(2)}) collective-permute-start(bf16[4,7296]{1,0:T(4,128)(2,1)S(1)} %fusion.1.after_ref), channel_id=1, source_target_pairs={{0,4},{2,6},{4,0},{6,2},{8,12},{10,14},{12,8},{14,10},{1,5},{3,7},... | collective-permute-start | bytes 175112 | tf_op jit(solution)/shard_map/ppermute | solution.py:25
  12.0 6.9 %collective-permute-start.3 = (bf16[16,7296]{1,0:T(8,128)(2,1)S(1)}, bf16[16,7296]{1,0:T(8,128)(2,1)S(1)}, u32[]{:S(2)}, u32[]{:S(2)}) collective-permute-start(bf16[16,7296]{1,0:T(8,128)(2,1)S(1)} %pad_maximum_fusion.after_ref.refs_0_), channel_id=1, source_target_pairs={{0,1},{1,0},{2,3},{3,2},{4,5},{5,4},{6,7},{7,6},{8,9},{9,8},{10,11... | collective-permute-start | bytes 700424 | tf_op jit(solution)/shard_map/ppermute | solution.py:17
  13.7 5.8 %collective-permute-start.4 = (bf16[16,7296]{1,0:T(8,128)(2,1)S(1)}, bf16[16,7296]{1,0:T(8,128)(2,1)S(1)}, u32[]{:S(2)}, u32[]{:S(2)}) collective-permute-start(bf16[16,7296]{1,0:T(8,128)(2,1)S(1)} %pad_maximum_fusion.after_ref.refs_0_), channel_id=1, source_target_pairs={{0,2},{2,0},{4,6},{6,4},{8,10},{10,8},{12,14},{14,12},{1,3},{3,1},... | collective-permute-start | bytes 700424 | tf_op jit(solution)/shard_map/ppermute | solution.py:29
  19.0 1.7 %collective-permute-start.5 = (bf16[16,7296]{1,0:T(8,128)(2,1)S(1)}, bf16[16,7296]{1,0:T(8,128)(2,1)S(1)}, u32[]{:S(2)}, u32[]{:S(2)}) collective-permute-start(bf16[16,7296]{1,0:T(8,128)(2,1)S(1)} %collective-permute-done.3.refs_1_), channel_id=1, source_target_pairs={{0,2},{2,0},{4,6},{6,4},{8,10},{10,8},{12,14},{14,12},{1,3},{3,1},... | collective-permute-start | bytes 700424 | tf_op jit(solution)/shard_map/ppermute | solution.py:29
  28.6 1.6 %collective-permute-start.7 = (bf16[16,7168]{1,0:T(8,128)(2,1)S(1)}, bf16[16,7168]{1,0:T(8,128)(2,1)S(1)}, u32[]{:S(2)}, u32[]{:S(2)}) collective-permute-start(bf16[16,7168]{1,0:T(8,128)(2,1)S(1)} %get-tuple-element.29), channel_id=1, source_target_pairs={{0,2},{2,0},{4,6},{6,4},{8,10},{10,8},{12,14},{14,12},{1,3},{3,1},... | collective-permute-start | bytes 688136 | tf_op jit(solution)/shard_map/ppermute | solution.py:29
  29.0 2.6 %collective-permute-start.6 = (bf16[16,7168]{1,0:T(8,128)(2,1)S(1)}, bf16[16,7168]{1,0:T(8,128)(2,1)S(1)}, u32[]{:S(2)}, u32[]{:S(2)}) collective-permute-start(bf16[16,7168]{1,0:T(8,128)(2,1)S(1)} %get-tuple-element.27), channel_id=1, source_target_pairs={{0,2},{2,0},{4,6},{6,4},{8,10},{10,8},{12,14},{14,12},{1,3},{3,1},... | collective-permute-start | bytes 688136 | tf_op jit(solution)/shard_map/ppermute | solution.py:29
  30.2 5.5 %collective-permute-start.8 = (bf16[8,7168]{1,0:T(8,128)(2,1)S(1)}, bf16[8,7168]{1,0:T(8,128)(2,1)S(1)}, u32[]{:S(2)}, u32[]{:S(2)}) collective-permute-start(bf16[8,7168]{1,0:T(8,128)(2,1)S(1)} %get-tuple-element.38), channel_id=1, source_target_pairs={{0,1},{1,0},{2,3},{3,2},{4,5},{5,4},{6,7},{7,6},{8,9},{9,8},{10,11... | collective-permute-start | bytes 344072 | tf_op jit(solution)/shard_map/ppermute | solution.py:17
  35.7 5.0 %collective-permute-start.9 = (bf16[8,7168]{1,0:T(8,128)(2,1)S(1)}, bf16[8,7168]{1,0:T(8,128)(2,1)S(1)}, u32[]{:S(2)}, u32[]{:S(2)}) collective-permute-start(bf16[8,7168]{1,0:T(8,128)(2,1)S(1)} %get-tuple-element.30), channel_id=1, source_target_pairs={{0,1},{1,0},{2,3},{3,2},{4,5},{5,4},{6,7},{7,6},{8,9},{9,8},{10,11... | collective-permute-start | bytes 344072 | tf_op jit(solution)/shard_map/ppermute | solution.py:17
  36.9 6.7 %collective-permute-start.11 = (bf16[4,7168]{1,0:T(4,128)(2,1)S(1)}, bf16[4,7168]{1,0:T(4,128)(2,1)S(1)}, u32[]{:S(2)}, u32[]{:S(2)}) collective-permute-start(bf16[4,7168]{1,0:T(4,128)(2,1)S(1)} %get-tuple-element.33), channel_id=1, source_target_pairs={{0,8},{2,10},{4,12},{6,14},{8,0},{10,2},{12,4},{14,6},{1,9},{3,11}... | collective-permute-start | bytes 172040 | tf_op jit(solution)/shard_map/ppermute | solution.py:25
  39.2 6.1 %collective-permute-start.12 = (bf16[4,7168]{1,0:T(4,128)(2,1)S(1)}, bf16[4,7168]{1,0:T(4,128)(2,1)S(1)}, u32[]{:S(2)}, u32[]{:S(2)}) collective-permute-start(bf16[4,7168]{1,0:T(4,128)(2,1)S(1)} %get-tuple-element.34), channel_id=1, source_target_pairs={{0,12},{2,14},{4,8},{6,10},{8,4},{10,6},{12,0},{14,2},{1,13},{3,15... | collective-permute-start | bytes 172040 | tf_op jit(solution)/shard_map/ppermute | solution.py:25
  40.7 4.9 %collective-permute-start.10 = (bf16[4,7168]{1,0:T(4,128)(2,1)S(1)}, bf16[4,7168]{1,0:T(4,128)(2,1)S(1)}, u32[]{:S(2)}, u32[]{:S(2)}) collective-permute-start(bf16[4,7168]{1,0:T(4,128)(2,1)S(1)} %get-tuple-element.32), channel_id=1, source_target_pairs={{0,4},{2,6},{4,0},{6,2},{8,12},{10,14},{12,8},{14,10},{1,5},{3,7},... | collective-permute-start | bytes 172040 | tf_op jit(solution)/shard_map/ppermute | solution.py:25

commit v5 on v4

--- a/solution.py
+++ b/solution.py
@@ -157,7 +157,7 @@
     line = jnp.concatenate([mine] + others, axis=0)
     crossed = [rotate(line, "local", k, 1) for k in range(1, locals_)]
     across_line = other_core(line)
-    up_here, crossed = lax.optimization_barrier((fetch(w_up, line, 26), crossed))
+    up_here, crossed = lax.optimization_barrier((fetch(w_up, line, 28), crossed))
     pieces = [line] + crossed + [across_line] + [other_core(part) for part in crossed]
     block = chips * rows_here
     rows = 2 * locals_ * block
@@ -171,24 +171,25 @@
             pltpu.VMEM((pairs * hidden_here, width), jnp.bfloat16),
             pltpu.VMEM((padded, width), jnp.bfloat16),
             pltpu.VMEM((pairs, 2, padded, hidden_here), jnp.float32),
-            pltpu.SemaphoreType.DMA((7,)),
+            pltpu.SemaphoreType.DMA((2 if padded <= LEAST_ROWS else 7,)),
         ],
-        compiler_params=pltpu.CompilerParams(vmem_limit_bytes=18 << 20),
+        compiler_params=pltpu.CompilerParams(vmem_limit_bytes=19 << 20),
     )(*pieces, gate_here, up_here, w_down.reshape(pairs * hidden_here, width))
     totals = [None] * locals_
     for k in reversed(range(locals_)):
         totals[k] = outs[k] + other_core(outs[locals_ + k]).astype(jnp.float32)
     home = [None] * chips
-    backs = None
+    done = None
     for low, high in ((chips // 2, chips), (0, chips // 2)):
         if low == high:
             continue
         part = slice(low * rows_here, high * rows_here)
         sent = [totals[k][part].astype(jnp.bfloat16) for k in range(1, locals_)]
-        if backs is not None:
-            sent, backs = lax.optimization_barrier((sent, backs))
+        if done is not None:
+            sent, done = lax.optimization_barrier((sent, done))
         backs = [rotate(sent[k - 1], "local", -k, 1) for k in range(1, locals_)]
         home[low:high] = join([totals[0][part]] + backs, high - low, low)
+        done = home[high - 1]
     result = home[0]
     for c in range(1, chips):
         result = result + chip_shift(home[c], c, True).astype(jnp.float32)

time: 46.5 us -> 45.5 us (0.978)
  Pallas kernels: 18.3 us -> 17.5 us
    pallas_call x1, Pallas kernels: 7.91 us -> 7.03 us  [on_device(): pl.pallas_call(functools.partial(experts_kernel, len(pieces)), out_shape=...]
  transfers between devices with their start and end apart: 13 -> 13, of which waited for: 6 -> 5; matrix products, arithmetic and copies ran while one was open for 0% -> 0% of each run, Pallas kernels for 23% -> 23%
where the time goes in v5:
time: 45.5 us; the launch traced here: 45.3 us
  Pallas kernels  17.5 us (38%)
  starting transfers between devices  15.9 us (35%)
  waiting for transfers between devices  9.9 us (22%)
  other arithmetic  1.88 us (4%)
    ppermute x6, starting transfers between devices, chip_shift(): return lax.ppermute(value, 'group', [(i, i ^ 2 * k) for i in range(size)])  10.5 us
    pallas_call x2, Pallas kernels, fetch(): pl.pallas_call(fetch_kernel, out_shape=jax.ShapeDtypeStruct(weights.shape...  10.4 us
    pallas_call x1, Pallas kernels, on_device(): pl.pallas_call(functools.partial(experts_kernel, len(pieces)), out_shape=...  7.03 us
    ppermute x3, starting transfers between devices, rotate(): lax.ppermute(value, axis, [(i, (i + shift * stride) % size) for i in rang...  4.29 us
    ppermute x3, waiting for transfers between devices, rotate(): lax.ppermute(value, axis, [(i, (i + shift * stride) % size) for i in rang...  4.24 us
    ppermute x6, waiting for transfers between devices, chip_shift(): return lax.ppermute(value, 'group', [(i, i ^ 2 * k) for i in range(size)])  3.56 us
    ppermute x4, waiting for transfers between devices, other_core(): lax.ppermute(value, 'group', [(i, i ^ 1) for i in range(lax.axis_size('gr...  2.1 us
    ppermute x4, starting transfers between devices, other_core(): lax.ppermute(value, 'group', [(i, i ^ 1) for i in range(lax.axis_size('gr...  1.14 us
  transfers between devices with their start and end apart: 13, of which 5 were waited for; matrix products, arithmetic and copies ran while one was open for 0% of the time, Pallas kernels for 23%

profile of v5, /device:TPU:0, one launch (start us, length us, event | category | flops | bytes accessed | tf_op | source)
XLA Modules:
  0.0 45.3 jit_solution(5119855300794553979)
XLA Ops:
  0.0 0.9 %fusion.1.after_ref = bf16[4,7296]{1,0:T(4,128)(2,1)S(1)} fusion(s32[4,4]{1,0:T(4,128)} %param.7, bf16[4,8]{1,0:T(4,128)(2,1)} %param.8, s32[7296]{0:T(1024)S(1)} %fusion.2, bf16[4,7168]{1,0:T(4,128)(2,1)} %param.6), kind=kLoop, calls=%fused_computation.6 | loop fusion | flops 233472 | bytes 145024 | tf_op jit(solution)/shard_map/add | solution.py:44
  1.0 5.1 %collective-permute-start.2 = (bf16[4,7296]{1,0:T(4,128)(2,1)S(1)}, bf16[4,7296]{1,0:T(4,128)(2,1)S(1)}, u32[]{:S(2)}, u32[]{:S(2)}) collective-permute-start(bf16[4,7296]{1,0:T(4,128)(2,1)S(1)} %fusion.1.after_ref), channel_id=1, source_target_pairs={{0,12},{2,14},{4,8},{6,10},{8,4},{10,6},{12,0},{14,2},{1,13},{3,15... | collective-permute-start | bytes 175112 | tf_op jit(solution)/shard_map/ppermute | solution.py:25
  6.0 0.0 collective-permute-start.1
  6.0 0.6 %collective-permute-start = (bf16[4,7296]{1,0:T(4,128)(2,1)S(1)}, bf16[4,7296]{1,0:T(4,128)(2,1)S(1)}, u32[]{:S(2)}, u32[]{:S(2)}) collective-permute-start(bf16[4,7296]{1,0:T(4,128)(2,1)S(1)} %fusion.1.after_ref), channel_id=1, source_target_pairs={{0,4},{2,6},{4,0},{6,2},{8,12},{10,14},{12,8},{14,10},{1,5},{3,7},... | collective-permute-start | bytes 175112 | tf_op jit(solution)/shard_map/ppermute | solution.py:25
  6.6 5.2 %shard_map.64.refs_4_ = bf16[2,7168,512]{2,1,0:T(8,128)(2,1)S(1)} custom-call(bf16[2,7168,512]{2,1,0:T(8,128)(2,1)} %source_ref.2, bf16[4,7296]{1,0:T(4,128)(2,1)S(1)} %fusion.1.after_ref), custom_call_target="tpu_custom_call" | custom-call | bytes 14680064 | tf_op jit(solution)/shard_map/pallas_call | solution.py:57
  11.9 0.1 pad_maximum_fusion.after_ref.refs_0_
  12.0 1.7 %collective-permute-start.3 = (bf16[16,7296]{1,0:T(8,128)(2,1)S(1)}, bf16[16,7296]{1,0:T(8,128)(2,1)S(1)}, u32[]{:S(2)}, u32[]{:S(2)}) collective-permute-start(bf16[16,7296]{1,0:T(8,128)(2,1)S(1)} %pad_maximum_fusion.after_ref.refs_0_), channel_id=1, source_target_pairs={{0,1},{1,0},{2,3},{3,2},{4,5},{5,4},{6,7},{7,6},{8,9},{9,8},{10,11... | collective-permute-start | bytes 700424 | tf_op jit(solution)/shard_map/ppermute | solution.py:17
  13.7 5.2 %shard_map.65.refs_5_ = bf16[2,7168,512]{2,1,0:T(8,128)(2,1)S(1)} custom-call(bf16[2,7168,512]{2,1,0:T(8,128)(2,1)} %source_ref.3, bf16[16,7296]{1,0:T(8,128)(2,1)S(1)} %pad_maximum_fusion.after_ref.refs_0_), custom_call_target="tpu_custom_call" | custom-call | bytes 14680064 | tf_op jit(solution)/shard_map/pallas_call | solution.py:57
  18.9 0.0 collective-permute-done.3.refs_1_
  19.0 0.6 %collective-permute-start.5 = (bf16[16,7296]{1,0:T(8,128)(2,1)S(1)}, bf16[16,7296]{1,0:T(8,128)(2,1)S(1)}, u32[]{:S(2)}, u32[]{:S(2)}) collective-permute-start(bf16[16,7296]{1,0:T(8,128)(2,1)S(1)} %collective-permute-done.3.refs_1_), channel_id=1, source_target_pairs={{0,2},{2,0},{4,6},{6,4},{8,10},{10,8},{12,14},{14,12},{1,3},{3,1},... | collective-permute-start | bytes 700424 | tf_op jit(solution)/shard_map/ppermute | solution.py:29
  19.5 1.1 %collective-permute-done.5.refs_3_ = bf16[16,7296]{1,0:T(8,128)(2,1)S(1)} collective-permute-done((bf16[16,7296]{1,0:T(8,128)(2,1)S(1)}, bf16[16,7296]{1,0:T(8,128)(2,1)S(1)}, u32[]{:S(2)}, u32[]{:S(2)}) %collective-permute-start.5) | collective-permute-done | bytes 233504 | tf_op jit(solution)/shard_map/ppermute | solution.py:29
  20.6 7.0 %shard_map.66 = (f32[16,7168]{1,0:T(8,128)S(1)}, f32[16,7168]{1,0:T(8,128)S(1)}, bf16[16,7168]{1,0:T(8,128)(2,1)S(1)}, bf16[16,7168]{1,0:T(8,128)(2,1)S(1)}) custom-call(bf16[16,7296]{1,0:T(8,128)(2,1)S(1)} %pad_maximum_fusion.after_ref.refs_0_, bf16[16,7296]{1,0:T(8,128)(2,1)S(1)} %collective-permute-done.3.refs_1_, ...), custom_call_target="tpu_custom_call" | custom-call | tf_op jit(solution)/shard_map/pallas_call | solution.py:165
  27.7 0.4 collective-permute-start.7
  28.1 0.1 collective-permute-start.6
  28.3 1.0 %collective-permute-done.7 = bf16[16,7168]{1,0:T(8,128)(2,1)S(1)} collective-permute-done((bf16[16,7168]{1,0:T(8,128)(2,1)S(1)}, bf16[16,7168]{1,0:T(8,128)(2,1)S(1)}, u32[]{:S(2)}, u32[]{:S(2)}) %collective-permute-start.7) | collective-permute-done | bytes 229408 | tf_op jit(solution)/shard_map/ppermute | solution.py:29
  29.2 0.1 add_convert_fusion
  29.3 1.4 %collective-permute-start.8 = (bf16[8,7168]{1,0:T(8,128)(2,1)S(1)}, bf16[8,7168]{1,0:T(8,128)(2,1)S(1)}, u32[]{:S(2)}, u32[]{:S(2)}) collective-permute-start(bf16[8,7168]{1,0:T(8,128)(2,1)S(1)} %get-tuple-element.38), channel_id=1, source_target_pairs={{0,1},{1,0},{2,3},{3,2},{4,5},{5,4},{6,7},{7,6},{8,9},{9,8},{10,11... | collective-permute-start | bytes 344072 | tf_op jit(solution)/shard_map/ppermute | solution.py:17
  30.8 4.0 %collective-permute-done.8.refs_1_ = bf16[8,7168]{1,0:T(8,128)(2,1)S(1)} collective-permute-done((bf16[8,7168]{1,0:T(8,128)(2,1)S(1)}, bf16[8,7168]{1,0:T(8,128)(2,1)S(1)}, u32[]{:S(2)}, u32[]{:S(2)}) %collective-permute-start.8) | collective-permute-done | bytes 114720 | tf_op jit(solution)/shard_map/ppermute | solution.py:17
  34.8 1.2 %collective-permute-start.9 = (bf16[8,7168]{1,0:T(8,128)(2,1)S(1)}, bf16[8,7168]{1,0:T(8,128)(2,1)S(1)}, u32[]{:S(2)}, u32[]{:S(2)}) collective-permute-start(bf16[8,7168]{1,0:T(8,128)(2,1)S(1)} %get-tuple-element.31), channel_id=1, source_target_pairs={{0,1},{1,0},{2,3},{3,2},{4,5},{5,4},{6,7},{7,6},{8,9},{9,8},{10,11... | collective-permute-start | bytes 344072 | tf_op jit(solution)/shard_map/ppermute | solution.py:17
  36.0 3.5 %collective-permute-start.12 = (bf16[4,7168]{1,0:T(4,128)(2,1)S(1)}, bf16[4,7168]{1,0:T(4,128)(2,1)S(1)}, u32[]{:S(2)}, u32[]{:S(2)}) collective-permute-start(bf16[4,7168]{1,0:T(4,128)(2,1)S(1)} %get-tuple-element.30), channel_id=1, source_target_pairs={{0,12},{2,14},{4,8},{6,10},{8,4},{10,6},{12,0},{14,2},{1,13},{3,15... | collective-permute-start | bytes 172040 | tf_op jit(solution)/shard_map/ppermute | solution.py:25
  39.5 0.2 collective-permute-done.9.refs_1_
  39.7 1.3 %collective-permute-start.10 = (bf16[4,7168]{1,0:T(4,128)(2,1)S(1)}, bf16[4,7168]{1,0:T(4,128)(2,1)S(1)}, u32[]{:S(2)}, u32[]{:S(2)}) collective-permute-start(bf16[4,7168]{1,0:T(4,128)(2,1)S(1)} %get-tuple-element.33), channel_id=1, source_target_pairs={{0,4},{2,6},{4,0},{6,2},{8,12},{10,14},{12,8},{14,10},{1,5},{3,7},... | collective-permute-start | bytes 172040 | tf_op jit(solution)/shard_map/ppermute | solution.py:25
  41.1 3.5 %collective-permute-done.11 = bf16[4,7168]{1,0:T(4,128)(2,1)S(1)} collective-permute-done((bf16[4,7168]{1,0:T(4,128)(2,1)S(1)}, bf16[4,7168]{1,0:T(4,128)(2,1)S(1)}, u32[]{:S(2)}, u32[]{:S(2)}) %collective-permute-start.11) | collective-permute-done | bytes 57376 | tf_op jit(solution)/shard_map/ppermute | solution.py:25
  44.6 0.7 %add_convert_fusion.1 = bf16[4,7168]{1,0:T(4,128)(2,1)} fusion(bf16[4,7168]{1,0:T(4,128)(2,1)S(1)} %collective-permute-done.12, bf16[4,7168]{1,0:T(4,128)(2,1)S(1)} %collective-permute-done.11, f32[4,7168]{1,0:T(4,128)S(1)} %get-tuple-element.32, bf16[4,7168]{1,0:T(4,128)(2,1)S(1)} %collective-permute-done.10), kind=kLoop, calls=%fused_computation.4 | loop fusion | flops 200704 | bytes 344064 | tf_op jit(solution)/shard_map/convert_element_type | solution.py:196
  (15 shorter events, 0.2 us)
Async XLA Ops:
  1.0 10.9 %collective-permute-start.2 = (bf16[4,7296]{1,0:T(4,128)(2,1)S(1)}, bf16[4,7296]{1,0:T(4,128)(2,1)S(1)}, u32[]{:S(2)}, u32[]{:S(2)}) collective-permute-start(bf16[4,7296]{1,0:T(4,128)(2,1)S(1)} %fusion.1.after_ref), channel_id=1, source_target_pairs={{0,12},{2,14},{4,8},{6,10},{8,4},{10,6},{12,0},{14,2},{1,13},{3,15... | collective-permute-start | bytes 175112 | tf_op jit(solution)/shard_map/ppermute | solution.py:25
  6.0 5.8 %collective-permute-start.1 = (bf16[4,7296]{1,0:T(4,128)(2,1)S(1)}, bf16[4,7296]{1,0:T(4,128)(2,1)S(1)}, u32[]{:S(2)}, u32[]{:S(2)}) collective-permute-start(bf16[4,7296]{1,0:T(4,128)(2,1)S(1)} %fusion.1.after_ref), channel_id=1, source_target_pairs={{0,8},{2,10},{4,12},{6,14},{8,0},{10,2},{12,4},{14,6},{1,9},{3,11}... | collective-permute-start | bytes 175112 | tf_op jit(solution)/shard_map/ppermute | solution.py:25
  6.0 5.9 %collective-permute-start = (bf16[4,7296]{1,0:T(4,128)(2,1)S(1)}, bf16[4,7296]{1,0:T(4,128)(2,1)S(1)}, u32[]{:S(2)}, u32[]{:S(2)}) collective-permute-start(bf16[4,7296]{1,0:T(4,128)(2,1)S(1)} %fusion.1.after_ref), channel_id=1, source_target_pairs={{0,4},{2,6},{4,0},{6,2},{8,12},{10,14},{12,8},{14,10},{1,5},{3,7},... | collective-permute-start | bytes 175112 | tf_op jit(solution)/shard_map/ppermute | solution.py:25
  12.0 6.9 %collective-permute-start.3 = (bf16[16,7296]{1,0:T(8,128)(2,1)S(1)}, bf16[16,7296]{1,0:T(8,128)(2,1)S(1)}, u32[]{:S(2)}, u32[]{:S(2)}) collective-permute-start(bf16[16,7296]{1,0:T(8,128)(2,1)S(1)} %pad_maximum_fusion.after_ref.refs_0_), channel_id=1, source_target_pairs={{0,1},{1,0},{2,3},{3,2},{4,5},{5,4},{6,7},{7,6},{8,9},{9,8},{10,11... | collective-permute-start | bytes 700424 | tf_op jit(solution)/shard_map/ppermute | solution.py:17
  13.7 5.8 %collective-permute-start.4 = (bf16[16,7296]{1,0:T(8,128)(2,1)S(1)}, bf16[16,7296]{1,0:T(8,128)(2,1)S(1)}, u32[]{:S(2)}, u32[]{:S(2)}) collective-permute-start(bf16[16,7296]{1,0:T(8,128)(2,1)S(1)} %pad_maximum_fusion.after_ref.refs_0_), channel_id=1, source_target_pairs={{0,2},{2,0},{4,6},{6,4},{8,10},{10,8},{12,14},{14,12},{1,3},{3,1},... | collective-permute-start | bytes 700424 | tf_op jit(solution)/shard_map/ppermute | solution.py:29
  19.0 1.7 %collective-permute-start.5 = (bf16[16,7296]{1,0:T(8,128)(2,1)S(1)}, bf16[16,7296]{1,0:T(8,128)(2,1)S(1)}, u32[]{:S(2)}, u32[]{:S(2)}) collective-permute-start(bf16[16,7296]{1,0:T(8,128)(2,1)S(1)} %collective-permute-done.3.refs_1_), channel_id=1, source_target_pairs={{0,2},{2,0},{4,6},{6,4},{8,10},{10,8},{12,14},{14,12},{1,3},{3,1},... | collective-permute-start | bytes 700424 | tf_op jit(solution)/shard_map/ppermute | solution.py:29
  27.7 1.6 %collective-permute-start.7 = (bf16[16,7168]{1,0:T(8,128)(2,1)S(1)}, bf16[16,7168]{1,0:T(8,128)(2,1)S(1)}, u32[]{:S(2)}, u32[]{:S(2)}) collective-permute-start(bf16[16,7168]{1,0:T(8,128)(2,1)S(1)} %get-tuple-element.29), channel_id=1, source_target_pairs={{0,2},{2,0},{4,6},{6,4},{8,10},{10,8},{12,14},{14,12},{1,3},{3,1},... | collective-permute-start | bytes 688136 | tf_op jit(solution)/shard_map/ppermute | solution.py:29
  28.1 2.6 %collective-permute-start.6 = (bf16[16,7168]{1,0:T(8,128)(2,1)S(1)}, bf16[16,7168]{1,0:T(8,128)(2,1)S(1)}, u32[]{:S(2)}, u32[]{:S(2)}) collective-permute-start(bf16[16,7168]{1,0:T(8,128)(2,1)S(1)} %get-tuple-element.27), channel_id=1, source_target_pairs={{0,2},{2,0},{4,6},{6,4},{8,10},{10,8},{12,14},{14,12},{1,3},{3,1},... | collective-permute-start | bytes 688136 | tf_op jit(solution)/shard_map/ppermute | solution.py:29
  29.3 5.5 %collective-permute-start.8 = (bf16[8,7168]{1,0:T(8,128)(2,1)S(1)}, bf16[8,7168]{1,0:T(8,128)(2,1)S(1)}, u32[]{:S(2)}, u32[]{:S(2)}) collective-permute-start(bf16[8,7168]{1,0:T(8,128)(2,1)S(1)} %get-tuple-element.38), channel_id=1, source_target_pairs={{0,1},{1,0},{2,3},{3,2},{4,5},{5,4},{6,7},{7,6},{8,9},{9,8},{10,11... | collective-permute-start | bytes 344072 | tf_op jit(solution)/shard_map/ppermute | solution.py:17
  34.8 4.9 %collective-permute-start.9 = (bf16[8,7168]{1,0:T(8,128)(2,1)S(1)}, bf16[8,7168]{1,0:T(8,128)(2,1)S(1)}, u32[]{:S(2)}, u32[]{:S(2)}) collective-permute-start(bf16[8,7168]{1,0:T(8,128)(2,1)S(1)} %get-tuple-element.31), channel_id=1, source_target_pairs={{0,1},{1,0},{2,3},{3,2},{4,5},{5,4},{6,7},{7,6},{8,9},{9,8},{10,11... | collective-permute-start | bytes 344072 | tf_op jit(solution)/shard_map/ppermute | solution.py:17
  36.0 8.6 %collective-permute-start.12 = (bf16[4,7168]{1,0:T(4,128)(2,1)S(1)}, bf16[4,7168]{1,0:T(4,128)(2,1)S(1)}, u32[]{:S(2)}, u32[]{:S(2)}) collective-permute-start(bf16[4,7168]{1,0:T(4,128)(2,1)S(1)} %get-tuple-element.30), channel_id=1, source_target_pairs={{0,12},{2,14},{4,8},{6,10},{8,4},{10,6},{12,0},{14,2},{1,13},{3,15... | collective-permute-start | bytes 172040 | tf_op jit(solution)/shard_map/ppermute | solution.py:25
  39.5 5.1 %collective-permute-start.11 = (bf16[4,7168]{1,0:T(4,128)(2,1)S(1)}, bf16[4,7168]{1,0:T(4,128)(2,1)S(1)}, u32[]{:S(2)}, u32[]{:S(2)}) collective-permute-start(bf16[4,7168]{1,0:T(4,128)(2,1)S(1)} %get-tuple-element.34), channel_id=1, source_target_pairs={{0,8},{2,10},{4,12},{6,14},{8,0},{10,2},{12,4},{14,6},{1,9},{3,11}... | collective-permute-start | bytes 172040 | tf_op jit(solution)/shard_map/ppermute | solution.py:25
  39.7 4.9 %collective-permute-start.10 = (bf16[4,7168]{1,0:T(4,128)(2,1)S(1)}, bf16[4,7168]{1,0:T(4,128)(2,1)S(1)}, u32[]{:S(2)}, u32[]{:S(2)}) collective-permute-start(bf16[4,7168]{1,0:T(4,128)(2,1)S(1)} %get-tuple-element.33), channel_id=1, source_target_pairs={{0,4},{2,6},{4,0},{6,2},{8,12},{10,14},{12,8},{14,10},{1,5},{3,7},... | collective-permute-start | bytes 172040 | tf_op jit(solution)/shard_map/ppermute | solution.py:25

commit v6 on v5

--- a/solution.py
+++ b/solution.py
@@ -47,16 +47,17 @@
 
 
 def fetch_kernel(source_ref, after_ref, out_ref, sem):
-    copy = pltpu.make_async_copy(source_ref, out_ref, sem)
+    copy = pltpu.make_async_copy(source_ref.at[:, : out_ref.shape[1]], out_ref, sem)
     copy.start()
     copy.wait()
 
 
-def fetch(weights, after, limit):
-    nbytes = weights.size * 2
+def fetch(weights, depth, after, limit):
+    shape = (weights.shape[0], depth, weights.shape[2])
+    nbytes = shape[0] * shape[1] * shape[2] * 2
     return pl.pallas_call(
         fetch_kernel,
-        out_shape=jax.ShapeDtypeStruct(weights.shape, weights.dtype),
+        out_shape=jax.ShapeDtypeStruct(shape, weights.dtype),
         in_specs=[pl.BlockSpec(memory_space=pl.ANY)] * 2,
         out_specs=pl.BlockSpec(memory_space=pltpu.VMEM),
         scratch_shapes=[pltpu.SemaphoreType.DMA],
@@ -66,8 +67,8 @@
 
 
 def experts_kernel(count, *refs):
-    pieces, (gate_ref, up_ref, down_hbm), outs = refs[:count], refs[count : count + 3], refs[count + 3 : -4]
-    down_ref, x_ref, acts_ref, sems = refs[-4:]
+    pieces, (gate_ref, up_ref, gate_hbm, down_hbm), outs = refs[:count], refs[count : count + 4], refs[count + 4 : -6]
+    down_ref, rest_ref, x_ref, acts_ref, sems, rest_sem = refs[-6:]
     depth, width = down_ref.shape
     pairs = gate_ref.shape[0]
     hidden_here = depth // pairs
@@ -79,6 +80,9 @@
         columns = pl.ds(pl.multiple_of(c * step, LANES), step)
         return columns, pltpu.make_async_copy(down_hbm.at[:, columns], down_ref.at[:, columns], sems.at[c])
 
+    early = gate_ref.shape[1]
+    rest = pltpu.make_async_copy(gate_hbm.at[:, early:], rest_ref, rest_sem)
+    rest.start()
     for c in range(chunks):
         piece(c)[1].start()
     group = lax.axis_index("group").astype(jnp.float32)
@@ -91,7 +95,7 @@
     rows = side.shape[0]
     acts_ref[...] = jnp.zeros_like(acts_ref)
 
-    half = width // 2
+    half = early // 2
 
     def enter(c, carry):
         depths = pl.ds(pl.multiple_of(c * half, LANES), half)
@@ -102,6 +106,11 @@
         return carry
 
     lax.fori_loop(0, 2, enter, 0)
+    rest.wait()
+    x = x_ref[:, early:]
+    for e in range(pairs):
+        acts_ref[e, 0] += jnp.dot(x, rest_ref[e], preferred_element_type=jnp.float32)
+        acts_ref[e, 1] += jnp.dot(x, up_ref[e, early:], preferred_element_type=jnp.float32)
     hidden, weight = [], []
     for e in range(pairs):
         total = jnp.zeros((rows, 1), jnp.float32)
@@ -152,12 +161,13 @@
     rows_here, width = tokens.shape
     pairs, _, hidden_here = w_gate.shape
     mine = pack(tokens, routes, gate_weights)
+    early = width - width // 7
     others = [chip_shift(mine, k, False) for k in range(1, chips)]
-    gate_here, others = lax.optimization_barrier((fetch(w_gate, mine, 34), others))
+    gate_here, others = lax.optimization_barrier((fetch(w_gate, early, mine, 38), others))
     line = jnp.concatenate([mine] + others, axis=0)
     crossed = [rotate(line, "local", k, 1) for k in range(1, locals_)]
     across_line = other_core(line)
-    up_here, crossed = lax.optimization_barrier((fetch(w_up, line, 28), crossed))
+    up_here, crossed = lax.optimization_barrier((fetch(w_up, width, line, 29), crossed))
     pieces = [line] + crossed + [across_line] + [other_core(part) for part in crossed]
     block = chips * rows_here
     rows = 2 * locals_ * block
@@ -166,15 +176,17 @@
         functools.partial(experts_kernel, len(pieces)),
         out_shape=[jax.ShapeDtypeStruct((block, width), jnp.float32)] * locals_
         + [jax.ShapeDtypeStruct((block, width), jnp.bfloat16)] * locals_,
-        in_specs=[pl.BlockSpec(memory_space=pltpu.VMEM)] * (len(pieces) + 2) + [pl.BlockSpec(memory_space=pl.ANY)],
+        in_specs=[pl.BlockSpec(memory_space=pltpu.VMEM)] * (len(pieces) + 2) + [pl.BlockSpec(memory_space=pl.ANY)] * 2,
         scratch_shapes=[
             pltpu.VMEM((pairs * hidden_here, width), jnp.bfloat16),
+            pltpu.VMEM((pairs, width - early, hidden_here), jnp.bfloat16),
             pltpu.VMEM((padded, width), jnp.bfloat16),
             pltpu.VMEM((pairs, 2, padded, hidden_here), jnp.float32),
             pltpu.SemaphoreType.DMA((2 if padded <= LEAST_ROWS else 7,)),
+            pltpu.SemaphoreType.DMA,
         ],
-        compiler_params=pltpu.CompilerParams(vmem_limit_bytes=19 << 20),
-    )(*pieces, gate_here, up_here, w_down.reshape(pairs * hidden_here, width))
+        compiler_params=pltpu.CompilerParams(vmem_limit_bytes=21 << 20),
+    )(*pieces, gate_here, up_here, w_gate, w_down.reshape(pairs * hidden_here, width))
     totals = [None] * locals_
     for k in reversed(range(locals_)):
         totals[k] = outs[k] + other_core(outs[locals_ + k]).astype(jnp.float32)

time: 45.5 us -> 44.9 us (0.987)
  Pallas kernels: 17.5 us -> 16.9 us
    pallas_call x2, Pallas kernels: 10.4 us -> 9.76 us  [fetch(): pl.pallas_call(fetch_kernel, out_shape=jax.ShapeDtypeStruct(shape, weight...]
  transfers between devices with their start and end apart: 13 -> 13, of which waited for: 5 -> 5; matrix products, arithmetic and copies ran while one was open for 0% -> 0% of each run, Pallas kernels for 23% -> 22%
where the time goes in v6:
time: 44.9 us; the launch traced here: 44.7 us
  Pallas kernels  16.9 us (38%)
  starting transfers between devices  15.9 us (35%)
  waiting for transfers between devices  9.87 us (22%)
  other arithmetic  1.88 us (4%)
    ppermute x6, starting transfers between devices, chip_shift(): return lax.ppermute(value, 'group', [(i, i ^ 2 * k) for i in range(size)])  10.5 us
    pallas_call x2, Pallas kernels, fetch(): pl.pallas_call(fetch_kernel, out_shape=jax.ShapeDtypeStruct(shape, weight...  9.76 us
    pallas_call x1, Pallas kernels, on_device(): pl.pallas_call(functools.partial(experts_kernel, len(pieces)), out_shape=...  7.02 us
    ppermute x3, starting transfers between devices, rotate(): lax.ppermute(value, axis, [(i, (i + shift * stride) % size) for i in rang...  4.29 us
    ppermute x3, waiting for transfers between devices, rotate(): lax.ppermute(value, axis, [(i, (i + shift * stride) % size) for i in rang...  4.23 us
    ppermute x6, waiting for transfers between devices, chip_shift(): return lax.ppermute(value, 'group', [(i, i ^ 2 * k) for i in range(size)])  3.54 us
    ppermute x4, waiting for transfers between devices, other_core(): lax.ppermute(value, 'group', [(i, i ^ 1) for i in range(lax.axis_size('gr...  2.1 us
    ppermute x4, starting transfers between devices, other_core(): lax.ppermute(value, 'group', [(i, i ^ 1) for i in range(lax.axis_size('gr...  1.14 us
  transfers between devices with their start and end apart: 13, of which 5 were waited for; matrix products, arithmetic and copies ran while one was open for 0% of the time, Pallas kernels for 22%

profile of v6, /device:TPU:0, one launch (start us, length us, event | category | flops | bytes accessed | tf_op | source)
XLA Modules:
  0.0 44.7 jit_solution(10237716402788066703)
XLA Ops:
  0.0 0.9 %fusion.1.after_ref = bf16[4,7296]{1,0:T(4,128)(2,1)S(1)} fusion(s32[4,4]{1,0:T(4,128)} %param.7, bf16[4,8]{1,0:T(4,128)(2,1)} %param.8, s32[7296]{0:T(1024)S(1)} %fusion.2, bf16[4,7168]{1,0:T(4,128)(2,1)} %param.6), kind=kLoop, calls=%fused_computation.6 | loop fusion | flops 233472 | bytes 145024 | tf_op jit(solution)/shard_map/add | solution.py:44
  1.0 5.1 %collective-permute-start.2 = (bf16[4,7296]{1,0:T(4,128)(2,1)S(1)}, bf16[4,7296]{1,0:T(4,128)(2,1)S(1)}, u32[]{:S(2)}, u32[]{:S(2)}) collective-permute-start(bf16[4,7296]{1,0:T(4,128)(2,1)S(1)} %fusion.1.after_ref), channel_id=1, source_target_pairs={{0,12},{2,14},{4,8},{6,10},{8,4},{10,6},{12,0},{14,2},{1,13},{3,15... | collective-permute-start | bytes 175112 | tf_op jit(solution)/shard_map/ppermute | solution.py:25
  6.0 0.0 collective-permute-start.1
  6.0 0.6 %collective-permute-start = (bf16[4,7296]{1,0:T(4,128)(2,1)S(1)}, bf16[4,7296]{1,0:T(4,128)(2,1)S(1)}, u32[]{:S(2)}, u32[]{:S(2)}) collective-permute-start(bf16[4,7296]{1,0:T(4,128)(2,1)S(1)} %fusion.1.after_ref), channel_id=1, source_target_pairs={{0,4},{2,6},{4,0},{6,2},{8,12},{10,14},{12,8},{14,10},{1,5},{3,7},... | collective-permute-start | bytes 175112 | tf_op jit(solution)/shard_map/ppermute | solution.py:25
  6.6 4.6 %shard_map.64.refs_4_ = bf16[2,6144,512]{2,1,0:T(8,128)(2,1)S(1)} custom-call(bf16[2,7168,512]{2,1,0:T(8,128)(2,1)} %refs_6_.1, bf16[4,7296]{1,0:T(4,128)(2,1)S(1)} %fusion.1.after_ref), custom_call_target="tpu_custom_call" | custom-call | bytes 12582912 | tf_op jit(solution)/shard_map/pallas_call | solution.py:58
  11.3 0.1 pad_maximum_fusion.after_ref.refs_0_
  11.4 1.7 %collective-permute-start.3 = (bf16[16,7296]{1,0:T(8,128)(2,1)S(1)}, bf16[16,7296]{1,0:T(8,128)(2,1)S(1)}, u32[]{:S(2)}, u32[]{:S(2)}) collective-permute-start(bf16[16,7296]{1,0:T(8,128)(2,1)S(1)} %pad_maximum_fusion.after_ref.refs_0_), channel_id=1, source_target_pairs={{0,1},{1,0},{2,3},{3,2},{4,5},{5,4},{6,7},{7,6},{8,9},{9,8},{10,11... | collective-permute-start | bytes 700424 | tf_op jit(solution)/shard_map/ppermute | solution.py:17
  13.2 5.2 %shard_map.65.refs_5_ = bf16[2,7168,512]{2,1,0:T(8,128)(2,1)S(1)} custom-call(bf16[2,7168,512]{2,1,0:T(8,128)(2,1)} %source_ref.3, bf16[16,7296]{1,0:T(8,128)(2,1)S(1)} %pad_maximum_fusion.after_ref.refs_0_), custom_call_target="tpu_custom_call" | custom-call | bytes 14680064 | tf_op jit(solution)/shard_map/pallas_call | solution.py:58
  18.3 0.0 collective-permute-done.3.refs_1_
  18.4 0.6 %collective-permute-start.5 = (bf16[16,7296]{1,0:T(8,128)(2,1)S(1)}, bf16[16,7296]{1,0:T(8,128)(2,1)S(1)}, u32[]{:S(2)}, u32[]{:S(2)}) collective-permute-start(bf16[16,7296]{1,0:T(8,128)(2,1)S(1)} %collective-permute-done.3.refs_1_), channel_id=1, source_target_pairs={{0,2},{2,0},{4,6},{6,4},{8,10},{10,8},{12,14},{14,12},{1,3},{3,1},... | collective-permute-start | bytes 700424 | tf_op jit(solution)/shard_map/ppermute | solution.py:29
  18.9 1.1 %collective-permute-done.5.refs_3_ = bf16[16,7296]{1,0:T(8,128)(2,1)S(1)} collective-permute-done((bf16[16,7296]{1,0:T(8,128)(2,1)S(1)}, bf16[16,7296]{1,0:T(8,128)(2,1)S(1)}, u32[]{:S(2)}, u32[]{:S(2)}) %collective-permute-start.5) | collective-permute-done | bytes 233504 | tf_op jit(solution)/shard_map/ppermute | solution.py:29
  20.0 7.0 %shard_map.66 = (f32[16,7168]{1,0:T(8,128)S(1)}, f32[16,7168]{1,0:T(8,128)S(1)}, bf16[16,7168]{1,0:T(8,128)(2,1)S(1)}, bf16[16,7168]{1,0:T(8,128)(2,1)S(1)}) custom-call(bf16[16,7296]{1,0:T(8,128)(2,1)S(1)} %pad_maximum_fusion.after_ref.refs_0_, bf16[16,7296]{1,0:T(8,128)(2,1)S(1)} %collective-permute-done.3.refs_1_, ...), custom_call_target="tpu_custom_call" | custom-call | tf_op jit(solution)/shard_map/pallas_call | solution.py:175
  27.1 0.4 collective-permute-start.7
  27.5 0.2 collective-permute-start.6
  27.6 1.0 %collective-permute-done.7 = bf16[16,7168]{1,0:T(8,128)(2,1)S(1)} collective-permute-done((bf16[16,7168]{1,0:T(8,128)(2,1)S(1)}, bf16[16,7168]{1,0:T(8,128)(2,1)S(1)}, u32[]{:S(2)}, u32[]{:S(2)}) %collective-permute-start.7) | collective-permute-done | bytes 229408 | tf_op jit(solution)/shard_map/ppermute | solution.py:29
  28.6 0.1 add_convert_fusion
  28.7 1.4 %collective-permute-start.8 = (bf16[8,7168]{1,0:T(8,128)(2,1)S(1)}, bf16[8,7168]{1,0:T(8,128)(2,1)S(1)}, u32[]{:S(2)}, u32[]{:S(2)}) collective-permute-start(bf16[8,7168]{1,0:T(8,128)(2,1)S(1)} %get-tuple-element.38), channel_id=1, source_target_pairs={{0,1},{1,0},{2,3},{3,2},{4,5},{5,4},{6,7},{7,6},{8,9},{9,8},{10,11... | collective-permute-start | bytes 344072 | tf_op jit(solution)/shard_map/ppermute | solution.py:17
  30.2 4.0 %collective-permute-done.8.refs_1_ = bf16[8,7168]{1,0:T(8,128)(2,1)S(1)} collective-permute-done((bf16[8,7168]{1,0:T(8,128)(2,1)S(1)}, bf16[8,7168]{1,0:T(8,128)(2,1)S(1)}, u32[]{:S(2)}, u32[]{:S(2)}) %collective-permute-start.8) | collective-permute-done | bytes 114720 | tf_op jit(solution)/shard_map/ppermute | solution.py:17
  34.2 1.2 %collective-permute-start.9 = (bf16[8,7168]{1,0:T(8,128)(2,1)S(1)}, bf16[8,7168]{1,0:T(8,128)(2,1)S(1)}, u32[]{:S(2)}, u32[]{:S(2)}) collective-permute-start(bf16[8,7168]{1,0:T(8,128)(2,1)S(1)} %get-tuple-element.31), channel_id=1, source_target_pairs={{0,1},{1,0},{2,3},{3,2},{4,5},{5,4},{6,7},{7,6},{8,9},{9,8},{10,11... | collective-permute-start | bytes 344072 | tf_op jit(solution)/shard_map/ppermute | solution.py:17
  35.4 3.5 %collective-permute-start.12 = (bf16[4,7168]{1,0:T(4,128)(2,1)S(1)}, bf16[4,7168]{1,0:T(4,128)(2,1)S(1)}, u32[]{:S(2)}, u32[]{:S(2)}) collective-permute-start(bf16[4,7168]{1,0:T(4,128)(2,1)S(1)} %get-tuple-element.30), channel_id=1, source_target_pairs={{0,12},{2,14},{4,8},{6,10},{8,4},{10,6},{12,0},{14,2},{1,13},{3,15... | collective-permute-start | bytes 172040 | tf_op jit(solution)/shard_map/ppermute | solution.py:25
  38.9 0.2 collective-permute-done.9.refs_1_
  39.1 1.3 %collective-permute-start.10 = (bf16[4,7168]{1,0:T(4,128)(2,1)S(1)}, bf16[4,7168]{1,0:T(4,128)(2,1)S(1)}, u32[]{:S(2)}, u32[]{:S(2)}) collective-permute-start(bf16[4,7168]{1,0:T(4,128)(2,1)S(1)} %get-tuple-element.33), channel_id=1, source_target_pairs={{0,4},{2,6},{4,0},{6,2},{8,12},{10,14},{12,8},{14,10},{1,5},{3,7},... | collective-permute-start | bytes 172040 | tf_op jit(solution)/shard_map/ppermute | solution.py:25
  40.4 3.5 %collective-permute-done.11 = bf16[4,7168]{1,0:T(4,128)(2,1)S(1)} collective-permute-done((bf16[4,7168]{1,0:T(4,128)(2,1)S(1)}, bf16[4,7168]{1,0:T(4,128)(2,1)S(1)}, u32[]{:S(2)}, u32[]{:S(2)}) %collective-permute-start.11) | collective-permute-done | bytes 57376 | tf_op jit(solution)/shard_map/ppermute | solution.py:25
  44.0 0.7 %add_convert_fusion.1 = bf16[4,7168]{1,0:T(4,128)(2,1)} fusion(bf16[4,7168]{1,0:T(4,128)(2,1)S(1)} %collective-permute-done.12, bf16[4,7168]{1,0:T(4,128)(2,1)S(1)} %collective-permute-done.11, f32[4,7168]{1,0:T(4,128)S(1)} %get-tuple-element.32, bf16[4,7168]{1,0:T(4,128)(2,1)S(1)} %collective-permute-done.10), kind=kLoop, calls=%fused_computation.4 | loop fusion | flops 200704 | bytes 344064 | tf_op jit(solution)/shard_map/convert_element_type | solution.py:208
  (15 shorter events, 0.2 us)
Async XLA Ops:
  1.0 10.3 %collective-permute-start.2 = (bf16[4,7296]{1,0:T(4,128)(2,1)S(1)}, bf16[4,7296]{1,0:T(4,128)(2,1)S(1)}, u32[]{:S(2)}, u32[]{:S(2)}) collective-permute-start(bf16[4,7296]{1,0:T(4,128)(2,1)S(1)} %fusion.1.after_ref), channel_id=1, source_target_pairs={{0,12},{2,14},{4,8},{6,10},{8,4},{10,6},{12,0},{14,2},{1,13},{3,15... | collective-permute-start | bytes 175112 | tf_op jit(solution)/shard_map/ppermute | solution.py:25
  6.0 5.2 %collective-permute-start.1 = (bf16[4,7296]{1,0:T(4,128)(2,1)S(1)}, bf16[4,7296]{1,0:T(4,128)(2,1)S(1)}, u32[]{:S(2)}, u32[]{:S(2)}) collective-permute-start(bf16[4,7296]{1,0:T(4,128)(2,1)S(1)} %fusion.1.after_ref), channel_id=1, source_target_pairs={{0,8},{2,10},{4,12},{6,14},{8,0},{10,2},{12,4},{14,6},{1,9},{3,11}... | collective-permute-start | bytes 175112 | tf_op jit(solution)/shard_map/ppermute | solution.py:25
  6.0 5.3 %collective-permute-start = (bf16[4,7296]{1,0:T(4,128)(2,1)S(1)}, bf16[4,7296]{1,0:T(4,128)(2,1)S(1)}, u32[]{:S(2)}, u32[]{:S(2)}) collective-permute-start(bf16[4,7296]{1,0:T(4,128)(2,1)S(1)} %fusion.1.after_ref), channel_id=1, source_target_pairs={{0,4},{2,6},{4,0},{6,2},{8,12},{10,14},{12,8},{14,10},{1,5},{3,7},... | collective-permute-start | bytes 175112 | tf_op jit(solution)/shard_map/ppermute | solution.py:25
  11.4 6.9 %collective-permute-start.3 = (bf16[16,7296]{1,0:T(8,128)(2,1)S(1)}, bf16[16,7296]{1,0:T(8,128)(2,1)S(1)}, u32[]{:S(2)}, u32[]{:S(2)}) collective-permute-start(bf16[16,7296]{1,0:T(8,128)(2,1)S(1)} %pad_maximum_fusion.after_ref.refs_0_), channel_id=1, source_target_pairs={{0,1},{1,0},{2,3},{3,2},{4,5},{5,4},{6,7},{7,6},{8,9},{9,8},{10,11... | collective-permute-start | bytes 700424 | tf_op jit(solution)/shard_map/ppermute | solution.py:17
  13.1 5.8 %collective-permute-start.4 = (bf16[16,7296]{1,0:T(8,128)(2,1)S(1)}, bf16[16,7296]{1,0:T(8,128)(2,1)S(1)}, u32[]{:S(2)}, u32[]{:S(2)}) collective-permute-start(bf16[16,7296]{1,0:T(8,128)(2,1)S(1)} %pad_maximum_fusion.after_ref.refs_0_), channel_id=1, source_target_pairs={{0,2},{2,0},{4,6},{6,4},{8,10},{10,8},{12,14},{14,12},{1,3},{3,1},... | collective-permute-start | bytes 700424 | tf_op jit(solution)/shard_map/ppermute | solution.py:29
  18.4 1.7 %collective-permute-start.5 = (bf16[16,7296]{1,0:T(8,128)(2,1)S(1)}, bf16[16,7296]{1,0:T(8,128)(2,1)S(1)}, u32[]{:S(2)}, u32[]{:S(2)}) collective-permute-start(bf16[16,7296]{1,0:T(8,128)(2,1)S(1)} %collective-permute-done.3.refs_1_), channel_id=1, source_target_pairs={{0,2},{2,0},{4,6},{6,4},{8,10},{10,8},{12,14},{14,12},{1,3},{3,1},... | collective-permute-start | bytes 700424 | tf_op jit(solution)/shard_map/ppermute | solution.py:29
  27.1 1.6 %collective-permute-start.7 = (bf16[16,7168]{1,0:T(8,128)(2,1)S(1)}, bf16[16,7168]{1,0:T(8,128)(2,1)S(1)}, u32[]{:S(2)}, u32[]{:S(2)}) collective-permute-start(bf16[16,7168]{1,0:T(8,128)(2,1)S(1)} %get-tuple-element.29), channel_id=1, source_target_pairs={{0,2},{2,0},{4,6},{6,4},{8,10},{10,8},{12,14},{14,12},{1,3},{3,1},... | collective-permute-start | bytes 688136 | tf_op jit(solution)/shard_map/ppermute | solution.py:29
  27.5 2.6 %collective-permute-start.6 = (bf16[16,7168]{1,0:T(8,128)(2,1)S(1)}, bf16[16,7168]{1,0:T(8,128)(2,1)S(1)}, u32[]{:S(2)}, u32[]{:S(2)}) collective-permute-start(bf16[16,7168]{1,0:T(8,128)(2,1)S(1)} %get-tuple-element.27), channel_id=1, source_target_pairs={{0,2},{2,0},{4,6},{6,4},{8,10},{10,8},{12,14},{14,12},{1,3},{3,1},... | collective-permute-start | bytes 688136 | tf_op jit(solution)/shard_map/ppermute | solution.py:29
  28.7 5.5 %collective-permute-start.8 = (bf16[8,7168]{1,0:T(8,128)(2,1)S(1)}, bf16[8,7168]{1,0:T(8,128)(2,1)S(1)}, u32[]{:S(2)}, u32[]{:S(2)}) collective-permute-start(bf16[8,7168]{1,0:T(8,128)(2,1)S(1)} %get-tuple-element.38), channel_id=1, source_target_pairs={{0,1},{1,0},{2,3},{3,2},{4,5},{5,4},{6,7},{7,6},{8,9},{9,8},{10,11... | collective-permute-start | bytes 344072 | tf_op jit(solution)/shard_map/ppermute | solution.py:17
  34.2 4.9 %collective-permute-start.9 = (bf16[8,7168]{1,0:T(8,128)(2,1)S(1)}, bf16[8,7168]{1,0:T(8,128)(2,1)S(1)}, u32[]{:S(2)}, u32[]{:S(2)}) collective-permute-start(bf16[8,7168]{1,0:T(8,128)(2,1)S(1)} %get-tuple-element.31), channel_id=1, source_target_pairs={{0,1},{1,0},{2,3},{3,2},{4,5},{5,4},{6,7},{7,6},{8,9},{9,8},{10,11... | collective-permute-start | bytes 344072 | tf_op jit(solution)/shard_map/ppermute | solution.py:17
  35.4 8.6 %collective-permute-start.12 = (bf16[4,7168]{1,0:T(4,128)(2,1)S(1)}, bf16[4,7168]{1,0:T(4,128)(2,1)S(1)}, u32[]{:S(2)}, u32[]{:S(2)}) collective-permute-start(bf16[4,7168]{1,0:T(4,128)(2,1)S(1)} %get-tuple-element.30), channel_id=1, source_target_pairs={{0,12},{2,14},{4,8},{6,10},{8,4},{10,6},{12,0},{14,2},{1,13},{3,15... | collective-permute-start | bytes 172040 | tf_op jit(solution)/shard_map/ppermute | solution.py:25
  38.9 5.1 %collective-permute-start.11 = (bf16[4,7168]{1,0:T(4,128)(2,1)S(1)}, bf16[4,7168]{1,0:T(4,128)(2,1)S(1)}, u32[]{:S(2)}, u32[]{:S(2)}) collective-permute-start(bf16[4,7168]{1,0:T(4,128)(2,1)S(1)} %get-tuple-element.34), channel_id=1, source_target_pairs={{0,8},{2,10},{4,12},{6,14},{8,0},{10,2},{12,4},{14,6},{1,9},{3,11}... | collective-permute-start | bytes 172040 | tf_op jit(solution)/shard_map/ppermute | solution.py:25
  39.1 4.9 %collective-permute-start.10 = (bf16[4,7168]{1,0:T(4,128)(2,1)S(1)}, bf16[4,7168]{1,0:T(4,128)(2,1)S(1)}, u32[]{:S(2)}, u32[]{:S(2)}) collective-permute-start(bf16[4,7168]{1,0:T(4,128)(2,1)S(1)} %get-tuple-element.33), channel_id=1, source_target_pairs={{0,4},{2,6},{4,0},{6,2},{8,12},{10,14},{12,8},{14,10},{1,5},{3,7},... | collective-permute-start | bytes 172040 | tf_op jit(solution)/shard_map/ppermute | solution.py:25

commit v7 on v6

--- a/solution.py
+++ b/solution.py
@@ -108,9 +108,6 @@
     lax.fori_loop(0, 2, enter, 0)
     rest.wait()
     x = x_ref[:, early:]
-    for e in range(pairs):
-        acts_ref[e, 0] += jnp.dot(x, rest_ref[e], preferred_element_type=jnp.float32)
-        acts_ref[e, 1] += jnp.dot(x, up_ref[e, early:], preferred_element_type=jnp.float32)
     hidden, weight = [], []
     for e in range(pairs):
         total = jnp.zeros((rows, 1), jnp.float32)
@@ -118,8 +115,9 @@
             column = GROUPS_ROW + k * pairs + e
             total = total + jnp.where(side[:, k : k + 1] == group, side[:, column : column + 1], 0.0)
         weight.append(total)
-        gate_act = acts_ref[e, 0]
-        hidden.append((gate_act / (1.0 + jnp.exp(-gate_act)) * acts_ref[e, 1]).astype(jnp.bfloat16))
+        gate_act = acts_ref[e, 0] + jnp.dot(x, rest_ref[e], preferred_element_type=jnp.float32)
+        up_act = acts_ref[e, 1] + jnp.dot(x, up_ref[e, early:], preferred_element_type=jnp.float32)
+        hidden.append((gate_act / (1.0 + jnp.exp(-gate_act)) * up_act).astype(jnp.bfloat16))
 
     def down(c, carry):
         columns, copy = piece(c)
@@ -189,22 +187,26 @@
     )(*pieces, gate_here, up_here, w_gate, w_down.reshape(pairs * hidden_here, width))
     totals = [None] * locals_
     for k in reversed(range(locals_)):
-        totals[k] = outs[k] + other_core(outs[locals_ + k]).astype(jnp.float32)
-    home = [None] * chips
-    done = None
-    for low, high in ((chips // 2, chips), (0, chips // 2)):
-        if low == high:
-            continue
-        part = slice(low * rows_here, high * rows_here)
-        sent = [totals[k][part].astype(jnp.bfloat16) for k in range(1, locals_)]
-        if done is not None:
-            sent, done = lax.optimization_barrier((sent, done))
-        backs = [rotate(sent[k - 1], "local", -k, 1) for k in range(1, locals_)]
-        home[low:high] = join([totals[0][part]] + backs, high - low, low)
-        done = home[high - 1]
-    result = home[0]
-    for c in range(1, chips):
-        result = result + chip_shift(home[c], c, True).astype(jnp.float32)
+        away = outs[locals_ + k]
+        if k + 1 < locals_:
+            away, _ = lax.optimization_barrier((away, totals[k + 1]))
+        totals[k] = outs[k] + other_core(away).astype(jnp.float32)
+    base = [total[:rows_here] for total in totals]
+    if chips > 1:
+        near = [total[rows_here : 2 * rows_here].astype(jnp.bfloat16) for total in totals]
+        near = chip_shift(jnp.concatenate(near, axis=0), 1, True).astype(jnp.float32)
+        base = [value + near[k * rows_here : (k + 1) * rows_here] for k, value in enumerate(base)]
+    home = []
+    if chips > 2:
+        far = [total[2 * rows_here :] for total in totals]
+        backs = [rotate(far[k].astype(jnp.bfloat16), "local", -k, 1) for k in range(1, locals_)]
+        home = join([far[0]] + backs, chips - 2, 2)
+    result = base[0]
+    for k in range(1, locals_):
+        sent = base[k].astype(jnp.bfloat16)
+        result = result + rotate(sent, "local", -k, 1).astype(jnp.float32)
+    for c, value in enumerate(home):
+        result = result + chip_shift(value, c + 2, True).astype(jnp.float32)
     return result.astype(jnp.bfloat16)
 
 

time: 44.9 us -> 43.6 us (0.971)
  waiting for transfers between devices: 9.87 us -> 7.74 us
  starting transfers between devices: 15.9 us -> 16.7 us
    ppermute x3, waiting for transfers between devices: 4.23 us -> 2.47 us  [rotate(): lax.ppermute(value, axis, [(i, (i + shift * stride) % size) for i in rang...]
    ppermute x6, waiting for transfers between devices: 3.54 us -> 3.02 us  [chip_shift(): return lax.ppermute(value, 'group', [(i, i ^ 2 * k) for i in range(size)])]
  transfers between devices with their start and end apart: 13 -> 13, of which waited for: 5 -> 4; matrix products, arithmetic and copies ran while one was open for 0% -> 1% of each run, Pallas kernels for 22% -> 23%
where the time goes in v7:
time: 43.6 us; the launch traced here: 43.4 us
  Pallas kernels  16.8 us (39%)
  starting transfers between devices  16.7 us (38%)
  waiting for transfers between devices  7.74 us (18%)
  other arithmetic  2 us (5%)
    ppermute x6, starting transfers between devices, chip_shift(): return lax.ppermute(value, 'group', [(i, i ^ 2 * k) for i in range(size)])  10.9 us
    pallas_call x2, Pallas kernels, fetch(): pl.pallas_call(fetch_kernel, out_shape=jax.ShapeDtypeStruct(shape, weight...  9.76 us
    pallas_call x1, Pallas kernels, on_device(): pl.pallas_call(functools.partial(experts_kernel, len(pieces)), out_shape=...  6.96 us
    ppermute x3, starting transfers between devices, rotate(): lax.ppermute(value, axis, [(i, (i + shift * stride) % size) for i in rang...  4.36 us
    ppermute x6, waiting for transfers between devices, chip_shift(): return lax.ppermute(value, 'group', [(i, i ^ 2 * k) for i in range(size)])  3.02 us
    ppermute x3, waiting for transfers between devices, rotate(): lax.ppermute(value, axis, [(i, (i + shift * stride) % size) for i in rang...  2.47 us
    ppermute x4, waiting for transfers between devices, other_core(): lax.ppermute(value, 'group', [(i, i ^ 1) for i in range(lax.axis_size('gr...  2.24 us
    ppermute x4, starting transfers between devices, other_core(): lax.ppermute(value, 'group', [(i, i ^ 1) for i in range(lax.axis_size('gr...  1.45 us
  transfers between devices with their start and end apart: 13, of which 4 were waited for; matrix products, arithmetic and copies ran while one was open for 1% of the time, Pallas kernels for 23%

profile of v7, /device:TPU:0, one launch (start us, length us, event | category | flops | bytes accessed | tf_op | source)
XLA Modules:
  0.0 43.4 jit_solution(11026982938185914893)
XLA Ops:
  0.0 0.9 %fusion.6.after_ref = bf16[4,7296]{1,0:T(4,128)(2,1)S(1)} fusion(s32[4,4]{1,0:T(4,128)} %param.7, bf16[4,8]{1,0:T(4,128)(2,1)} %param.8, s32[7296]{0:T(1024)S(1)} %fusion.7, bf16[4,7168]{1,0:T(4,128)(2,1)} %param.6), kind=kLoop, calls=%fused_computation.14 | loop fusion | flops 233472 | bytes 145024 | tf_op jit(solution)/shard_map/add | solution.py:44
  1.0 5.1 %collective-permute-start.2 = (bf16[4,7296]{1,0:T(4,128)(2,1)S(1)}, bf16[4,7296]{1,0:T(4,128)(2,1)S(1)}, u32[]{:S(2)}, u32[]{:S(2)}) collective-permute-start(bf16[4,7296]{1,0:T(4,128)(2,1)S(1)} %fusion.6.after_ref), channel_id=1, source_target_pairs={{0,12},{2,14},{4,8},{6,10},{8,4},{10,6},{12,0},{14,2},{1,13},{3,15... | collective-permute-start | bytes 175112 | tf_op jit(solution)/shard_map/ppermute | solution.py:25
  6.0 0.6 %collective-permute-start = (bf16[4,7296]{1,0:T(4,128)(2,1)S(1)}, bf16[4,7296]{1,0:T(4,128)(2,1)S(1)}, u32[]{:S(2)}, u32[]{:S(2)}) collective-permute-start(bf16[4,7296]{1,0:T(4,128)(2,1)S(1)} %fusion.6.after_ref), channel_id=1, source_target_pairs={{0,4},{2,6},{4,0},{6,2},{8,12},{10,14},{12,8},{14,10},{1,5},{3,7},... | collective-permute-start | bytes 175112 | tf_op jit(solution)/shard_map/ppermute | solution.py:25
  6.6 4.6 %shard_map.64.refs_4_ = bf16[2,6144,512]{2,1,0:T(8,128)(2,1)S(1)} custom-call(bf16[2,7168,512]{2,1,0:T(8,128)(2,1)} %refs_6_.1, bf16[4,7296]{1,0:T(4,128)(2,1)S(1)} %fusion.6.after_ref), custom_call_target="tpu_custom_call" | custom-call | bytes 12582912 | tf_op jit(solution)/shard_map/pallas_call | solution.py:58
  11.3 0.1 pad_maximum_fusion.after_ref.refs_0_
  11.4 1.7 %collective-permute-start.3 = (bf16[16,7296]{1,0:T(8,128)(2,1)S(1)}, bf16[16,7296]{1,0:T(8,128)(2,1)S(1)}, u32[]{:S(2)}, u32[]{:S(2)}) collective-permute-start(bf16[16,7296]{1,0:T(8,128)(2,1)S(1)} %pad_maximum_fusion.after_ref.refs_0_), channel_id=1, source_target_pairs={{0,1},{1,0},{2,3},{3,2},{4,5},{5,4},{6,7},{7,6},{8,9},{9,8},{10,11... | collective-permute-start | bytes 700424 | tf_op jit(solution)/shard_map/ppermute | solution.py:17
  13.2 5.2 %shard_map.65.refs_5_ = bf16[2,7168,512]{2,1,0:T(8,128)(2,1)S(1)} custom-call(bf16[2,7168,512]{2,1,0:T(8,128)(2,1)} %source_ref.3, bf16[16,7296]{1,0:T(8,128)(2,1)S(1)} %pad_maximum_fusion.after_ref.refs_0_), custom_call_target="tpu_custom_call" | custom-call | bytes 14680064 | tf_op jit(solution)/shard_map/pallas_call | solution.py:58
  18.3 0.0 collective-permute-done.3.refs_1_
  18.4 0.6 %collective-permute-start.5 = (bf16[16,7296]{1,0:T(8,128)(2,1)S(1)}, bf16[16,7296]{1,0:T(8,128)(2,1)S(1)}, u32[]{:S(2)}, u32[]{:S(2)}) collective-permute-start(bf16[16,7296]{1,0:T(8,128)(2,1)S(1)} %collective-permute-done.3.refs_1_), channel_id=1, source_target_pairs={{0,2},{2,0},{4,6},{6,4},{8,10},{10,8},{12,14},{14,12},{1,3},{3,1},... | collective-permute-start | bytes 700424 | tf_op jit(solution)/shard_map/ppermute | solution.py:29
  18.9 1.1 %collective-permute-done.5.refs_3_ = bf16[16,7296]{1,0:T(8,128)(2,1)S(1)} collective-permute-done((bf16[16,7296]{1,0:T(8,128)(2,1)S(1)}, bf16[16,7296]{1,0:T(8,128)(2,1)S(1)}, u32[]{:S(2)}, u32[]{:S(2)}) %collective-permute-start.5) | collective-permute-done | bytes 233504 | tf_op jit(solution)/shard_map/ppermute | solution.py:29
  20.0 7.0 %shard_map.66 = (f32[16,7168]{1,0:T(8,128)S(1)}, f32[16,7168]{1,0:T(8,128)S(1)}, bf16[16,7168]{1,0:T(8,128)(2,1)S(1)}, bf16[16,7168]{1,0:T(8,128)(2,1)S(1)}) custom-call(bf16[16,7296]{1,0:T(8,128)(2,1)S(1)} %pad_maximum_fusion.after_ref.refs_0_, bf16[16,7296]{1,0:T(8,128)(2,1)S(1)} %collective-permute-done.3.refs_1_, ...), custom_call_target="tpu_custom_call" | custom-call | tf_op jit(solution)/shard_map/pallas_call | solution.py:173
  27.0 0.4 %collective-permute-start.6 = (bf16[16,7168]{1,0:T(8,128)(2,1)S(1)}, bf16[16,7168]{1,0:T(8,128)(2,1)S(1)}, u32[]{:S(2)}, u32[]{:S(2)}) collective-permute-start(bf16[16,7168]{1,0:T(8,128)(2,1)S(1)} %get-tuple-element.27), channel_id=1, source_target_pairs={{0,2},{2,0},{4,6},{6,4},{8,10},{10,8},{12,14},{14,12},{1,3},{3,1},... | collective-permute-start | bytes 688136 | tf_op jit(solution)/shard_map/ppermute | solution.py:29
  27.5 1.1 %collective-permute-done.6 = bf16[16,7168]{1,0:T(8,128)(2,1)S(1)} collective-permute-done((bf16[16,7168]{1,0:T(8,128)(2,1)S(1)}, bf16[16,7168]{1,0:T(8,128)(2,1)S(1)}, u32[]{:S(2)}, u32[]{:S(2)}) %collective-permute-start.6) | collective-permute-done | bytes 229408 | tf_op jit(solution)/shard_map/ppermute | solution.py:29
  28.6 0.1 fusion.8
  28.6 0.4 %collective-permute-start.7 = (bf16[16,7168]{1,0:T(8,128)(2,1)S(1)}, bf16[16,7168]{1,0:T(8,128)(2,1)S(1)}, u32[]{:S(2)}, u32[]{:S(2)}) collective-permute-start(bf16[16,7168]{1,0:T(8,128)(2,1)S(1)} %get-tuple-element.28), channel_id=1, source_target_pairs={{0,2},{2,0},{4,6},{6,4},{8,10},{10,8},{12,14},{14,12},{1,3},{3,1},... | collective-permute-start | bytes 688136 | tf_op jit(solution)/shard_map/ppermute | solution.py:29
  29.1 1.2 %collective-permute-start.10 = (bf16[8,7168]{1,0:T(8,128)(2,1)S(1)}, bf16[8,7168]{1,0:T(8,128)(2,1)S(1)}, u32[]{:S(2)}, u32[]{:S(2)}) collective-permute-start(bf16[8,7168]{1,0:T(8,128)(2,1)S(1)} %slice.42), channel_id=1, source_target_pairs={{0,1},{1,0},{2,3},{3,2},{4,5},{5,4},{6,7},{7,6},{8,9},{9,8},{10,11... | collective-permute-start | bytes 344072 | tf_op jit(solution)/shard_map/ppermute | solution.py:17
  30.4 0.1 pad_maximum_fusion.1
  30.5 1.5 %collective-permute-start.8 = (bf16[8,7168]{1,0:T(8,128)(2,1)S(1)}, bf16[8,7168]{1,0:T(8,128)(2,1)S(1)}, u32[]{:S(2)}, u32[]{:S(2)}) collective-permute-start(bf16[8,7168]{1,0:T(8,128)(2,1)S(1)} %pad_maximum_fusion.1), channel_id=1, source_target_pairs={{0,4},{2,6},{4,0},{6,2},{8,12},{10,14},{12,8},{14,10},{1,5},{3,7},... | collective-permute-start | bytes 344072 | tf_op jit(solution)/shard_map/ppermute | solution.py:25
  31.9 2.5 %collective-permute-done.10.refs_1_ = bf16[8,7168]{1,0:T(8,128)(2,1)S(1)} collective-permute-done((bf16[8,7168]{1,0:T(8,128)(2,1)S(1)}, bf16[8,7168]{1,0:T(8,128)(2,1)S(1)}, u32[]{:S(2)}, u32[]{:S(2)}) %collective-permute-start.10) | collective-permute-done | bytes 114720 | tf_op jit(solution)/shard_map/ppermute | solution.py:17
  34.4 2.2 %collective-permute-start.11 = (bf16[4,7168]{1,0:T(4,128)(2,1)S(1)}, bf16[4,7168]{1,0:T(4,128)(2,1)S(1)}, u32[]{:S(2)}, u32[]{:S(2)}) collective-permute-start(bf16[4,7168]{1,0:T(4,128)(2,1)S(1)} %get-tuple-element.29), channel_id=1, source_target_pairs={{0,8},{2,10},{4,12},{6,14},{8,0},{10,2},{12,4},{14,6},{1,9},{3,11}... | collective-permute-start | bytes 172040 | tf_op jit(solution)/shard_map/ppermute | solution.py:25
  36.6 1.5 %collective-permute-start.12 = (bf16[4,7168]{1,0:T(4,128)(2,1)S(1)}, bf16[4,7168]{1,0:T(4,128)(2,1)S(1)}, u32[]{:S(2)}, u32[]{:S(2)}) collective-permute-start(bf16[4,7168]{1,0:T(4,128)(2,1)S(1)} %get-tuple-element.30), channel_id=1, source_target_pairs={{0,12},{2,14},{4,8},{6,10},{8,4},{10,6},{12,0},{14,2},{1,13},{3,15... | collective-permute-start | bytes 172040 | tf_op jit(solution)/shard_map/ppermute | solution.py:25
  38.2 1.5 %collective-permute-start.9 = (bf16[4,7168]{1,0:T(4,128)(2,1)S(1)}, bf16[4,7168]{1,0:T(4,128)(2,1)S(1)}, u32[]{:S(2)}, u32[]{:S(2)}) collective-permute-start(bf16[4,7168]{1,0:T(4,128)(2,1)S(1)} %fusion), channel_id=1, source_target_pairs={{0,1},{1,0},{2,3},{3,2},{4,5},{5,4},{6,7},{7,6},{8,9},{9,8},{10,11... | collective-permute-start | bytes 172040 | tf_op jit(solution)/shard_map/ppermute | solution.py:17
  39.7 3.0 %collective-permute-done.12 = bf16[4,7168]{1,0:T(4,128)(2,1)S(1)} collective-permute-done((bf16[4,7168]{1,0:T(4,128)(2,1)S(1)}, bf16[4,7168]{1,0:T(4,128)(2,1)S(1)}, u32[]{:S(2)}, u32[]{:S(2)}) %collective-permute-start.12) | collective-permute-done | bytes 57376 | tf_op jit(solution)/shard_map/ppermute | solution.py:25
  42.7 0.7 %fusion.4 = bf16[4,7168]{1,0:T(4,128)(2,1)} fusion(f32[8,7168]{1,0:T(8,128)S(1)} %convert_element_type.33, f32[16,7168]{1,0:T(8,128)S(1)} %convert_add_fusion, bf16[4,7168]{1,0:T(4,128)(2,1)S(1)} %collective-permute-done.12, bf16[4,7168]{1,0:T(4,128)(2,1)S(1)} %collective-permute-done.11, bf16[4,7168]{1,0:T(4,128)(2,1)S(1)} %collective-permute-done.9), kind=kLoop, calls=%fused_computation.10 | loop fusion | flops 229376 | bytes 458752 | tf_op jit(solution)/shard_map/convert_element_type | solution.py:210
  (19 shorter events, 0.2 us)
Async XLA Ops:
  1.0 10.3 %collective-permute-start.2 = (bf16[4,7296]{1,0:T(4,128)(2,1)S(1)}, bf16[4,7296]{1,0:T(4,128)(2,1)S(1)}, u32[]{:S(2)}, u32[]{:S(2)}) collective-permute-start(bf16[4,7296]{1,0:T(4,128)(2,1)S(1)} %fusion.6.after_ref), channel_id=1, source_target_pairs={{0,12},{2,14},{4,8},{6,10},{8,4},{10,6},{12,0},{14,2},{1,13},{3,15... | collective-permute-start | bytes 175112 | tf_op jit(solution)/shard_map/ppermute | solution.py:25
  6.0 5.2 %collective-permute-start.1 = (bf16[4,7296]{1,0:T(4,128)(2,1)S(1)}, bf16[4,7296]{1,0:T(4,128)(2,1)S(1)}, u32[]{:S(2)}, u32[]{:S(2)}) collective-permute-start(bf16[4,7296]{1,0:T(4,128)(2,1)S(1)} %fusion.6.after_ref), channel_id=1, source_target_pairs={{0,8},{2,10},{4,12},{6,14},{8,0},{10,2},{12,4},{14,6},{1,9},{3,11}... | collective-permute-start | bytes 175112 | tf_op jit(solution)/shard_map/ppermute | solution.py:25
  6.0 5.3 %collective-permute-start = (bf16[4,7296]{1,0:T(4,128)(2,1)S(1)}, bf16[4,7296]{1,0:T(4,128)(2,1)S(1)}, u32[]{:S(2)}, u32[]{:S(2)}) collective-permute-start(bf16[4,7296]{1,0:T(4,128)(2,1)S(1)} %fusion.6.after_ref), channel_id=1, source_target_pairs={{0,4},{2,6},{4,0},{6,2},{8,12},{10,14},{12,8},{14,10},{1,5},{3,7},... | collective-permute-start | bytes 175112 | tf_op jit(solution)/shard_map/ppermute | solution.py:25
  11.4 6.9 %collective-permute-start.3 = (bf16[16,7296]{1,0:T(8,128)(2,1)S(1)}, bf16[16,7296]{1,0:T(8,128)(2,1)S(1)}, u32[]{:S(2)}, u32[]{:S(2)}) collective-permute-start(bf16[16,7296]{1,0:T(8,128)(2,1)S(1)} %pad_maximum_fusion.after_ref.refs_0_), channel_id=1, source_target_pairs={{0,1},{1,0},{2,3},{3,2},{4,5},{5,4},{6,7},{7,6},{8,9},{9,8},{10,11... | collective-permute-start | bytes 700424 | tf_op jit(solution)/shard_map/ppermute | solution.py:17
  13.1 5.8 %collective-permute-start.4 = (bf16[16,7296]{1,0:T(8,128)(2,1)S(1)}, bf16[16,7296]{1,0:T(8,128)(2,1)S(1)}, u32[]{:S(2)}, u32[]{:S(2)}) collective-permute-start(bf16[16,7296]{1,0:T(8,128)(2,1)S(1)} %pad_maximum_fusion.after_ref.refs_0_), channel_id=1, source_target_pairs={{0,2},{2,0},{4,6},{6,4},{8,10},{10,8},{12,14},{14,12},{1,3},{3,1},... | collective-permute-start | bytes 700424 | tf_op jit(solution)/shard_map/ppermute | solution.py:29
  18.4 1.7 %collective-permute-start.5 = (bf16[16,7296]{1,0:T(8,128)(2,1)S(1)}, bf16[16,7296]{1,0:T(8,128)(2,1)S(1)}, u32[]{:S(2)}, u32[]{:S(2)}) collective-permute-start(bf16[16,7296]{1,0:T(8,128)(2,1)S(1)} %collective-permute-done.3.refs_1_), channel_id=1, source_target_pairs={{0,2},{2,0},{4,6},{6,4},{8,10},{10,8},{12,14},{14,12},{1,3},{3,1},... | collective-permute-start | bytes 700424 | tf_op jit(solution)/shard_map/ppermute | solution.py:29
  27.0 1.6 %collective-permute-start.6 = (bf16[16,7168]{1,0:T(8,128)(2,1)S(1)}, bf16[16,7168]{1,0:T(8,128)(2,1)S(1)}, u32[]{:S(2)}, u32[]{:S(2)}) collective-permute-start(bf16[16,7168]{1,0:T(8,128)(2,1)S(1)} %get-tuple-element.27), channel_id=1, source_target_pairs={{0,2},{2,0},{4,6},{6,4},{8,10},{10,8},{12,14},{14,12},{1,3},{3,1},... | collective-permute-start | bytes 688136 | tf_op jit(solution)/shard_map/ppermute | solution.py:29
  28.6 1.7 %collective-permute-start.7 = (bf16[16,7168]{1,0:T(8,128)(2,1)S(1)}, bf16[16,7168]{1,0:T(8,128)(2,1)S(1)}, u32[]{:S(2)}, u32[]{:S(2)}) collective-permute-start(bf16[16,7168]{1,0:T(8,128)(2,1)S(1)} %get-tuple-element.28), channel_id=1, source_target_pairs={{0,2},{2,0},{4,6},{6,4},{8,10},{10,8},{12,14},{14,12},{1,3},{3,1},... | collective-permute-start | bytes 688136 | tf_op jit(solution)/shard_map/ppermute | solution.py:29
  29.1 5.3 %collective-permute-start.10 = (bf16[8,7168]{1,0:T(8,128)(2,1)S(1)}, bf16[8,7168]{1,0:T(8,128)(2,1)S(1)}, u32[]{:S(2)}, u32[]{:S(2)}) collective-permute-start(bf16[8,7168]{1,0:T(8,128)(2,1)S(1)} %slice.42), channel_id=1, source_target_pairs={{0,1},{1,0},{2,3},{3,2},{4,5},{5,4},{6,7},{7,6},{8,9},{9,8},{10,11... | collective-permute-start | bytes 344072 | tf_op jit(solution)/shard_map/ppermute | solution.py:17
  30.5 7.7 %collective-permute-start.8 = (bf16[8,7168]{1,0:T(8,128)(2,1)S(1)}, bf16[8,7168]{1,0:T(8,128)(2,1)S(1)}, u32[]{:S(2)}, u32[]{:S(2)}) collective-permute-start(bf16[8,7168]{1,0:T(8,128)(2,1)S(1)} %pad_maximum_fusion.1), channel_id=1, source_target_pairs={{0,4},{2,6},{4,0},{6,2},{8,12},{10,14},{12,8},{14,10},{1,5},{3,7},... | collective-permute-start | bytes 344072 | tf_op jit(solution)/shard_map/ppermute | solution.py:25
  34.4 5.3 %collective-permute-start.11 = (bf16[4,7168]{1,0:T(4,128)(2,1)S(1)}, bf16[4,7168]{1,0:T(4,128)(2,1)S(1)}, u32[]{:S(2)}, u32[]{:S(2)}) collective-permute-start(bf16[4,7168]{1,0:T(4,128)(2,1)S(1)} %get-tuple-element.29), channel_id=1, source_target_pairs={{0,8},{2,10},{4,12},{6,14},{8,0},{10,2},{12,4},{14,6},{1,9},{3,11}... | collective-permute-start | bytes 172040 | tf_op jit(solution)/shard_map/ppermute | solution.py:25
  36.6 6.1 %collective-permute-start.12 = (bf16[4,7168]{1,0:T(4,128)(2,1)S(1)}, bf16[4,7168]{1,0:T(4,128)(2,1)S(1)}, u32[]{:S(2)}, u32[]{:S(2)}) collective-permute-start(bf16[4,7168]{1,0:T(4,128)(2,1)S(1)} %get-tuple-element.30), channel_id=1, source_target_pairs={{0,12},{2,14},{4,8},{6,10},{8,4},{10,6},{12,0},{14,2},{1,13},{3,15... | collective-permute-start | bytes 172040 | tf_op jit(solution)/shard_map/ppermute | solution.py:25
  38.2 4.5 %collective-permute-start.9 = (bf16[4,7168]{1,0:T(4,128)(2,1)S(1)}, bf16[4,7168]{1,0:T(4,128)(2,1)S(1)}, u32[]{:S(2)}, u32[]{:S(2)}) collective-permute-start(bf16[4,7168]{1,0:T(4,128)(2,1)S(1)} %fusion), channel_id=1, source_target_pairs={{0,1},{1,0},{2,3},{3,2},{4,5},{5,4},{6,7},{7,6},{8,9},{9,8},{10,11... | collective-permute-start | bytes 172040 | tf_op jit(solution)/shard_map/ppermute | solution.py:17
